TPU v7x, 512 devices: a whole 4x8x8 slice. The times are simulated.
512 devices in a mesh: diam: 16 (over x, y_lo), mesh: 32 (over z, y_hi, core).
Axes of the slice: x: 4, y: 8 (y_hi: 2, y_lo: 4; y = y_hi * 4 + y_lo), z: 8, core: 2. Of those that a mesh axis runs over, the one named last changes fastest.
Arguments:
- perturbation: float32 [16, 2, 2, 5, 1024, 128], P('diam', None, None, None, 'mesh'), may hold values from -6 to 6
- source: float32 [2, 2, 5, 1024, 128], P(None, None, None, 'mesh'), may hold values from -6 to 6
- time_step: float32 [1024, 128], P('mesh'), may hold values from 0.25 to 0.3
- jac_axial: float32 [5, 5], replicated, may hold values from -3.354102 to 3.354102
- jac_circ: float32 [5, 5], replicated, may hold values from -3.354102 to 3.354102
- omega: float32 [2], replicated, may hold values from 0.5 to 2
- diam_ids: int32 [16], replicated, may hold values from 0 to 71, as said below
- surf_cell: int32 [16384], P('mesh'), may hold values from 0 to 4095
- surf_weight: float32 [16, 16384], P(None, 'mesh'), may hold values from -0.375 to 0.375
- face_count: int32 [32], P('mesh'), may hold values from 1 to 512, 8192 in all
Outputs:
- perturbation_new: float32 [16, 2, 2, 5, 1024, 128], P('diam', None, None, None, 'mesh')
- influence: float32 [16, 2, 2, 72], P('diam')
Inputs may be any that keep to these rules, and one draw needn't show every extreme that they name: `diam_ids`: distinct nodal diameters; diameter 0 and diameter 72 - 1 are always among them. `face_count`: sum over blocks is 8192; some block owns all its 512 slots.
All inputs are finite; a program needn't handle non-finite values.
Results may differ from a plain program's by a relative error of at most 0.00017.
Values sent between devices are 32-bit elements; how exact they have to be, the bound alone decides.
No kernel may reach another device: no remote copies, remote signals or barrier semaphores. Data moves between devices by JAX's collectives and lax.ppermute only.
A program may use at most 64 MiB of HBM per device.

v0:
```python
import jax
import jax.numpy as jnp
from jax import lax
from jax.sharding import PartitionSpec as P

BLADES = 72
MODES = 16
ITERS = 3
SECTIONS = 4


HIGH = lax.Precision.HIGHEST
ALPHAS = (0.25, 1.0 / 3.0, 0.5, 1.0)


def padded_2(value, sides, width):
    for axis, dim in sides:
        peers, length = (lax.axis_size(axis), value.shape[dim])
        up = [(i, (i + 1) % peers) for i in range(peers - 1)]
        down = [(j, i) for i, j in up]
        last = lax.slice_in_dim(value, length - width, length, axis=dim)
        initial = lax.slice_in_dim(value, 0, width, axis=dim)
        before = lax.ppermute(last, axis, up)
        after = lax.ppermute(initial, axis, down)
        value = jnp.concatenate([before, value, after], axis=dim)
    return value


def rotate(field, cosine, sine):
    real_part = field[:, :, 0:1]
    imag_part = field[:, :, 1:2]
    return jnp.concatenate(
        [cosine * real_part - sine * imag_part, sine * real_part + cosine * imag_part], axis=2
    )


def rhs(center, upper, lower, cosine, sine, src, jac_axial, jac_circ, omega):
    width = center.shape[-1]
    column = jnp.arange(width)
    right_base = jnp.roll(center, -1, axis=-1)
    right = jnp.where(column == width - 1, rotate(right_base, cosine, sine), right_base)
    left_base = jnp.roll(center, 1, axis=-1)
    left = jnp.where(column == 0, rotate(left_base, cosine, -sine), left_base)
    axial = (upper - lower) * 0.5
    circ = (right - left) * 0.5
    lap = upper + lower + right + left - 4.0 * center
    conv = jnp.einsum("uv,decvij->decuij", jac_axial, axial, precision=HIGH)
    conv = conv + jnp.einsum("uv,decvij->decuij", jac_circ, circ, precision=HIGH)
    freq = omega.reshape(1, -1, 1, 1, 1, 1)
    spin = jnp.concatenate([-freq * center[:, :, 1:2], freq * center[:, :, 0:1]], axis=2)
    return spin + conv - 0.2 * lap - src[None]


def transform(force, idents):
    blade = jnp.arange(BLADES, dtype=jnp.int32)
    angle = 2.0 * jnp.pi * (idents[:, None] * blade[None, :] % BLADES).astype(jnp.float32) / BLADES
    cosine = jnp.cos(angle)
    sine = jnp.sin(angle)
    f_real = force[:, :, 0]
    f_imag = force[:, :, 1]
    k_real = jnp.einsum("nem,nb->meb", f_real, cosine, precision=HIGH) - jnp.einsum(
        "nem,nb->meb", f_imag, sine, precision=HIGH
    )
    k_imag = jnp.einsum("nem,nb->meb", f_real, sine, precision=HIGH) + jnp.einsum(
        "nem,nb->meb", f_imag, cosine, precision=HIGH
    )
    return jnp.stack([k_real, k_imag], axis=1) / BLADES


def per_device(
    perturbation,
    source,
    time_step,
    jac_axial,
    jac_circ,
    omega,
    diam_ids,
    surf_cell,
    surf_weight,
    face_count,
):
    slots = perturbation.shape[0]
    rows = perturbation.shape[4]
    width = perturbation.shape[5]
    mine = lax.dynamic_slice_in_dim(diam_ids, lax.axis_index("diam") * slots, slots)
    sigma = 2.0 * jnp.pi * mine.astype(jnp.float32) / BLADES
    cosine = jnp.cos(sigma).reshape(slots, 1, 1, 1, 1, 1)
    sine = jnp.sin(sigma).reshape(slots, 1, 1, 1, 1, 1)

    def one_step(step, field):
        start = field
        for section in range(SECTIONS):
            padded = padded_2(field, (("mesh", 4),), 1)
            res = rhs(
                field,
                padded[..., 2:, :],
                padded[..., :-2, :],
                cosine,
                sine,
                source,
                jac_axial,
                jac_circ,
                omega,
            )
            field = start - ALPHAS[section] * time_step * res
        return field

    result = lax.fori_loop(0, ITERS, one_step, perturbation)
    pressure = result[:, :, :, 4].reshape(slots, result.shape[1], 2, rows * width)
    picked = jnp.take(pressure, surf_cell, axis=3)
    live = (jnp.arange(surf_cell.shape[0]) < face_count[0]).astype(jnp.float32)
    force = jnp.einsum("decf,mf->decm", picked * live, surf_weight, precision=HIGH)
    share = MODES // lax.axis_size("diam")
    mode_start = lax.axis_index("diam") * share
    summed = lax.psum(force, "mesh")
    every = lax.all_gather(summed, "diam", axis=0, tiled=True)
    chosen = lax.dynamic_slice_in_dim(every, mode_start, share, 3)
    influence = transform(chosen, diam_ids)
    return (result, influence)


def solution(mesh):
    in_specs = (
        P("diam", None, None, None, "mesh", None),
        P(None, None, None, "mesh", None),
        P("mesh", None),
        P(),
        P(),
        P(),
        P(),
        P("mesh"),
        P(None, "mesh"),
        P("mesh"),
    )
    out_specs = (P("diam", None, None, None, "mesh", None), P("diam", None, None, None))
    return jax.shard_map(
        per_device, mesh=mesh, in_specs=in_specs, out_specs=out_specs, check_vma=False
    )
```

profile of v0, /device:TPU:256, one launch (start us, length us, event | category | flops | bytes accessed | tf_op | source)
XLA Modules:
  0.0 380.4 jit_solution(15215005033958376713)
XLA Ops:
  4.8 238.5 %while.11 = (s32[]{:T(128)}, f32[1,2,2,5,32,128]{5,4,3,2,1,0:T(8,128)S(1)}, f32[32,128]{1,0:T(8,128)}, f32[1,2,1,1,1,1]{1,5,4,3,2,0:T(1,128)}, f32[2]{0:T(128)},...) while((s32[]{:T(128)}, ...), condition=%wide.region_1.2_spmd, body=%wide.region_0.1_spmd.sunk | while | flops 53301504 | bytes 52118112 | solution.py:108
  4.8 6.3 %collective-permute-start = (f32[1,2,2,5,1,128]{5,4,3,1,2,0:T(1,128)S(1)}, f32[1,2,2,5,1,128]{5,4,3,1,2,0:T(1,128)S(1)}, u32[]{:S(2)}, u32[]{:S(2)}) collective-permute-start(f32[1,2,2,5,1,128]{5,4,3,1,2,0:T(1,128)S(1)} %get-tuple-element.377), channel_id=1, source_target_pairs={{1,0},{2,1},{3,2},{4,3},{5,4},{6,5},{7,6},{8,7},{9,8},{10,9},{11,1... | collective-permute-start | bytes 30728 | tf_op jit(solution)/shard_map/while/body/eval_jaxpr/ppermute | solution.py:24
  19.2 2.9 collective-permute-done.1
  29.7 6.7 %collective-permute-start.2 = (f32[1,2,2,5,1,128]{5,4,3,1,2,0:T(1,128)S(1)}, f32[1,2,2,5,1,128]{5,4,3,1,2,0:T(1,128)S(1)}, u32[]{:S(2)}, u32[]{:S(2)}) collective-permute-start(f32[1,2,2,5,1,128]{5,4,3,1,2,0:T(1,128)S(1)} %get-tuple-element.391), channel_id=1, source_target_pairs={{1,0},{2,1},{3,2},{4,3},{5,4},{6,5},{7,6},{8,7},{9,8},{10,9},{11,1... | collective-permute-start | bytes 30728 | tf_op jit(solution)/shard_map/while/body/eval_jaxpr/ppermute | solution.py:24
  38.5 9.0 %collective-permute-done.3 = f32[1,2,2,5,1,128]{5,4,3,1,2,0:T(1,128)S(1)} collective-permute-done((f32[1,2,2,5,1,128]{5,4,3,1,2,0:T(1,128)S(1)}, f32[1,2,2,5,1,128]{5,4,3,1,2,0:T(1,128)S(1)}, u32[]{:S(2)}, u32[]{:S(2)}) %collective-permute-start.3) | collective-permute-done | bytes 10272 | tf_op jit(solution)/shard_map/while/body/eval_jaxpr/ppermute | solution.py:23
  55.1 2.4 collective-permute-start.5
  57.6 8.5 %collective-permute-done.5 = f32[1,2,2,5,1,128]{5,4,3,1,2,0:T(1,128)S(1)} collective-permute-done((f32[1,2,2,5,1,128]{5,4,3,1,2,0:T(1,128)S(1)}, f32[1,2,2,5,1,128]{5,4,3,1,2,0:T(1,128)S(1)}, u32[]{:S(2)}, u32[]{:S(2)}) %collective-permute-start.5) | collective-permute-done | bytes 10272 | tf_op jit(solution)/shard_map/while/body/eval_jaxpr/ppermute | solution.py:23
  74.7 2.4 collective-permute-start.7
  77.3 8.5 %collective-permute-done.7 = f32[1,2,2,5,1,128]{5,4,3,1,2,0:T(1,128)S(1)} collective-permute-done((f32[1,2,2,5,1,128]{5,4,3,1,2,0:T(1,128)S(1)}, f32[1,2,2,5,1,128]{5,4,3,1,2,0:T(1,128)S(1)}, u32[]{:S(2)}, u32[]{:S(2)}) %collective-permute-start.7) | collective-permute-done | bytes 10272 | tf_op jit(solution)/shard_map/while/body/eval_jaxpr/ppermute | solution.py:23
  89.1 2.4 collective-permute-start.1
  97.6 2.5 collective-permute-done.1
  107.7 6.7 %collective-permute-start.2 = (f32[1,2,2,5,1,128]{5,4,3,1,2,0:T(1,128)S(1)}, f32[1,2,2,5,1,128]{5,4,3,1,2,0:T(1,128)S(1)}, u32[]{:S(2)}, u32[]{:S(2)}) collective-permute-start(f32[1,2,2,5,1,128]{5,4,3,1,2,0:T(1,128)S(1)} %get-tuple-element.391), channel_id=1, source_target_pairs={{1,0},{2,1},{3,2},{4,3},{5,4},{6,5},{7,6},{8,7},{9,8},{10,9},{11,1... | collective-permute-start | bytes 30728 | tf_op jit(solution)/shard_map/while/body/eval_jaxpr/ppermute | solution.py:24
  116.5 9.0 %collective-permute-done.3 = f32[1,2,2,5,1,128]{5,4,3,1,2,0:T(1,128)S(1)} collective-permute-done((f32[1,2,2,5,1,128]{5,4,3,1,2,0:T(1,128)S(1)}, f32[1,2,2,5,1,128]{5,4,3,1,2,0:T(1,128)S(1)}, u32[]{:S(2)}, u32[]{:S(2)}) %collective-permute-start.3) | collective-permute-done | bytes 10272 | tf_op jit(solution)/shard_map/while/body/eval_jaxpr/ppermute | solution.py:23
  135.6 8.5 %collective-permute-done.5 = f32[1,2,2,5,1,128]{5,4,3,1,2,0:T(1,128)S(1)} collective-permute-done((f32[1,2,2,5,1,128]{5,4,3,1,2,0:T(1,128)S(1)}, f32[1,2,2,5,1,128]{5,4,3,1,2,0:T(1,128)S(1)}, u32[]{:S(2)}, u32[]{:S(2)}) %collective-permute-start.5) | collective-permute-done | bytes 10272 | tf_op jit(solution)/shard_map/while/body/eval_jaxpr/ppermute | solution.py:23
  155.3 8.5 %collective-permute-done.7 = f32[1,2,2,5,1,128]{5,4,3,1,2,0:T(1,128)S(1)} collective-permute-done((f32[1,2,2,5,1,128]{5,4,3,1,2,0:T(1,128)S(1)}, f32[1,2,2,5,1,128]{5,4,3,1,2,0:T(1,128)S(1)}, u32[]{:S(2)}, u32[]{:S(2)}) %collective-permute-start.7) | collective-permute-done | bytes 10272 | tf_op jit(solution)/shard_map/while/body/eval_jaxpr/ppermute | solution.py:23
  175.6 2.5 collective-permute-done.1
  185.7 6.7 %collective-permute-start.2 = (f32[1,2,2,5,1,128]{5,4,3,1,2,0:T(1,128)S(1)}, f32[1,2,2,5,1,128]{5,4,3,1,2,0:T(1,128)S(1)}, u32[]{:S(2)}, u32[]{:S(2)}) collective-permute-start(f32[1,2,2,5,1,128]{5,4,3,1,2,0:T(1,128)S(1)} %get-tuple-element.391), channel_id=1, source_target_pairs={{1,0},{2,1},{3,2},{4,3},{5,4},{6,5},{7,6},{8,7},{9,8},{10,9},{11,1... | collective-permute-start | bytes 30728 | tf_op jit(solution)/shard_map/while/body/eval_jaxpr/ppermute | solution.py:24
  194.5 9.0 %collective-permute-done.3 = f32[1,2,2,5,1,128]{5,4,3,1,2,0:T(1,128)S(1)} collective-permute-done((f32[1,2,2,5,1,128]{5,4,3,1,2,0:T(1,128)S(1)}, f32[1,2,2,5,1,128]{5,4,3,1,2,0:T(1,128)S(1)}, u32[]{:S(2)}, u32[]{:S(2)}) %collective-permute-start.3) | collective-permute-done | bytes 10272 | tf_op jit(solution)/shard_map/while/body/eval_jaxpr/ppermute | solution.py:23
  213.6 8.5 %collective-permute-done.5 = f32[1,2,2,5,1,128]{5,4,3,1,2,0:T(1,128)S(1)} collective-permute-done((f32[1,2,2,5,1,128]{5,4,3,1,2,0:T(1,128)S(1)}, f32[1,2,2,5,1,128]{5,4,3,1,2,0:T(1,128)S(1)}, u32[]{:S(2)}, u32[]{:S(2)}) %collective-permute-start.5) | collective-permute-done | bytes 10272 | tf_op jit(solution)/shard_map/while/body/eval_jaxpr/ppermute | solution.py:23
  233.3 8.5 %collective-permute-done.7 = f32[1,2,2,5,1,128]{5,4,3,1,2,0:T(1,128)S(1)} collective-permute-done((f32[1,2,2,5,1,128]{5,4,3,1,2,0:T(1,128)S(1)}, f32[1,2,2,5,1,128]{5,4,3,1,2,0:T(1,128)S(1)}, u32[]{:S(2)}, u32[]{:S(2)}) %collective-permute-start.7) | collective-permute-done | bytes 10272 | tf_op jit(solution)/shard_map/while/body/eval_jaxpr/ppermute | solution.py:23
  243.4 3.1 copy.380
  246.5 3.7 gather_fusion
  254.1 84.3 %psum.7 = f32[1,2,2,16]{3,2,1,0:T(2,128)S(1)} all-reduce(f32[1,2,2,16]{3,2,1,0:T(2,128)S(1)} %convolution_bitcast_fusion), channel_id=1, replica_groups=mesh['diam'=16,'mesh'=32] {'mesh'}, use_global_device_ids=true, to_apply=%region_2.3 | all-reduce | flops 64 | bytes 512 | tf_op jit(solution)/shard_map/psum | solution.py:115
  338.4 40.0 %all_gather.3 = f32[16,2,2,16]{3,2,1,0:T(2,128)S(1)} all-gather(f32[1,2,2,16]{3,2,1,0:T(2,128)S(1)} %psum.7), channel_id=1, replica_groups=mesh['diam'=16,'mesh'=32] {'diam'}, dimensions={0}, use_global_device_ids=true | all-gather | bytes 4352 | tf_op jit(solution)/shard_map/all_gather | solution.py:116
  (282 shorter events, 126.4 us)
Async XLA Ops:
  4.8 14.3 %collective-permute-start = (f32[1,2,2,5,1,128]{5,4,3,1,2,0:T(1,128)S(1)}, f32[1,2,2,5,1,128]{5,4,3,1,2,0:T(1,128)S(1)}, u32[]{:S(2)}, u32[]{:S(2)}) collective-permute-start(f32[1,2,2,5,1,128]{5,4,3,1,2,0:T(1,128)S(1)} %get-tuple-element.377), channel_id=1, source_target_pairs={{1,0},{2,1},{3,2},{4,3},{5,4},{6,5},{7,6},{8,7},{9,8},{10,9},{11,1... | collective-permute-start | bytes 30728 | tf_op jit(solution)/shard_map/while/body/eval_jaxpr/ppermute | solution.py:24
  11.1 11.0 %collective-permute-start.1 = (f32[1,2,2,5,1,128]{5,4,3,1,2,0:T(1,128)S(1)}, f32[1,2,2,5,1,128]{5,4,3,1,2,0:T(1,128)S(1)}, u32[]{:S(2)}, u32[]{:S(2)}) collective-permute-start(f32[1,2,2,5,1,128]{5,4,3,1,2,0:T(1,128)S(1)} %get-tuple-element.378), channel_id=1, source_target_pairs={{0,1},{1,2},{2,3},{3,4},{4,5},{5,6},{6,7},{7,8},{8,9},{9,10},{10,1... | collective-permute-start | bytes 30728 | tf_op jit(solution)/shard_map/while/body/eval_jaxpr/ppermute | solution.py:23
  29.7 8.8 %collective-permute-start.2 = (f32[1,2,2,5,1,128]{5,4,3,1,2,0:T(1,128)S(1)}, f32[1,2,2,5,1,128]{5,4,3,1,2,0:T(1,128)S(1)}, u32[]{:S(2)}, u32[]{:S(2)}) collective-permute-start(f32[1,2,2,5,1,128]{5,4,3,1,2,0:T(1,128)S(1)} %get-tuple-element.391), channel_id=1, source_target_pairs={{1,0},{2,1},{3,2},{4,3},{5,4},{6,5},{7,6},{8,7},{9,8},{10,9},{11,1... | collective-permute-start | bytes 30728 | tf_op jit(solution)/shard_map/while/body/eval_jaxpr/ppermute | solution.py:24
  36.5 11.0 %collective-permute-start.3 = (f32[1,2,2,5,1,128]{5,4,3,1,2,0:T(1,128)S(1)}, f32[1,2,2,5,1,128]{5,4,3,1,2,0:T(1,128)S(1)}, u32[]{:S(2)}, u32[]{:S(2)}) collective-permute-start(f32[1,2,2,5,1,128]{5,4,3,1,2,0:T(1,128)S(1)} %get-tuple-element.392), channel_id=1, source_target_pairs={{0,1},{1,2},{2,3},{3,4},{4,5},{5,6},{6,7},{7,8},{8,9},{9,10},{10,1... | collective-permute-start | bytes 30728 | tf_op jit(solution)/shard_map/while/body/eval_jaxpr/ppermute | solution.py:23
  53.2 4.4 %collective-permute-start.4 = (f32[1,2,2,5,1,128]{5,4,3,1,2,0:T(1,128)S(1)}, f32[1,2,2,5,1,128]{5,4,3,1,2,0:T(1,128)S(1)}, u32[]{:S(2)}, u32[]{:S(2)}) collective-permute-start(f32[1,2,2,5,1,128]{5,4,3,1,2,0:T(1,128)S(1)} %get-tuple-element.408), channel_id=1, source_target_pairs={{1,0},{2,1},{3,2},{4,3},{5,4},{6,5},{7,6},{8,7},{9,8},{10,9},{11,1... | collective-permute-start | bytes 30728 | tf_op jit(solution)/shard_map/while/body/eval_jaxpr/ppermute | solution.py:24
  55.1 11.0 %collective-permute-start.5 = (f32[1,2,2,5,1,128]{5,4,3,1,2,0:T(1,128)S(1)}, f32[1,2,2,5,1,128]{5,4,3,1,2,0:T(1,128)S(1)}, u32[]{:S(2)}, u32[]{:S(2)}) collective-permute-start(f32[1,2,2,5,1,128]{5,4,3,1,2,0:T(1,128)S(1)} %get-tuple-element.409), channel_id=1, source_target_pairs={{0,1},{1,2},{2,3},{3,4},{4,5},{5,6},{6,7},{7,8},{8,9},{9,10},{10,1... | collective-permute-start | bytes 30728 | tf_op jit(solution)/shard_map/while/body/eval_jaxpr/ppermute | solution.py:23
  72.8 4.4 %collective-permute-start.6 = (f32[1,2,2,5,1,128]{5,4,3,1,2,0:T(1,128)S(1)}, f32[1,2,2,5,1,128]{5,4,3,1,2,0:T(1,128)S(1)}, u32[]{:S(2)}, u32[]{:S(2)}) collective-permute-start(f32[1,2,2,5,1,128]{5,4,3,1,2,0:T(1,128)S(1)} %get-tuple-element.428), channel_id=1, source_target_pairs={{1,0},{2,1},{3,2},{4,3},{5,4},{6,5},{7,6},{8,7},{9,8},{10,9},{11,1... | collective-permute-start | bytes 30728 | tf_op jit(solution)/shard_map/while/body/eval_jaxpr/ppermute | solution.py:24
  74.7 11.0 %collective-permute-start.7 = (f32[1,2,2,5,1,128]{5,4,3,1,2,0:T(1,128)S(1)}, f32[1,2,2,5,1,128]{5,4,3,1,2,0:T(1,128)S(1)}, u32[]{:S(2)}, u32[]{:S(2)}) collective-permute-start(f32[1,2,2,5,1,128]{5,4,3,1,2,0:T(1,128)S(1)} %get-tuple-element.429), channel_id=1, source_target_pairs={{0,1},{1,2},{2,3},{3,4},{4,5},{5,6},{6,7},{7,8},{8,9},{9,10},{10,1... | collective-permute-start | bytes 30728 | tf_op jit(solution)/shard_map/while/body/eval_jaxpr/ppermute | solution.py:23
  87.2 10.5 %collective-permute-start = (f32[1,2,2,5,1,128]{5,4,3,1,2,0:T(1,128)S(1)}, f32[1,2,2,5,1,128]{5,4,3,1,2,0:T(1,128)S(1)}, u32[]{:S(2)}, u32[]{:S(2)}) collective-permute-start(f32[1,2,2,5,1,128]{5,4,3,1,2,0:T(1,128)S(1)} %get-tuple-element.377), channel_id=1, source_target_pairs={{1,0},{2,1},{3,2},{4,3},{5,4},{6,5},{7,6},{8,7},{9,8},{10,9},{11,1... | collective-permute-start | bytes 30728 | tf_op jit(solution)/shard_map/while/body/eval_jaxpr/ppermute | solution.py:24
  89.1 11.0 %collective-permute-start.1 = (f32[1,2,2,5,1,128]{5,4,3,1,2,0:T(1,128)S(1)}, f32[1,2,2,5,1,128]{5,4,3,1,2,0:T(1,128)S(1)}, u32[]{:S(2)}, u32[]{:S(2)}) collective-permute-start(f32[1,2,2,5,1,128]{5,4,3,1,2,0:T(1,128)S(1)} %get-tuple-element.378), channel_id=1, source_target_pairs={{0,1},{1,2},{2,3},{3,4},{4,5},{5,6},{6,7},{7,8},{8,9},{9,10},{10,1... | collective-permute-start | bytes 30728 | tf_op jit(solution)/shard_map/while/body/eval_jaxpr/ppermute | solution.py:23
  107.7 8.8 %collective-permute-start.2 = (f32[1,2,2,5,1,128]{5,4,3,1,2,0:T(1,128)S(1)}, f32[1,2,2,5,1,128]{5,4,3,1,2,0:T(1,128)S(1)}, u32[]{:S(2)}, u32[]{:S(2)}) collective-permute-start(f32[1,2,2,5,1,128]{5,4,3,1,2,0:T(1,128)S(1)} %get-tuple-element.391), channel_id=1, source_target_pairs={{1,0},{2,1},{3,2},{4,3},{5,4},{6,5},{7,6},{8,7},{9,8},{10,9},{11,1... | collective-permute-start | bytes 30728 | tf_op jit(solution)/shard_map/while/body/eval_jaxpr/ppermute | solution.py:24
  114.5 11.0 %collective-permute-start.3 = (f32[1,2,2,5,1,128]{5,4,3,1,2,0:T(1,128)S(1)}, f32[1,2,2,5,1,128]{5,4,3,1,2,0:T(1,128)S(1)}, u32[]{:S(2)}, u32[]{:S(2)}) collective-permute-start(f32[1,2,2,5,1,128]{5,4,3,1,2,0:T(1,128)S(1)} %get-tuple-element.392), channel_id=1, source_target_pairs={{0,1},{1,2},{2,3},{3,4},{4,5},{5,6},{6,7},{7,8},{8,9},{9,10},{10,1... | collective-permute-start | bytes 30728 | tf_op jit(solution)/shard_map/while/body/eval_jaxpr/ppermute | solution.py:23
  131.2 4.4 %collective-permute-start.4 = (f32[1,2,2,5,1,128]{5,4,3,1,2,0:T(1,128)S(1)}, f32[1,2,2,5,1,128]{5,4,3,1,2,0:T(1,128)S(1)}, u32[]{:S(2)}, u32[]{:S(2)}) collective-permute-start(f32[1,2,2,5,1,128]{5,4,3,1,2,0:T(1,128)S(1)} %get-tuple-element.408), channel_id=1, source_target_pairs={{1,0},{2,1},{3,2},{4,3},{5,4},{6,5},{7,6},{8,7},{9,8},{10,9},{11,1... | collective-permute-start | bytes 30728 | tf_op jit(solution)/shard_map/while/body/eval_jaxpr/ppermute | solution.py:24
  133.1 11.0 %collective-permute-start.5 = (f32[1,2,2,5,1,128]{5,4,3,1,2,0:T(1,128)S(1)}, f32[1,2,2,5,1,128]{5,4,3,1,2,0:T(1,128)S(1)}, u32[]{:S(2)}, u32[]{:S(2)}) collective-permute-start(f32[1,2,2,5,1,128]{5,4,3,1,2,0:T(1,128)S(1)} %get-tuple-element.409), channel_id=1, source_target_pairs={{0,1},{1,2},{2,3},{3,4},{4,5},{5,6},{6,7},{7,8},{8,9},{9,10},{10,1... | collective-permute-start | bytes 30728 | tf_op jit(solution)/shard_map/while/body/eval_jaxpr/ppermute | solution.py:23
  150.8 4.4 %collective-permute-start.6 = (f32[1,2,2,5,1,128]{5,4,3,1,2,0:T(1,128)S(1)}, f32[1,2,2,5,1,128]{5,4,3,1,2,0:T(1,128)S(1)}, u32[]{:S(2)}, u32[]{:S(2)}) collective-permute-start(f32[1,2,2,5,1,128]{5,4,3,1,2,0:T(1,128)S(1)} %get-tuple-element.428), channel_id=1, source_target_pairs={{1,0},{2,1},{3,2},{4,3},{5,4},{6,5},{7,6},{8,7},{9,8},{10,9},{11,1... | collective-permute-start | bytes 30728 | tf_op jit(solution)/shard_map/while/body/eval_jaxpr/ppermute | solution.py:24
  152.7 11.0 %collective-permute-start.7 = (f32[1,2,2,5,1,128]{5,4,3,1,2,0:T(1,128)S(1)}, f32[1,2,2,5,1,128]{5,4,3,1,2,0:T(1,128)S(1)}, u32[]{:S(2)}, u32[]{:S(2)}) collective-permute-start(f32[1,2,2,5,1,128]{5,4,3,1,2,0:T(1,128)S(1)} %get-tuple-element.429), channel_id=1, source_target_pairs={{0,1},{1,2},{2,3},{3,4},{4,5},{5,6},{6,7},{7,8},{8,9},{9,10},{10,1... | collective-permute-start | bytes 30728 | tf_op jit(solution)/shard_map/while/body/eval_jaxpr/ppermute | solution.py:23
  165.2 10.5 %collective-permute-start = (f32[1,2,2,5,1,128]{5,4,3,1,2,0:T(1,128)S(1)}, f32[1,2,2,5,1,128]{5,4,3,1,2,0:T(1,128)S(1)}, u32[]{:S(2)}, u32[]{:S(2)}) collective-permute-start(f32[1,2,2,5,1,128]{5,4,3,1,2,0:T(1,128)S(1)} %get-tuple-element.377), channel_id=1, source_target_pairs={{1,0},{2,1},{3,2},{4,3},{5,4},{6,5},{7,6},{8,7},{9,8},{10,9},{11,1... | collective-permute-start | bytes 30728 | tf_op jit(solution)/shard_map/while/body/eval_jaxpr/ppermute | solution.py:24
  167.1 11.0 %collective-permute-start.1 = (f32[1,2,2,5,1,128]{5,4,3,1,2,0:T(1,128)S(1)}, f32[1,2,2,5,1,128]{5,4,3,1,2,0:T(1,128)S(1)}, u32[]{:S(2)}, u32[]{:S(2)}) collective-permute-start(f32[1,2,2,5,1,128]{5,4,3,1,2,0:T(1,128)S(1)} %get-tuple-element.378), channel_id=1, source_target_pairs={{0,1},{1,2},{2,3},{3,4},{4,5},{5,6},{6,7},{7,8},{8,9},{9,10},{10,1... | collective-permute-start | bytes 30728 | tf_op jit(solution)/shard_map/while/body/eval_jaxpr/ppermute | solution.py:23
  185.7 8.8 %collective-permute-start.2 = (f32[1,2,2,5,1,128]{5,4,3,1,2,0:T(1,128)S(1)}, f32[1,2,2,5,1,128]{5,4,3,1,2,0:T(1,128)S(1)}, u32[]{:S(2)}, u32[]{:S(2)}) collective-permute-start(f32[1,2,2,5,1,128]{5,4,3,1,2,0:T(1,128)S(1)} %get-tuple-element.391), channel_id=1, source_target_pairs={{1,0},{2,1},{3,2},{4,3},{5,4},{6,5},{7,6},{8,7},{9,8},{10,9},{11,1... | collective-permute-start | bytes 30728 | tf_op jit(solution)/shard_map/while/body/eval_jaxpr/ppermute | solution.py:24
  192.5 11.0 %collective-permute-start.3 = (f32[1,2,2,5,1,128]{5,4,3,1,2,0:T(1,128)S(1)}, f32[1,2,2,5,1,128]{5,4,3,1,2,0:T(1,128)S(1)}, u32[]{:S(2)}, u32[]{:S(2)}) collective-permute-start(f32[1,2,2,5,1,128]{5,4,3,1,2,0:T(1,128)S(1)} %get-tuple-element.392), channel_id=1, source_target_pairs={{0,1},{1,2},{2,3},{3,4},{4,5},{5,6},{6,7},{7,8},{8,9},{9,10},{10,1... | collective-permute-start | bytes 30728 | tf_op jit(solution)/shard_map/while/body/eval_jaxpr/ppermute | solution.py:23
  209.2 4.4 %collective-permute-start.4 = (f32[1,2,2,5,1,128]{5,4,3,1,2,0:T(1,128)S(1)}, f32[1,2,2,5,1,128]{5,4,3,1,2,0:T(1,128)S(1)}, u32[]{:S(2)}, u32[]{:S(2)}) collective-permute-start(f32[1,2,2,5,1,128]{5,4,3,1,2,0:T(1,128)S(1)} %get-tuple-element.408), channel_id=1, source_target_pairs={{1,0},{2,1},{3,2},{4,3},{5,4},{6,5},{7,6},{8,7},{9,8},{10,9},{11,1... | collective-permute-start | bytes 30728 | tf_op jit(solution)/shard_map/while/body/eval_jaxpr/ppermute | solution.py:24
  211.1 11.0 %collective-permute-start.5 = (f32[1,2,2,5,1,128]{5,4,3,1,2,0:T(1,128)S(1)}, f32[1,2,2,5,1,128]{5,4,3,1,2,0:T(1,128)S(1)}, u32[]{:S(2)}, u32[]{:S(2)}) collective-permute-start(f32[1,2,2,5,1,128]{5,4,3,1,2,0:T(1,128)S(1)} %get-tuple-element.409), channel_id=1, source_target_pairs={{0,1},{1,2},{2,3},{3,4},{4,5},{5,6},{6,7},{7,8},{8,9},{9,10},{10,1... | collective-permute-start | bytes 30728 | tf_op jit(solution)/shard_map/while/body/eval_jaxpr/ppermute | solution.py:23
  228.8 4.4 %collective-permute-start.6 = (f32[1,2,2,5,1,128]{5,4,3,1,2,0:T(1,128)S(1)}, f32[1,2,2,5,1,128]{5,4,3,1,2,0:T(1,128)S(1)}, u32[]{:S(2)}, u32[]{:S(2)}) collective-permute-start(f32[1,2,2,5,1,128]{5,4,3,1,2,0:T(1,128)S(1)} %get-tuple-element.428), channel_id=1, source_target_pairs={{1,0},{2,1},{3,2},{4,3},{5,4},{6,5},{7,6},{8,7},{9,8},{10,9},{11,1... | collective-permute-start | bytes 30728 | tf_op jit(solution)/shard_map/while/body/eval_jaxpr/ppermute | solution.py:24
  230.8 11.0 %collective-permute-start.7 = (f32[1,2,2,5,1,128]{5,4,3,1,2,0:T(1,128)S(1)}, f32[1,2,2,5,1,128]{5,4,3,1,2,0:T(1,128)S(1)}, u32[]{:S(2)}, u32[]{:S(2)}) collective-permute-start(f32[1,2,2,5,1,128]{5,4,3,1,2,0:T(1,128)S(1)} %get-tuple-element.429), channel_id=1, source_target_pairs={{0,1},{1,2},{2,3},{3,4},{4,5},{5,6},{6,7},{7,8},{8,9},{9,10},{10,1... | collective-permute-start | bytes 30728 | tf_op jit(solution)/shard_map/while/body/eval_jaxpr/ppermute | solution.py:23
  (22 other events, 672.9 us)
where the time goes:
time: 382 us; the launch traced here: 380 us
  blocking collectives  124 us (32%)
  waiting for transfers between devices  85.7 us (22%)
  starting transfers between devices  68.7 us (18%)
  other arithmetic  41.4 us (11%)
  local copies, waits for them, and re-layouts  36.8 us (10%)
  matrix products  19.9 us (5%)
    ppermute x12, waiting for transfers between devices, padded_2(): before = lax.ppermute(last, axis, up)  85.7 us
    psum x1, blocking collectives, per_device(): summed = lax.psum(force, 'mesh')  84.3 us
    ppermute x12, starting transfers between devices, padded_2(): after = lax.ppermute(initial, axis, down)  41.8 us
    all_gather x1, blocking collectives, per_device(): every = lax.all_gather(summed, 'diam', axis=0, tiled=True)  40 us
    ppermute x12, starting transfers between devices, padded_2(): before = lax.ppermute(last, axis, up)  26.9 us
    concatenate x24, local copies, waits for them, and re-layouts, rhs(): left_base = jnp.roll(center, 1, axis=-1)  18.3 us
    mul x12, other arithmetic, rhs(): circ = (right - left) * 0.5  15.9 us
    dot_general x12, matrix products, rhs(): jnp.einsum('uv,decvij->decuij', jac_circ, circ, precision=HIGH)  8.93 us
  transfers between devices with their start and end apart: 24, of which 12 were waited for; matrix products, arithmetic and copies ran while one was open for 5% of the time, Pallas kernels for 0%

commit v1 on v0

v1 whole, which is shorter than its diff:
```python
import functools
import itertools

import jax
import jax.numpy as jnp
from jax import lax
from jax.experimental import pallas as pl
from jax.experimental.pallas import tpu as pltpu
from jax.sharding import Mesh
from jax.sharding import PartitionSpec as P

BLADES = 72
ITERS = 3
SECTIONS = 4
HALO = ITERS * SECTIONS
ALPHAS = (0.25, 1.0 / 3.0, 0.5, 1.0)
HIGH = lax.Precision.HIGHEST
AXES = ("x", "yl", "z", "yh", "core")
SIZES = (4, 4, 8, 2, 2)
PLANES = 20
ROWS = 32
LANES = 128
MSG = 2 * PLANES * HALO + 16
TOP = 8
OWN = TOP + HALO
LOW = OWN + ROWS
BUF = LOW + HALO + 8


def flat(*coords):
    out = 0
    for c, n in zip(coords, SIZES):
        out = out * n + c
    return out


def swap_pairs(same_chip):
    pairs = []
    blocks = SIZES[2] * SIZES[3] * SIZES[4]
    for x, yl, p in itertools.product(range(SIZES[0]), range(SIZES[1]), range(blocks)):
        if same_chip:
            q = p ^ 1
        else:
            q = p + 1 if p % 2 else p - 1
        if 0 <= q < blocks:
            ends = [flat(x, yl, b // 4, (b // 2) % 2, b % 2) for b in (p, q)]
            pairs.append(tuple(ends))
    return pairs


def pack_kernel(q_ref, s_ref, t_ref, near_ref, far_ref):
    even = lax.axis_index("core") == 0

    def put(row, low, high):
        near_ref[pl.ds(row, HALO), :] = jnp.where(even, high, low)
        far_ref[pl.ds(row, HALO), :] = jnp.where(even, low, high)

    for i in range(PLANES):
        put(i * HALO, q_ref[i, 0:HALO, :], q_ref[i, ROWS - HALO : ROWS, :])
        put((PLANES + i) * HALO, s_ref[i, 0:HALO, :], s_ref[i, ROWS - HALO : ROWS, :])
    put(2 * PLANES * HALO, t_ref[0:HALO, :], t_ref[ROWS - HALO : ROWS, :])
    tail = jnp.zeros((MSG - 2 * PLANES * HALO - HALO, LANES), jnp.float32)
    near_ref[MSG - tail.shape[0] :, :] = tail
    far_ref[MSG - tail.shape[0] :, :] = tail


def prep_kernel(cell_ref, weight_ref, count_ref, ids_ref, moments_ref, table_ref):
    faces = cell_ref.shape[1]
    modes = weight_ref.shape[0]
    cell = cell_ref[...]
    row = lax.shift_right_logical(cell, 7)
    col = jnp.bitwise_and(cell, LANES - 1)
    live = lax.broadcasted_iota(jnp.int32, (1, faces), 1) < count_ref[0]
    weight = jnp.where(live, weight_ref[...], 0.0)
    in_row = lax.broadcasted_iota(jnp.int32, (ROWS, faces), 0) == row
    in_col = (lax.broadcasted_iota(jnp.int32, (LANES, faces), 0) == col).astype(jnp.float32)
    spread = jnp.concatenate(
        [jnp.where(in_row, weight[m : m + 1, :], 0.0) for m in range(modes)], axis=0
    )
    moments_ref[...] = lax.dot_general(
        spread, in_col, (((1,), (1,)), ((), ())), precision=HIGH, preferred_element_type=jnp.float32
    )

    blade = lax.broadcasted_iota(jnp.int32, (1, LANES), 1)
    rows = []
    for yl, x in itertools.product(range(SIZES[1]), range(SIZES[0])):
        rows.append(blade * ids_ref[x * SIZES[1] + yl])
    product = jnp.concatenate(rows, axis=0)
    turns = ((product.astype(jnp.float32) + 0.5) * (1.0 / BLADES)).astype(jnp.int32)
    angle = 2.0 * jnp.pi * (product - turns * BLADES).astype(jnp.float32) / BLADES
    n = len(rows)
    table_ref[0:n, :] = jnp.cos(angle)
    table_ref[n : 2 * n, :] = jnp.sin(angle)
    mine = ids_ref[lax.axis_index("x") * SIZES[1] + lax.axis_index("yl")]
    sigma = jnp.full((8, LANES), mine, jnp.int32).astype(jnp.float32)
    sigma = 2.0 * jnp.pi * sigma / BLADES
    table_ref[2 * n : 2 * n + 8, :] = jnp.cos(sigma)
    table_ref[2 * n + 8 : 2 * n + 16, :] = jnp.sin(sigma)


def sweep_kernel(
    ja_ref, jc_ref, omega_ref, q_ref, s_ref, t_ref, near_ref, far_ref, moments_ref, table_ref,
    out_ref, force_ref, base, first, second, forced, step,
):
    even = lax.axis_index("core") == 0
    edge = jnp.zeros((8, LANES), jnp.float32)
    for buf in (base, first, second):
        for i in range(PLANES):
            buf[i, 0:8, :] = edge
            buf[i, BUF - 8 : BUF, :] = edge

    def put(buf, row, own):
        near = near_ref[pl.ds(row, HALO), :]
        far = far_ref[pl.ds(row, HALO), :]
        buf[TOP:OWN, :] = jnp.where(even, far, near)
        buf[OWN:LOW, :] = own
        buf[LOW : LOW + HALO, :] = jnp.where(even, near, far)

    for i in range(PLANES):
        put(base.at[i], i * HALO, q_ref[i])
        put(forced.at[i], (PLANES + i) * HALO, s_ref[i])
    put(step, 2 * PLANES * HALO, t_ref[...])

    lane = lax.broadcasted_iota(jnp.int32, (8, LANES), 1)
    is_first, is_last = lane == 0, lane == LANES - 1
    cosine = table_ref[32:40, :]
    sine = table_ref[40:48, :]
    turn_c = jnp.where(is_first | is_last, cosine, 1.0)
    turn_s = jnp.where(is_first, -sine, jnp.where(is_last, sine, 0.0))

    def section(cur, new, alpha, row):
        here = pl.ds(row, 8)
        dt = step[here, :] * alpha
        for e in range(2):
            center, axial, circ, total = [], [], [], []
            for c in range(2):
                for v in range(5):
                    i = e * 10 + c * 5 + v
                    center.append(cur[i, here, :])
            for c in range(2):
                for v in range(5):
                    i = e * 10 + c * 5 + v
                    up = cur[i, pl.ds(row + 1, 8), :]
                    down = cur[i, pl.ds(row - 1, 8), :]
                    mid, other = center[c * 5 + v], center[(1 - c) * 5 + v]
                    if c == 0:
                        turned = turn_c * mid + turn_s * other
                    else:
                        turned = turn_c * mid - turn_s * other
                    right = pltpu.roll(jnp.where(is_first, turned, mid), LANES - 1, 1)
                    left = pltpu.roll(jnp.where(is_last, turned, mid), 1, 1)
                    axial.append(up - down)
                    circ.append(right - left)
                    total.append((up + down) + (right + left))
            freq = omega_ref[e]
            for c in range(2):
                for u in range(5):
                    i = e * 10 + c * 5 + u
                    conv = None
                    for v in range(5):
                        a = (ja_ref[u, v] * 0.5) * axial[c * 5 + v]
                        b = (jc_ref[u, v] * 0.5) * circ[c * 5 + v]
                        conv = a + b if conv is None else conv + (a + b)
                    spin = freq * center[(1 - c) * 5 + u]
                    res = conv - 0.2 * total[c * 5 + u] + 0.8 * center[c * 5 + u] - forced[i, here, :]
                    res = res - spin if c == 0 else res + spin
                    new[i, here, :] = base[i, here, :] - dt * res

    bufs = (base, first, second, first, base)
    for it in range(ITERS):
        for k in range(SECTIONS):
            reach = HALO - 1 - (it * SECTIONS + k)
            start = OWN - reach
            tiles = (ROWS + 2 * reach + 7) // 8

            def body(j, carry, cur=bufs[k], new=bufs[k + 1], alpha=ALPHAS[k], start=start):
                section(cur, new, alpha, start + j * 8)
                return carry

            lax.fori_loop(0, tiles, body, 0)

    for i in range(PLANES):
        out_ref[i] = base[i, OWN:LOW, :]

    sums = []
    modes = moments_ref.shape[0] // ROWS
    for m in range(modes):
        for ec in range(4):
            acc = None
            for r in range(0, ROWS, 8):
                term = moments_ref[m * ROWS + r : m * ROWS + r + 8, :] * base[ec * 5 + 4, OWN + r : OWN + r + 8, :]
                acc = term if acc is None else acc + term
            sums.append(acc)
    stacked = jnp.concatenate(sums, axis=0)
    count = len(sums)
    pick = lax.broadcasted_iota(jnp.int32, (LANES, count * 8), 1) // 8
    pick = (pick == lax.broadcasted_iota(jnp.int32, (LANES, count * 8), 0)).astype(jnp.float32)
    by_lane = jnp.dot(pick, stacked, precision=HIGH, preferred_element_type=jnp.float32)
    ones = jnp.ones(force_ref.shape, jnp.float32)
    force_ref[...] = lax.dot_general(
        ones, by_lane, (((1,), (1,)), ((), ())), precision=HIGH, preferred_element_type=jnp.float32
    )


def middle_kernel(in_ref, out_ref):
    got = in_ref[...]
    mine = lax.axis_index("yl")
    lane = lax.broadcasted_iota(jnp.int32, (1, LANES), 1)
    keep = (lane % 16 < 4) & (lane < 64)
    total = None
    for yl in range(SIZES[1]):
        part = jnp.sum(got[yl * 4 : yl * 4 + 4, :], axis=0, keepdims=True)
        part = pltpu.roll(part, (LANES - 4 * mine) % LANES, 1)
        part = jnp.where(keep, part, 0.0)
        if yl:
            part = pltpu.roll(part, 4 * yl, 1)
        total = part if total is None else total + part
    out_ref[...] = jnp.broadcast_to(total, out_ref.shape)


def final_kernel(in_ref, table_ref, out_ref):
    mine = lax.axis_index("x")
    depth = SIZES[2]
    parts = [
        jnp.sum(in_ref[x * depth : (x + 1) * depth, :], axis=0, keepdims=True) for x in range(SIZES[0])
    ]
    force = pltpu.roll(jnp.concatenate(parts, axis=0), (LANES - 16 * mine) % LANES, 1)
    n = SIZES[0] * SIZES[1]
    for e in range(2):
        real, imag = None, None
        for yl in range(SIZES[1]):
            at = yl * 4 + e * 2
            f_r = force[:, at : at + 1]
            f_i = force[:, at + 1 : at + 2]
            cosine = table_ref[yl * 4 : yl * 4 + 4, :]
            sine = table_ref[n + yl * 4 : n + yl * 4 + 4, :]
            r = f_r * cosine - f_i * sine
            i = f_r * sine + f_i * cosine
            real = r if real is None else real + r
            imag = i if imag is None else imag + i
        scale = 1.0 / BLADES
        out_ref[0, 0, e : e + 1, :] = (jnp.sum(real, axis=0, keepdims=True) * scale)[:, :BLADES]
        out_ref[0, 1, e : e + 1, :] = (jnp.sum(imag, axis=0, keepdims=True) * scale)[:, :BLADES]


def shape(*dims):
    return jax.ShapeDtypeStruct(dims, jnp.float32)


VMEM = pl.BlockSpec(memory_space=pltpu.VMEM)
SMEM = pl.BlockSpec(memory_space=pltpu.SMEM)


def call(kernel, out_shape, in_specs, scratch=(), cost=(1000, 1000)):
    return pl.pallas_call(
        kernel,
        out_shape=out_shape,
        in_specs=in_specs,
        out_specs=jax.tree.map(lambda _: VMEM, out_shape),
        scratch_shapes=list(scratch),
        compiler_params=pltpu.CompilerParams(vmem_limit_bytes=32 * 1024 * 1024),
        cost_estimate=pl.CostEstimate(flops=cost[0], bytes_accessed=cost[1], transcendentals=0),
    )


def per_device(
    perturbation, source, time_step, jac_axial, jac_circ, omega, diam_ids, surf_cell, surf_weight, face_count
):
    q = perturbation.reshape(PLANES, ROWS, LANES)
    src = source.reshape(PLANES, ROWS, LANES)
    near, far = call(pack_kernel, (shape(MSG, LANES),) * 2, [VMEM] * 3)(q, src, time_step)
    far = lax.ppermute(far, AXES, swap_pairs(False))
    near = lax.ppermute(near, AXES, swap_pairs(True))
    moments, table = call(
        prep_kernel, (shape(16 * ROWS, LANES), shape(48, LANES)), [VMEM, VMEM, SMEM, SMEM], cost=(400_000_000, 1_000_000)
    )(surf_cell.reshape(1, -1), surf_weight, face_count, diam_ids)
    big = pltpu.VMEM((PLANES, BUF, LANES), jnp.float32)
    result, force = call(
        sweep_kernel,
        (shape(PLANES, ROWS, LANES), shape(16, LANES)),
        [SMEM] * 3 + [VMEM] * 7,
        [big, big, big, big, pltpu.VMEM((BUF, LANES), jnp.float32)],
        cost=(100_000_000, 2_000_000),
    )(jac_axial, jac_circ, omega, q, src, time_step, near, far, moments, table)
    got = lax.all_to_all(force, ("yl", "yh", "core"), 0, 0, tiled=True)
    middle = call(middle_kernel, shape(32, LANES), [VMEM])(got)
    got = lax.all_to_all(middle, ("x", "z"), 0, 0, tiled=True)
    influence = call(final_kernel, shape(1, 2, 2, BLADES), [VMEM, VMEM])(got, table)
    return result.reshape(perturbation.shape), influence


def solution(mesh):
    fine = Mesh(mesh.devices.reshape(SIZES), AXES)
    diam, blocks = ("x", "yl"), ("z", "yh", "core")
    in_specs = (
        P(diam, None, None, None, blocks, None),
        P(None, None, None, blocks, None),
        P(blocks, None),
        P(),
        P(),
        P(),
        P(),
        P(blocks),
        P(None, blocks),
        P(blocks),
    )
    out_specs = (P(diam, None, None, None, blocks, None), P(diam, None, None, None))
    return jax.shard_map(per_device, mesh=fine, in_specs=in_specs, out_specs=out_specs, check_vma=False)
```

time: 382 us -> 75.9 us (0.20)
  the two profiles are of different devices: /device:TPU:256 before, /device:TPU:1 now
where the time goes in v1:
time: 75.9 us; the launch traced here: 75.4 us
  blocking collectives  36.3 us (48%)
  Pallas kernels  15.3 us (20%)
  starting transfers between devices  10.8 us (14%)
  waiting for transfers between devices  7.83 us (10%)
  local copies, waits for them, and re-layouts  3.95 us (5%)
  between operations  1.36 us (2%)
    all_to_all x1, blocking collectives, per_device(): got = lax.all_to_all(middle, ('x', 'z'), 0, 0, tiled=True)  20.9 us
    all_to_all x1, blocking collectives, per_device(): got = lax.all_to_all(force, ('yl', 'yh', 'core'), 0, 0, tiled=True)  15.4 us
    pallas_call x1, Pallas kernels, per_device(): call(sweep_kernel, (shape(PLANES, ROWS, LANES), shape(16, LANES)), [SMEM]...  12.6 us
    ppermute x1, starting transfers between devices, per_device(): near = lax.ppermute(near, AXES, swap_pairs(True))  8.79 us
    ppermute x1, waiting for transfers between devices, per_device(): far = lax.ppermute(far, AXES, swap_pairs(False))  7.83 us
    unnamed x20, local copies, waits for them, and re-layouts  3.95 us
    ppermute x1, starting transfers between devices, per_device(): far = lax.ppermute(far, AXES, swap_pairs(False))  1.98 us
    pallas_call x1, Pallas kernels, per_device(): call(prep_kernel, (shape(16 * ROWS, LANES), shape(48, LANES)), [VMEM, VME...  1.67 us
  transfers between devices with their start and end apart: 2, of which 1 were waited for; matrix products, arithmetic and copies ran while one was open for 0% of the time, Pallas kernels for 2%

profile of v1, /device:TPU:1, one launch (start us, length us, event | category | flops | bytes accessed | tf_op | source)
XLA Modules:
  0.0 75.4 jit_solution(1301469176688040035)
XLA Ops:
  0.6 0.0 copy-start
  0.6 1.0 %copy-done = f32[1,2,2,5,32,128]{5,4,3,2,1,0:T(8,128)S(1)} copy-done((f32[1,2,2,5,32,128]{5,4,3,2,1,0:T(8,128)S(1)}, f32[1,2,2,5,32,128]{5,4,3,2,1,0:T(8,128)}, u32[]{:S(2)}) %copy-start) | copy-done | bytes 327704
  1.6 1.0 %copy-done.2 = f32[2,2,5,32,128]{4,3,2,1,0:T(8,128)S(1)} copy-done((f32[2,2,5,32,128]{4,3,2,1,0:T(8,128)S(1)}, f32[2,2,5,32,128]{4,3,2,1,0:T(8,128)}, u32[]{:S(2)}) %copy-start.2) | copy-done | bytes 327704
  2.6 0.7 copy-done.3
  3.3 0.1 shard_map.113
  3.4 8.8 %collective-permute-start = (f32[496,128]{1,0:T(8,128)S(1)}, f32[496,128]{1,0:T(8,128)S(1)}, u32[]{:S(2)}, u32[]{:S(2)}) collective-permute-start(f32[496,128]{1,0:T(8,128)S(1)} %get-tuple-element.8), channel_id=1, source_target_pairs={{0,1},{1,0},{2,3},{3,2},{4,5},{5,4},{6,7},{7,6},{8,9},{9,8},{10,11... | collective-permute-start | bytes 761864 | tf_op jit(solution)/shard_map/ppermute | solution.py:273
  12.2 0.0 copy-start.8
  12.2 2.0 %collective-permute-start.1 = (f32[496,128]{1,0:T(8,128)S(1)}, f32[496,128]{1,0:T(8,128)S(1)}, u32[]{:S(2)}, u32[]{:S(2)}) collective-permute-start(f32[496,128]{1,0:T(8,128)S(1)} %get-tuple-element.9), channel_id=1, source_target_pairs={{1,2},{2,1},{3,4},{4,3},{5,6},{6,5},{7,8},{8,7},{9,10},{10,9},{11,... | collective-permute-start | bytes 761864 | tf_op jit(solution)/shard_map/ppermute | solution.py:272
  14.8 0.0 copy-start.9
  14.8 0.0 copy-done.7
  14.8 0.0 copy-done.8
  14.8 0.6 copy-done.9
  15.5 1.7 %shard_map.114 = (f32[512,128]{1,0:T(8,128)S(1)}, f32[48,128]{1,0:T(8,128)S(1)}) custom-call(s32[1,512]{1,0:T(1,128)S(1)} %bitcast.20, f32[16,512]{1,0:T(8,128)S(1)} %copy-done.7, s32[1]{0:T(128)S(6)} %copy.14.count_ref, s32[16]{0:T(128)S(1)} %copy-done.9), custom_call_target="tpu_custom_call" | custom-call | flops 400000000 | bytes 1000000 | tf_op jit(solution)/shard_map/pallas_call | solution.py:274
  17.1 0.0 collective-permute-done.near_ref
  17.1 7.8 %collective-permute-done.1.far_ref = f32[496,128]{1,0:T(8,128)S(1)} collective-permute-done((f32[496,128]{1,0:T(8,128)S(1)}, f32[496,128]{1,0:T(8,128)S(1)}, u32[]{:S(2)}, u32[]{:S(2)}) %collective-permute-start.1) | collective-permute-done | bytes 253984 | tf_op jit(solution)/shard_map/ppermute | solution.py:272
  25.0 0.0 copy-done.1
  25.0 0.0 copy-done.4
  25.0 0.0 copy-done.5
  25.0 0.6 copy-done.6
  25.6 12.6 %shard_map.115 = (f32[20,32,128]{2,1,0:T(8,128)}, f32[16,128]{1,0:T(8,128)S(1)}) custom-call(f32[5,5]{1,0:T(8,128)S(1)} %copy-done.4, f32[5,5]{1,0:T(8,128)S(1)} %copy-done.5, f32[2]{0:T(128)S(1)} %copy-done.6, f32[20,32,128]{2,1,0:T(8,128)S(1)} %bitcast.13, f32[20,32,128]{2,1,0:T(8,128)S(1)} %bitcast.15, f32[32,128]{1,0:T(8,128)S(1)} %copy-done.3, ...), custom_call_target="tpu_custom_call" | custom-call | flops 100000000 | bytes 2000000 | tf_op jit(solution)/shard_map/pallas_call | solution.py:278
  38.3 15.4 %all_to_all.22 = f32[16,1,128]{2,1,0:T(1,128)S(1)} all-to-all(f32[16,1,128]{2,1,0:T(1,128)S(1)} %bitcast.19), channel_id=1, replica_groups=mesh['x'=4,'yl'=4,'z'=8,'yh'=2,'core'=2] {'yl','yh','core'}, dimensions={0} | all-to-all | bytes 16384 | tf_op jit(solution)/shard_map/all_to_all | solution.py:285
  53.7 0.1 shard_map.116
  53.8 20.9 %all_to_all.23 = f32[32,1,128]{2,1,0:T(1,128)S(1)} all-to-all(f32[32,1,128]{2,1,0:T(1,128)S(1)} %bitcast.17), channel_id=1, replica_groups=mesh['x'=4,'yl'=4,'z'=8,'yh'=2,'core'=2] {'x','z'}, dimensions={0} | all-to-all | bytes 32768 | tf_op jit(solution)/shard_map/all_to_all | solution.py:287
  74.7 0.8 %shard_map.117 = f32[1,2,2,72]{3,2,1,0:T(2,128)} custom-call(f32[32,128]{1,0:T(8,128)S(1)} %bitcast.16, f32[48,128]{1,0:T(8,128)S(1)} %get-tuple-element.11.table_ref), custom_call_target="tpu_custom_call" | custom-call | flops 1000 | bytes 1000 | tf_op jit(solution)/shard_map/pallas_call | solution.py:288
  (7 shorter events, 0.0 us)
Async XLA Ops:
  0.6 1.0 %copy-start = (f32[1,2,2,5,32,128]{5,4,3,2,1,0:T(8,128)S(1)}, f32[1,2,2,5,32,128]{5,4,3,2,1,0:T(8,128)}, u32[]{:S(2)}) copy-start(f32[1,2,2,5,32,128]{5,4,3,2,1,0:T(8,128)} %param.10) | copy-start | bytes 983044
  1.6 1.0 %copy-start.2 = (f32[2,2,5,32,128]{4,3,2,1,0:T(8,128)S(1)}, f32[2,2,5,32,128]{4,3,2,1,0:T(8,128)}, u32[]{:S(2)}) copy-start(f32[2,2,5,32,128]{4,3,2,1,0:T(8,128)} %param.11) | copy-start | bytes 983044
  2.6 0.7 copy-start.3
  3.3 11.5 %copy-start.7 = (f32[16,512]{1,0:T(8,128)S(1)}, f32[16,512]{1,0:T(8,128)}, u32[]{:S(2)}) copy-start(f32[16,512]{1,0:T(8,128)} %weight_ref.1) | copy-start | bytes 98308
  3.4 13.8 %collective-permute-start = (f32[496,128]{1,0:T(8,128)S(1)}, f32[496,128]{1,0:T(8,128)S(1)}, u32[]{:S(2)}, u32[]{:S(2)}) collective-permute-start(f32[496,128]{1,0:T(8,128)S(1)} %get-tuple-element.8), channel_id=1, source_target_pairs={{0,1},{1,0},{2,3},{3,2},{4,5},{5,4},{6,7},{7,6},{8,9},{9,8},{10,11... | collective-permute-start | bytes 761864 | tf_op jit(solution)/shard_map/ppermute | solution.py:273
  12.2 2.7 %copy-start.8 = (s32[512]{0:T(512)S(1)}, s32[512]{0:T(512)}, u32[]{:S(2)}) copy-start(s32[512]{0:T(512)} %param.17) | copy-start | bytes 6148
  12.2 12.8 %collective-permute-start.1 = (f32[496,128]{1,0:T(8,128)S(1)}, f32[496,128]{1,0:T(8,128)S(1)}, u32[]{:S(2)}, u32[]{:S(2)}) collective-permute-start(f32[496,128]{1,0:T(8,128)S(1)} %get-tuple-element.9), channel_id=1, source_target_pairs={{1,2},{2,1},{3,4},{4,3},{5,6},{6,5},{7,8},{8,7},{9,10},{10,9},{11,... | collective-permute-start | bytes 761864 | tf_op jit(solution)/shard_map/ppermute | solution.py:272
  14.8 0.7 copy-start.9
  15.5 9.5 %copy-start.1 = (f32[1,2,2,5,32,128]{5,4,3,2,1,0:T(8,128)S(1)}, f32[1,2,2,5,32,128]{5,4,3,2,1,0:T(8,128)}, u32[]{:S(2)}) copy-start(f32[1,2,2,5,32,128]{5,4,3,2,1,0:T(8,128)} %param.10) | copy-start | bytes 983044
  15.5 9.5 %copy-start.4 = (f32[5,5]{1,0:T(8,128)S(1)}, f32[5,5]{1,0:T(8,128)}, u32[]{:S(2)}) copy-start(f32[5,5]{1,0:T(8,128)} %ja_ref.1) | copy-start | bytes 304
  15.5 9.5 %copy-start.5 = (f32[5,5]{1,0:T(8,128)S(1)}, f32[5,5]{1,0:T(8,128)}, u32[]{:S(2)}) copy-start(f32[5,5]{1,0:T(8,128)} %jc_ref.1) | copy-start | bytes 304
  25.0 0.7 copy-start.6

commit v2 on v1

v2 whole, which is shorter than its diff:
```python
import itertools

import jax
import jax.numpy as jnp
from jax import lax
from jax.experimental import pallas as pl
from jax.experimental.pallas import tpu as pltpu
from jax.sharding import Mesh
from jax.sharding import PartitionSpec as P

BLADES = 72
ITERS = 3
SECTIONS = 4
HALO = ITERS * SECTIONS
ALPHAS = (0.25, 1.0 / 3.0, 0.5, 1.0)
HIGH = lax.Precision.HIGHEST
AXES = ("x", "yl", "z", "yh", "core")
SIZES = (4, 4, 8, 2, 2)
PLANES = 20
ROWS = 32
LANES = 128
MSG = 2 * PLANES * HALO + 16
LEVELS = HALO
OWN = 8
PART = 32
TILE = 8


def flat(*coords):
    out = 0
    for c, n in zip(coords, SIZES):
        out = out * n + c
    return out


def swap_pairs(same_chip):
    pairs = []
    blocks = SIZES[2] * SIZES[3] * SIZES[4]
    for x, yl, p in itertools.product(range(SIZES[0]), range(SIZES[1]), range(blocks)):
        if same_chip:
            q = p ^ 1
        else:
            q = p + 1 if p % 2 else p - 1
        if 0 <= q < blocks:
            ends = [flat(x, yl, b // 4, (b // 2) % 2, b % 2) for b in (p, q)]
            pairs.append(tuple(ends))
    return pairs


def pack_kernel(q_ref, s_ref, t_ref, near_ref, far_ref, q_buf, s_buf, t_buf, sems):
    core = lax.axis_index("core")
    wide = q_buf.shape[2]
    copies = []
    for side in range(2):
        start = (core if side == 0 else 1 - core) * (ROWS - wide)
        rows = pl.ds(pl.multiple_of(start, TILE), wide)
        copies.append(pltpu.make_async_copy(q_ref.at[:, rows, :], q_buf.at[side], sems.at[side, 0]))
        copies.append(pltpu.make_async_copy(s_ref.at[:, rows, :], s_buf.at[side], sems.at[side, 1]))
        copies.append(pltpu.make_async_copy(t_ref.at[rows, :], t_buf.at[side], sems.at[side, 2]))
    for copy in copies:
        copy.start()
    for side, out in ((0, far_ref), (1, near_ref)):
        for copy in copies[side * 3 : side * 3 + 3]:
            copy.wait()
        shift = (core if side == 0 else 1 - core) * (wide - HALO)
        rows = pl.ds(shift, HALO)
        for i in range(PLANES):
            out[i * HALO : (i + 1) * HALO, :] = q_buf[side, i, rows, :]
            out[(PLANES + i) * HALO : (PLANES + i + 1) * HALO, :] = s_buf[side, i, rows, :]
        at = 2 * PLANES * HALO
        out[at : at + HALO, :] = t_buf[side, rows, :]
        out[at + HALO :, :] = jnp.zeros((MSG - at - HALO, LANES), jnp.float32)


def coefficients(ja_ref, jc_ref, coef):
    for u in range(5):
        for v in range(5):
            coef[u * 5 + v] = jnp.full((TILE, LANES), ja_ref[u, v] * 2.5, jnp.float32)
            coef[25 + u * 5 + v] = jnp.full((TILE, LANES), jc_ref[u, v] * 2.5, jnp.float32)


def phases(table_ref):
    lane = lax.broadcasted_iota(jnp.int32, (TILE, LANES), 1)
    is_first, is_last = lane == 0, lane == LANES - 1
    cosine = table_ref[32:40, :]
    sine = table_ref[40:48, :]
    turn_c = jnp.where(is_first | is_last, cosine, 1.0)
    turn_s = jnp.where(is_first, -sine, jnp.where(is_last, sine, 0.0))
    return is_first, is_last, turn_c, turn_s


def tile_update(cur, base, new, forced, step, coef, omega_ref, phase, alpha, row):
    is_first, is_last, turn_c, turn_s = phase
    here = pl.ds(row, TILE)
    dt = step[here, :] * (alpha * 0.2)
    for e in range(2):
        center, axial, circ, total = [], [], [], []
        for c in range(2):
            for v in range(5):
                center.append(cur[e * 10 + c * 5 + v, here, :])
        for c in range(2):
            for v in range(5):
                i = e * 10 + c * 5 + v
                up = cur[i, pl.ds(row + 1, TILE), :]
                down = cur[i, pl.ds(row - 1, TILE), :]
                mid, other = center[c * 5 + v], center[(1 - c) * 5 + v]
                turned = turn_c * mid + turn_s * other if c == 0 else turn_c * mid - turn_s * other
                right = pltpu.roll(jnp.where(is_first, turned, mid), LANES - 1, 1)
                left = pltpu.roll(jnp.where(is_last, turned, mid), 1, 1)
                axial.append(up - down)
                circ.append(right - left)
                total.append((up + down) + (right + left))
        freq = omega_ref[e] * 5.0
        for c in range(2):
            for u in range(5):
                i = e * 10 + c * 5 + u
                acc = total[c * 5 + u] + forced[i, here, :] - 4.0 * center[c * 5 + u]
                spin = freq * center[(1 - c) * 5 + u]
                acc = acc + spin if c == 0 else acc - spin
                conv = None
                for v in range(5):
                    a = coef[u * 5 + v] * axial[c * 5 + v]
                    b = coef[25 + u * 5 + v] * circ[c * 5 + v]
                    conv = a + b if conv is None else conv + (a + b)
                new[i, here, :] = base[i, here, :] + dt * (acc - conv)


def make_moments(cell_ref, weight_ref, count_ref, moments_ref):
    faces = cell_ref.shape[1]
    modes = weight_ref.shape[0]
    cell = cell_ref[...]
    row = lax.shift_right_logical(cell, 7)
    col = jnp.bitwise_and(cell, LANES - 1)
    live = lax.broadcasted_iota(jnp.int32, (1, faces), 1) < count_ref[0]
    weight = jnp.where(live, weight_ref[...], 0.0)
    in_row = lax.broadcasted_iota(jnp.int32, (ROWS, faces), 0) == row
    in_col = (lax.broadcasted_iota(jnp.int32, (LANES, faces), 0) == col).astype(jnp.float32)
    spread = jnp.concatenate(
        [jnp.where(in_row, weight[m : m + 1, :], 0.0) for m in range(modes)], axis=0
    )
    moments_ref[...] = lax.dot_general(
        spread, in_col, (((1,), (1,)), ((), ())), precision=HIGH, preferred_element_type=jnp.float32
    )


def make_tables(ids_ref, table_ref):
    blade = lax.broadcasted_iota(jnp.int32, (1, LANES), 1)
    rows = []
    for yl, x in itertools.product(range(SIZES[1]), range(SIZES[0])):
        rows.append(blade * ids_ref[x * SIZES[1] + yl])
    product = jnp.concatenate(rows, axis=0)
    turns = ((product.astype(jnp.float32) + 0.5) * (1.0 / BLADES)).astype(jnp.int32)
    angle = 2.0 * jnp.pi * (product - turns * BLADES).astype(jnp.float32) / BLADES
    n = len(rows)
    table_ref[0:n, :] = jnp.cos(angle)
    table_ref[n : 2 * n, :] = jnp.sin(angle)
    mine = ids_ref[lax.axis_index("x") * SIZES[1] + lax.axis_index("yl")]
    sigma = jnp.full((TILE, LANES), mine, jnp.int32).astype(jnp.float32)
    sigma = 2.0 * jnp.pi * sigma / BLADES
    table_ref[2 * n : 2 * n + 8, :] = jnp.cos(sigma)
    table_ref[2 * n + 8 : 2 * n + 16, :] = jnp.sin(sigma)


def inner_kernel(
    cell_ref, weight_ref, count_ref, ids_ref, ja_ref, jc_ref, omega_ref, q_ref, s_ref, t_ref,
    moments_ref, table_ref, rim_ref, core_ref, base, first, second, forced, step, coef,
):
    make_moments(cell_ref, weight_ref, count_ref, moments_ref)
    make_tables(ids_ref, table_ref)
    coefficients(ja_ref, jc_ref, coef)
    phase = phases(table_ref)
    own = pl.ds(OWN, ROWS)
    for i in range(PLANES):
        base[i, own, :] = q_ref[i]
        forced[i, own, :] = s_ref[i] * 5.0
    step[own, :] = t_ref[...]

    bufs = (base, first, second, first, base)
    for t in range(1, LEVELS + 1):
        k = (t - 1) % SECTIONS
        cur, new = bufs[k], bufs[k + 1]
        valid = ROWS - 2 * t
        tiles = (valid + TILE - 1) // TILE

        def body(j, carry, cur=cur, new=new, alpha=ALPHAS[k], t=t, valid=valid, tiles=tiles):
            row = OWN + t + j * TILE
            tile_update(cur, base, new, forced, step, coef, omega_ref, phase, alpha, row)
            return carry

        lax.fori_loop(0, tiles, body, 0)
        if t < LEVELS:
            for i in range(PLANES):
                rim_ref[t - 1, i, 0:4, :] = new[i, OWN + t : OWN + t + 4, :]
                rim_ref[t - 1, i, 4:8, :] = new[i, OWN + ROWS - 4 - t : OWN + ROWS - t, :]
        else:
            for i in range(PLANES):
                core_ref[i] = new[i, OWN + t : OWN + ROWS - t, :]


def rim_kernel(
    ja_ref, jc_ref, omega_ref, q_ref, s_ref, t_ref, near_ref, far_ref, moments_ref, table_ref, rim_ref, core_ref,
    out_ref, force_ref, base, other, first, second, forced, step, coef,
):
    even = lax.axis_index("core") == 0
    coefficients(ja_ref, jc_ref, coef)
    phase = phases(table_ref)
    edge = jnp.zeros((4, LANES), jnp.float32)

    def put(buf, at, top, low, scale):
        near = near_ref[pl.ds(at, HALO), :]
        far = far_ref[pl.ds(at, HALO), :]
        buf[0:4, :] = edge
        buf[4:16, :] = jnp.where(even, far, near) * scale
        buf[16:PART, :] = top * scale
        buf[PART : PART + 16, :] = low * scale
        buf[PART + 16 : PART + 28, :] = jnp.where(even, near, far) * scale
        buf[PART + 28 : PART + 32, :] = edge

    for i in range(PLANES):
        put(base.at[i], i * HALO, q_ref[i, 0:16, :], q_ref[i, 16:32, :], 1.0)
        put(forced.at[i], (PLANES + i) * HALO, s_ref[i, 0:16, :], s_ref[i, 16:32, :], 5.0)
        for buf in (other, first, second):
            buf[i, 0:8, :] = jnp.zeros((8, LANES), jnp.float32)
            buf[i, PART + 24 : PART + 32, :] = jnp.zeros((8, LANES), jnp.float32)
    put(step, 2 * PLANES * HALO, t_ref[0:16, :], t_ref[16:32, :], 1.0)

    for it in range(ITERS):
        start, end = (base, other) if it % 2 == 0 else (other, base)
        bufs = (start, first, second, first, end)
        for k in range(SECTIONS):
            t = it * SECTIONS + k + 1
            cur, new = bufs[k], bufs[k + 1]
            for row in (4 + t, 8 + t, PART + 16 - t, PART + 20 - t):
                tile_update(cur, start, new, forced, step, coef, omega_ref, phase, ALPHAS[k], row)
            if t < LEVELS:
                for i in range(PLANES):
                    new[i, 16 + t : 20 + t, :] = rim_ref[t - 1, i, 0:4, :]
                    new[i, PART + 12 - t : PART + 16 - t, :] = rim_ref[t - 1, i, 4:8, :]
    for i in range(PLANES):
        out_ref[i, 0:HALO, :] = end[i, 16 : 16 + HALO, :]
        out_ref[i, HALO : ROWS - HALO, :] = core_ref[i]
        out_ref[i, ROWS - HALO : ROWS, :] = end[i, PART + 4 : PART + 16, :]

    sums = []
    modes = moments_ref.shape[0] // ROWS
    for m in range(modes):
        for ec in range(4):
            acc = None
            for r in range(0, ROWS, TILE):
                term = moments_ref[m * ROWS + r : m * ROWS + r + TILE, :] * out_ref[ec * 5 + 4, r : r + TILE, :]
                acc = term if acc is None else acc + term
            sums.append(acc)
    stacked = jnp.concatenate(sums, axis=0)
    count = len(sums)
    pick = lax.broadcasted_iota(jnp.int32, (LANES, count * TILE), 1) // TILE
    pick = (pick == lax.broadcasted_iota(jnp.int32, (LANES, count * TILE), 0)).astype(jnp.float32)
    by_lane = jnp.dot(pick, stacked, precision=HIGH, preferred_element_type=jnp.float32)
    ones = jnp.ones(force_ref.shape, jnp.float32)
    force_ref[...] = lax.dot_general(
        ones, by_lane, (((1,), (1,)), ((), ())), precision=HIGH, preferred_element_type=jnp.float32
    )


def middle_kernel(in_ref, out_ref):
    got = in_ref[...]
    mine = lax.axis_index("yl")
    lane = lax.broadcasted_iota(jnp.int32, (1, LANES), 1)
    keep = (lane % 16 < 4) & (lane < 64)
    total = None
    for yl in range(SIZES[1]):
        part = jnp.sum(got[yl * 4 : yl * 4 + 4, :], axis=0, keepdims=True)
        part = pltpu.roll(part, (LANES - 4 * mine) % LANES, 1)
        part = jnp.where(keep, part, 0.0)
        if yl:
            part = pltpu.roll(part, 4 * yl, 1)
        total = part if total is None else total + part
    out_ref[...] = jnp.broadcast_to(total, out_ref.shape)


def final_kernel(in_ref, table_ref, out_ref):
    mine = lax.axis_index("x")
    depth = SIZES[2]
    parts = [
        jnp.sum(in_ref[x * depth : (x + 1) * depth, :], axis=0, keepdims=True) for x in range(SIZES[0])
    ]
    force = pltpu.roll(jnp.concatenate(parts, axis=0), (LANES - 16 * mine) % LANES, 1)
    n = SIZES[0] * SIZES[1]
    for e in range(2):
        real, imag = None, None
        for yl in range(SIZES[1]):
            at = yl * 4 + e * 2
            f_r = force[:, at : at + 1]
            f_i = force[:, at + 1 : at + 2]
            cosine = table_ref[yl * 4 : yl * 4 + 4, :]
            sine = table_ref[n + yl * 4 : n + yl * 4 + 4, :]
            r = f_r * cosine - f_i * sine
            i = f_r * sine + f_i * cosine
            real = r if real is None else real + r
            imag = i if imag is None else imag + i
        scale = 1.0 / BLADES
        out_ref[0, 0, e : e + 1, :] = (jnp.sum(real, axis=0, keepdims=True) * scale)[:, :BLADES]
        out_ref[0, 1, e : e + 1, :] = (jnp.sum(imag, axis=0, keepdims=True) * scale)[:, :BLADES]


def shape(*dims):
    return jax.ShapeDtypeStruct(dims, jnp.float32)


VMEM = pl.BlockSpec(memory_space=pltpu.VMEM)
SMEM = pl.BlockSpec(memory_space=pltpu.SMEM)
ANY = pl.BlockSpec(memory_space=pltpu.HBM)


def call(kernel, out_shape, in_specs, scratch=(), cost=(1000, 1000)):
    return pl.pallas_call(
        kernel,
        out_shape=out_shape,
        in_specs=in_specs,
        out_specs=jax.tree.map(lambda _: VMEM, out_shape),
        scratch_shapes=list(scratch),
        compiler_params=pltpu.CompilerParams(vmem_limit_bytes=32 * 1024 * 1024),
        cost_estimate=pl.CostEstimate(flops=cost[0], bytes_accessed=cost[1], transcendentals=0),
    )


def per_device(
    perturbation, source, time_step, jac_axial, jac_circ, omega, diam_ids, surf_cell, surf_weight, face_count
):
    q = perturbation.reshape(PLANES, ROWS, LANES)
    src = source.reshape(PLANES, ROWS, LANES)
    edges = pltpu.VMEM((2, PLANES, 16, LANES), jnp.float32)
    near, far = call(
        pack_kernel,
        (shape(MSG, LANES),) * 2,
        [ANY] * 3,
        [edges, edges, pltpu.VMEM((2, 16, LANES), jnp.float32), pltpu.SemaphoreType.DMA((2, 3))],
    )(*(pltpu.with_memory_space_constraint(a, pltpu.HBM) for a in (q, src, time_step)))
    near = lax.ppermute(near, AXES, swap_pairs(True))
    far = lax.ppermute(far, AXES, swap_pairs(False))
    coef = pltpu.VMEM((50, TILE, LANES), jnp.float32)
    big = pltpu.VMEM((PLANES, ROWS + 16, LANES), jnp.float32)
    moments, table, rim, core = call(
        inner_kernel,
        (shape(16 * ROWS, LANES), shape(48, LANES), shape(LEVELS - 1, PLANES, TILE, LANES), shape(PLANES, TILE, LANES)),
        [VMEM, VMEM] + [SMEM] * 5 + [VMEM] * 3,
        [big, big, big, big, pltpu.VMEM((ROWS + 16, LANES), jnp.float32), coef],
        cost=(400_000_000, 1_000_000),
    )(surf_cell.reshape(1, -1), surf_weight, face_count, diam_ids, jac_axial, jac_circ, omega, q, src, time_step)
    big = pltpu.VMEM((PLANES, 2 * PART, LANES), jnp.float32)
    result, force = call(
        rim_kernel,
        (shape(PLANES, ROWS, LANES), shape(16, LANES)),
        [SMEM] * 3 + [VMEM] * 9,
        [big] * 5 + [pltpu.VMEM((2 * PART, LANES), jnp.float32), coef],
        cost=(100_000_000, 2_000_000),
    )(jac_axial, jac_circ, omega, q, src, time_step, near, far, moments, table, rim, core)
    got = lax.all_to_all(force, ("yl", "yh", "core"), 0, 0, tiled=True)
    middle = call(middle_kernel, shape(32, LANES), [VMEM])(got)
    got = lax.all_to_all(middle, ("x", "z"), 0, 0, tiled=True)
    influence = call(final_kernel, shape(1, 2, 2, BLADES), [VMEM, VMEM])(got, table)
    return result.reshape(perturbation.shape), influence


def solution(mesh):
    fine = Mesh(mesh.devices.reshape(SIZES), AXES)
    diam, blocks = ("x", "yl"), ("z", "yh", "core")
    in_specs = (
        P(diam, None, None, None, blocks, None),
        P(None, None, None, blocks, None),
        P(blocks, None),
        P(),
        P(),
        P(),
        P(),
        P(blocks),
        P(None, blocks),
        P(blocks),
    )
    out_specs = (P(diam, None, None, None, blocks, None), P(diam, None, None, None))
    return jax.shard_map(per_device, mesh=fine, in_specs=in_specs, out_specs=out_specs, check_vma=False)
```

time: 75.9 us -> 68.7 us (0.905)
  waiting for transfers between devices: 7.83 us -> 1.01 us
  local copies, waits for them, and re-layouts: 3.95 us -> 2.07 us
  Pallas kernels: 15.3 us -> 16.8 us
    ppermute x1, waiting for transfers between devices: 7.83 us -> 1.01 us  [per_device(): far = lax.ppermute(far, AXES, swap_pairs(False))]
    unnamed x20 -> x18, local copies, waits for them, and re-layouts: 3.95 us -> 2.07 us
    pallas_call x3, Pallas kernels: 14.4 us -> 15.9 us  [the longest x1 7.53 us: per_device(): call(rim_kernel, (shape(PLANES, ROWS, LANES), shape(16, LANES)), [SMEM] *...]
  transfers between devices with their start and end apart: 2 -> 2, of which waited for: 1 -> 1; matrix products, arithmetic and copies ran while one was open for 0% -> 0% of each run, Pallas kernels for 2% -> 10%
where the time goes in v2:
time: 68.7 us; the launch traced here: 68.3 us
  blocking collectives  36.3 us (53%)
  Pallas kernels  16.8 us (24%)
  starting transfers between devices  10.8 us (16%)
  local copies, waits for them, and re-layouts  2.07 us (3%)
  between operations  1.42 us (2%)
  waiting for transfers between devices  1.01 us (1%)
    all_to_all x1, blocking collectives, per_device(): got = lax.all_to_all(middle, ('x', 'z'), 0, 0, tiled=True)  20.9 us
    all_to_all x1, blocking collectives, per_device(): got = lax.all_to_all(force, ('yl', 'yh', 'core'), 0, 0, tiled=True)  15.4 us
    ppermute x1, starting transfers between devices, per_device(): near = lax.ppermute(near, AXES, swap_pairs(True))  8.79 us
    pallas_call x1, Pallas kernels, per_device(): call(rim_kernel, (shape(PLANES, ROWS, LANES), shape(16, LANES)), [SMEM] *...  7.53 us
    pallas_call x1, Pallas kernels, per_device(): call(inner_kernel, (shape(16 * ROWS, LANES), shape(48, LANES), shape(LEVE...  7.03 us
    unnamed x18, local copies, waits for them, and re-layouts  2.07 us
    ppermute x1, starting transfers between devices, per_device(): far = lax.ppermute(far, AXES, swap_pairs(False))  1.98 us
  transfers between devices with their start and end apart: 2, of which 1 were waited for; matrix products, arithmetic and copies ran while one was open for 0% of the time, Pallas kernels for 10%

profile of v2, /device:TPU:1, one launch (start us, length us, event | category | flops | bytes accessed | tf_op | source)
XLA Modules:
  0.0 68.3 jit_solution(7318137969600327387)
XLA Ops:
  0.6 0.0 copy-start.4
  0.6 0.0 copy-start
  0.7 0.0 copy-start.1
  0.7 0.0 copy-start.2
  0.7 1.3 %shard_map.113 = (f32[496,128]{1,0:T(8,128)S(1)}, f32[496,128]{1,0:T(8,128)S(1)}) custom-call(f32[20,32,128]{2,1,0:T(8,128)} %bitcast.12, f32[20,32,128]{2,1,0:T(8,128)} %bitcast.15, f32[32,128]{1,0:T(8,128)} %t_ref.5), custom_call_target="tpu_custom_call" | custom-call | flops 1000 | bytes 1000 | tf_op jit(solution)/shard_map/pallas_call | solution.py:332
  2.0 0.0 copy-start.3
  2.0 8.8 %collective-permute-start = (f32[496,128]{1,0:T(8,128)S(1)}, f32[496,128]{1,0:T(8,128)S(1)}, u32[]{:S(2)}, u32[]{:S(2)}) collective-permute-start(f32[496,128]{1,0:T(8,128)S(1)} %get-tuple-element.10), channel_id=1, source_target_pairs={{0,1},{1,0},{2,3},{3,2},{4,5},{5,4},{6,7},{7,6},{8,9},{9,8},{10,11... | collective-permute-start | bytes 761864 | tf_op jit(solution)/shard_map/ppermute | solution.py:338
  10.8 2.0 %collective-permute-start.1 = (f32[496,128]{1,0:T(8,128)S(1)}, f32[496,128]{1,0:T(8,128)S(1)}, u32[]{:S(2)}, u32[]{:S(2)}) collective-permute-start(f32[496,128]{1,0:T(8,128)S(1)} %get-tuple-element.11), channel_id=1, source_target_pairs={{1,2},{2,1},{3,4},{4,3},{5,6},{6,5},{7,8},{8,7},{9,10},{10,9},{11,... | collective-permute-start | bytes 761864 | tf_op jit(solution)/shard_map/ppermute | solution.py:339
  13.4 0.0 copy-start.5
  13.4 0.0 copy-start.8
  13.5 0.0 copy-done.4
  13.5 0.0 copy-done
  13.5 0.6 copy-done.5
  14.1 0.0 copy-done.8
  14.1 0.8 %copy-done.6 = f32[16,512]{1,0:T(8,128)S(1)} copy-done((f32[16,512]{1,0:T(8,128)S(1)}, f32[16,512]{1,0:T(8,128)}, u32[]{:S(2)}) %copy-start.6) | copy-done | bytes 32792
  14.9 0.7 copy-done.7
  15.5 7.0 %shard_map.114 = (f32[512,128]{1,0:T(8,128)S(1)}, f32[48,128]{1,0:T(8,128)S(1)}, f32[11,20,8,128]{3,2,1,0:T(8,128)S(1)}, f32[20,8,128]{2,1,0:T(8,128)S(1)}) custom-call(s32[1,512]{1,0:T(1,128)S(1)} %bitcast.22, f32[16,512]{1,0:T(8,128)S(1)} %copy-done.6, s32[1]{0:T(128)S(6)} %copy.14.count_ref, s32[16]{0:T(128)S(1)} %copy-done.8, f32[5,5]{1,0:T(8,128)S(1)} %copy-done.3, ...), custom_call_target="tpu_custom_call" | custom-call | flops 400000000 | bytes 1000000 | tf_op jit(solution)/shard_map/pallas_call | solution.py:342
  22.6 0.0 collective-permute-done.near_ref
  22.6 1.0 %collective-permute-done.1.far_ref = f32[496,128]{1,0:T(8,128)S(1)} collective-permute-done((f32[496,128]{1,0:T(8,128)S(1)}, f32[496,128]{1,0:T(8,128)S(1)}, u32[]{:S(2)}, u32[]{:S(2)}) %collective-permute-start.1) | collective-permute-done | bytes 253984 | tf_op jit(solution)/shard_map/ppermute | solution.py:339
  23.6 7.5 %shard_map.115 = (f32[20,32,128]{2,1,0:T(8,128)}, f32[16,128]{1,0:T(8,128)S(1)}) custom-call(f32[5,5]{1,0:T(8,128)S(1)} %copy-done.3, f32[5,5]{1,0:T(8,128)S(1)} %copy-done.4, f32[2]{0:T(128)S(1)} %copy-done.5, f32[20,32,128]{2,1,0:T(8,128)S(1)} %bitcast.14, f32[20,32,128]{2,1,0:T(8,128)S(1)} %bitcast.17, f32[32,128]{1,0:T(8,128)S(1)} %copy-done.2, ...), custom_call_target="tpu_custom_call" | custom-call | flops 100000000 | bytes 2000000 | tf_op jit(solution)/shard_map/pallas_call | solution.py:350
  31.1 15.4 %all_to_all.22 = f32[16,1,128]{2,1,0:T(1,128)S(1)} all-to-all(f32[16,1,128]{2,1,0:T(1,128)S(1)} %bitcast.21), channel_id=1, replica_groups=mesh['x'=4,'yl'=4,'z'=8,'yh'=2,'core'=2] {'yl','yh','core'}, dimensions={0} | all-to-all | bytes 16384 | tf_op jit(solution)/shard_map/all_to_all | solution.py:357
  46.5 0.1 shard_map.116
  46.7 20.9 %all_to_all.23 = f32[32,1,128]{2,1,0:T(1,128)S(1)} all-to-all(f32[32,1,128]{2,1,0:T(1,128)S(1)} %bitcast.19), channel_id=1, replica_groups=mesh['x'=4,'yl'=4,'z'=8,'yh'=2,'core'=2] {'x','z'}, dimensions={0} | all-to-all | bytes 32768 | tf_op jit(solution)/shard_map/all_to_all | solution.py:359
  67.6 0.8 %shard_map.117 = f32[1,2,2,72]{3,2,1,0:T(2,128)} custom-call(f32[32,128]{1,0:T(8,128)S(1)} %bitcast.18, f32[48,128]{1,0:T(8,128)S(1)} %get-tuple-element.13.table_ref), custom_call_target="tpu_custom_call" | custom-call | flops 1000 | bytes 1000 | tf_op jit(solution)/shard_map/pallas_call | solution.py:360
  (5 shorter events, 0.0 us)
Async XLA Ops:
  0.6 12.8 %copy-start.4 = (f32[5,5]{1,0:T(8,128)S(1)}, f32[5,5]{1,0:T(8,128)}, u32[]{:S(2)}) copy-start(f32[5,5]{1,0:T(8,128)} %jc_ref.3) | copy-start | bytes 304
  0.6 12.8 %copy-start = (f32[1,2,2,5,32,128]{5,4,3,2,1,0:T(8,128)S(1)}, f32[1,2,2,5,32,128]{5,4,3,2,1,0:T(8,128)}, u32[]{:S(2)}) copy-start(f32[1,2,2,5,32,128]{5,4,3,2,1,0:T(8,128)} %param.10) | copy-start | bytes 983044
  0.7 12.8 %copy-start.1 = (f32[2,2,5,32,128]{4,3,2,1,0:T(8,128)S(1)}, f32[2,2,5,32,128]{4,3,2,1,0:T(8,128)}, u32[]{:S(2)}) copy-start(f32[2,2,5,32,128]{4,3,2,1,0:T(8,128)} %param.11) | copy-start | bytes 983044
  0.7 12.8 %copy-start.2 = (f32[32,128]{1,0:T(8,128)S(1)}, f32[32,128]{1,0:T(8,128)}, u32[]{:S(2)}) copy-start(f32[32,128]{1,0:T(8,128)} %t_ref.5) | copy-start | bytes 49156
  2.0 11.5 %copy-start.3 = (f32[5,5]{1,0:T(8,128)S(1)}, f32[5,5]{1,0:T(8,128)}, u32[]{:S(2)}) copy-start(f32[5,5]{1,0:T(8,128)} %ja_ref.3) | copy-start | bytes 304
  2.0 20.6 %collective-permute-start = (f32[496,128]{1,0:T(8,128)S(1)}, f32[496,128]{1,0:T(8,128)S(1)}, u32[]{:S(2)}, u32[]{:S(2)}) collective-permute-start(f32[496,128]{1,0:T(8,128)S(1)} %get-tuple-element.10), channel_id=1, source_target_pairs={{0,1},{1,0},{2,3},{3,2},{4,5},{5,4},{6,7},{7,6},{8,9},{9,8},{10,11... | collective-permute-start | bytes 761864 | tf_op jit(solution)/shard_map/ppermute | solution.py:338
  10.8 12.8 %collective-permute-start.1 = (f32[496,128]{1,0:T(8,128)S(1)}, f32[496,128]{1,0:T(8,128)S(1)}, u32[]{:S(2)}, u32[]{:S(2)}) collective-permute-start(f32[496,128]{1,0:T(8,128)S(1)} %get-tuple-element.11), channel_id=1, source_target_pairs={{1,2},{2,1},{3,4},{4,3},{5,6},{6,5},{7,8},{8,7},{9,10},{10,9},{11,... | collective-permute-start | bytes 761864 | tf_op jit(solution)/shard_map/ppermute | solution.py:339
  13.4 0.7 copy-start.5
  13.4 0.7 copy-start.8
  14.1 0.8 %copy-start.6 = (f32[16,512]{1,0:T(8,128)S(1)}, f32[16,512]{1,0:T(8,128)}, u32[]{:S(2)}) copy-start(f32[16,512]{1,0:T(8,128)} %weight_ref.1) | copy-start | bytes 98308
  14.9 0.7 copy-start.7

commit v3 on v2

--- a/solution.py
+++ b/solution.py
@@ -47,29 +47,29 @@
     return pairs
 
 
-def pack_kernel(q_ref, s_ref, t_ref, near_ref, far_ref, q_buf, s_buf, t_buf, sems):
+def fill_message(out, rows, q_buf, s_buf, t_buf):
+    for i in range(PLANES):
+        out[i * HALO : (i + 1) * HALO, :] = q_buf[i, rows, :]
+        out[(PLANES + i) * HALO : (PLANES + i + 1) * HALO, :] = s_buf[i, rows, :]
+    at = 2 * PLANES * HALO
+    out[at : at + HALO, :] = t_buf[rows, :]
+    out[at + HALO :, :] = jnp.zeros((MSG - at - HALO, LANES), jnp.float32)
+
+
+def far_kernel(q_ref, s_ref, t_ref, out_ref, q_buf, s_buf, t_buf, sems):
     core = lax.axis_index("core")
-    wide = q_buf.shape[2]
-    copies = []
-    for side in range(2):
-        start = (core if side == 0 else 1 - core) * (ROWS - wide)
-        rows = pl.ds(pl.multiple_of(start, TILE), wide)
-        copies.append(pltpu.make_async_copy(q_ref.at[:, rows, :], q_buf.at[side], sems.at[side, 0]))
-        copies.append(pltpu.make_async_copy(s_ref.at[:, rows, :], s_buf.at[side], sems.at[side, 1]))
-        copies.append(pltpu.make_async_copy(t_ref.at[rows, :], t_buf.at[side], sems.at[side, 2]))
+    wide = q_buf.shape[1]
+    rows = pl.ds(pl.multiple_of(core * (ROWS - wide), TILE), wide)
+    copies = [
+        pltpu.make_async_copy(q_ref.at[:, rows, :], q_buf, sems.at[0]),
+        pltpu.make_async_copy(s_ref.at[:, rows, :], s_buf, sems.at[1]),
+        pltpu.make_async_copy(t_ref.at[rows, :], t_buf, sems.at[2]),
+    ]
     for copy in copies:
         copy.start()
-    for side, out in ((0, far_ref), (1, near_ref)):
-        for copy in copies[side * 3 : side * 3 + 3]:
-            copy.wait()
-        shift = (core if side == 0 else 1 - core) * (wide - HALO)
-        rows = pl.ds(shift, HALO)
-        for i in range(PLANES):
-            out[i * HALO : (i + 1) * HALO, :] = q_buf[side, i, rows, :]
-            out[(PLANES + i) * HALO : (PLANES + i + 1) * HALO, :] = s_buf[side, i, rows, :]
-        at = 2 * PLANES * HALO
-        out[at : at + HALO, :] = t_buf[side, rows, :]
-        out[at + HALO :, :] = jnp.zeros((MSG - at - HALO, LANES), jnp.float32)
+    for copy in copies:
+        copy.wait()
+    fill_message(out_ref, pl.ds(core * (wide - HALO), HALO), q_buf, s_buf, t_buf)
 
 
 def coefficients(ja_ref, jc_ref, coef):
@@ -163,9 +163,16 @@
 
 def inner_kernel(
     cell_ref, weight_ref, count_ref, ids_ref, ja_ref, jc_ref, omega_ref, q_ref, s_ref, t_ref,
-    moments_ref, table_ref, rim_ref, core_ref, base, first, second, forced, step, coef,
+    near_ref, moments_ref, table_ref, rim_ref, core_ref,
+    base, first, second, forced, step, coef, cell, weight, sems,
 ):
-    make_moments(cell_ref, weight_ref, count_ref, moments_ref)
+    copies = [
+        pltpu.make_async_copy(cell_ref, cell, sems.at[0]),
+        pltpu.make_async_copy(weight_ref, weight, sems.at[1]),
+    ]
+    for copy in copies:
+        copy.start()
+    fill_message(near_ref, pl.ds((1 - lax.axis_index("core")) * (ROWS - HALO), HALO), q_ref, s_ref, t_ref)
     make_tables(ids_ref, table_ref)
     coefficients(ja_ref, jc_ref, coef)
     phase = phases(table_ref)
@@ -174,6 +181,9 @@
         base[i, own, :] = q_ref[i]
         forced[i, own, :] = s_ref[i] * 5.0
     step[own, :] = t_ref[...]
+    for copy in copies:
+        copy.wait()
+    make_moments(cell, weight, count_ref, moments_ref)
 
     bufs = (base, first, second, first, base)
     for t in range(1, LEVELS + 1):
@@ -323,29 +333,44 @@
     )
 
 
+def in_hbm(value):
+    return pltpu.with_memory_space_constraint(value, pltpu.HBM)
+
+
 def per_device(
     perturbation, source, time_step, jac_axial, jac_circ, omega, diam_ids, surf_cell, surf_weight, face_count
 ):
     q = perturbation.reshape(PLANES, ROWS, LANES)
     src = source.reshape(PLANES, ROWS, LANES)
-    edges = pltpu.VMEM((2, PLANES, 16, LANES), jnp.float32)
-    near, far = call(
-        pack_kernel,
-        (shape(MSG, LANES),) * 2,
+    edge = pltpu.VMEM((PLANES, 16, LANES), jnp.float32)
+    far = call(
+        far_kernel,
+        shape(MSG, LANES),
         [ANY] * 3,
-        [edges, edges, pltpu.VMEM((2, 16, LANES), jnp.float32), pltpu.SemaphoreType.DMA((2, 3))],
-    )(*(pltpu.with_memory_space_constraint(a, pltpu.HBM) for a in (q, src, time_step)))
-    near = lax.ppermute(near, AXES, swap_pairs(True))
+        [edge, edge, pltpu.VMEM((16, LANES), jnp.float32), pltpu.SemaphoreType.DMA((3,))],
+    )(*map(in_hbm, (q, src, time_step)))
     far = lax.ppermute(far, AXES, swap_pairs(False))
     coef = pltpu.VMEM((50, TILE, LANES), jnp.float32)
     big = pltpu.VMEM((PLANES, ROWS + 16, LANES), jnp.float32)
-    moments, table, rim, core = call(
+    faces = surf_cell.shape[0]
+    near, moments, table, rim, core = call(
         inner_kernel,
-        (shape(16 * ROWS, LANES), shape(48, LANES), shape(LEVELS - 1, PLANES, TILE, LANES), shape(PLANES, TILE, LANES)),
-        [VMEM, VMEM] + [SMEM] * 5 + [VMEM] * 3,
-        [big, big, big, big, pltpu.VMEM((ROWS + 16, LANES), jnp.float32), coef],
+        (
+            shape(MSG, LANES),
+            shape(16 * ROWS, LANES),
+            shape(48, LANES),
+            shape(LEVELS - 1, PLANES, TILE, LANES),
+            shape(PLANES, TILE, LANES),
+        ),
+        [ANY, ANY] + [SMEM] * 5 + [VMEM] * 3,
+        [big, big, big, big, pltpu.VMEM((ROWS + 16, LANES), jnp.float32), coef]
+        + [pltpu.VMEM((1, faces), jnp.int32), pltpu.VMEM((16, faces), jnp.float32), pltpu.SemaphoreType.DMA((2,))],
         cost=(400_000_000, 1_000_000),
-    )(surf_cell.reshape(1, -1), surf_weight, face_count, diam_ids, jac_axial, jac_circ, omega, q, src, time_step)
+    )(
+        in_hbm(surf_cell.reshape(1, -1)), in_hbm(surf_weight), face_count, diam_ids,
+        jac_axial, jac_circ, omega, q, src, time_step,
+    )
+    near = lax.ppermute(near, AXES, swap_pairs(True))
     big = pltpu.VMEM((PLANES, 2 * PART, LANES), jnp.float32)
     result, force = call(
         rim_kernel,

time: 68.7 us -> 66.5 us (0.968)
  blocking collectives: 36.3 us -> 34.6 us
  local copies, waits for them, and re-layouts: 2.07 us -> 0.63 us
    ppermute x1, starting transfers between devices: 8.79 us -> 1.92 us  [per_device(): near = lax.ppermute(near, AXES, swap_pairs(True))]
    ppermute x1, starting transfers between devices: 1.98 us -> 8.84 us  [per_device(): far = lax.ppermute(far, AXES, swap_pairs(False))]
    all_to_all x1, blocking collectives: 15.4 us -> 13 us  [per_device(): got = lax.all_to_all(force, ('yl', 'yh', 'core'), 0, 0, tiled=True)]
    ppermute x1, waiting for transfers between devices: 0.01 us -> 1.48 us  [per_device(): near = lax.ppermute(near, AXES, swap_pairs(True))]
    unnamed x18 -> x14, local copies, waits for them, and re-layouts: 2.07 us -> 0.63 us
    ppermute x1, waiting for transfers between devices: 1.01 us -> 0.01 us  [per_device(): far = lax.ppermute(far, AXES, swap_pairs(False))]
    all_to_all x1, blocking collectives: 20.9 us -> 21.6 us  [per_device(): got = lax.all_to_all(middle, ('x', 'z'), 0, 0, tiled=True)]
  transfers between devices with their start and end apart: 2 -> 2, of which waited for: 1 -> 1; matrix products, arithmetic and copies ran while one was open for 0% -> 0% of each run, Pallas kernels for 10% -> 12%
where the time goes in v3:
time: 66.5 us; the launch traced here: 66.2 us
  blocking collectives  34.6 us (52%)
  Pallas kernels  17.3 us (26%)
  starting transfers between devices  10.8 us (16%)
  waiting for transfers between devices  1.48 us (2%)
  between operations  1.42 us (2%)
    all_to_all x1, blocking collectives, per_device(): got = lax.all_to_all(middle, ('x', 'z'), 0, 0, tiled=True)  21.6 us
    all_to_all x1, blocking collectives, per_device(): got = lax.all_to_all(force, ('yl', 'yh', 'core'), 0, 0, tiled=True)  13 us
    ppermute x1, starting transfers between devices, per_device(): far = lax.ppermute(far, AXES, swap_pairs(False))  8.84 us
    pallas_call x1, Pallas kernels, per_device(): call(inner_kernel, (shape(MSG, LANES), shape(16 * ROWS, LANES), shape(48,...  7.76 us
    pallas_call x1, Pallas kernels, per_device(): call(rim_kernel, (shape(PLANES, ROWS, LANES), shape(16, LANES)), [SMEM] *...  7.54 us
    ppermute x1, starting transfers between devices, per_device(): near = lax.ppermute(near, AXES, swap_pairs(True))  1.92 us
    ppermute x1, waiting for transfers between devices, per_device(): near = lax.ppermute(near, AXES, swap_pairs(True))  1.48 us
  transfers between devices with their start and end apart: 2, of which 1 were waited for; matrix products, arithmetic and copies ran while one was open for 0% of the time, Pallas kernels for 12%

profile of v3, /device:TPU:1, one launch (start us, length us, event | category | flops | bytes accessed | tf_op | source)
XLA Modules:
  0.0 66.2 jit_solution(17221406800274984928)
XLA Ops:
  0.6 0.0 copy-start
  0.6 0.0 copy-start.1
  0.7 0.0 copy-start.2
  0.7 0.0 copy-start.3
  0.7 0.0 copy-start.4
  0.7 1.1 %shard_map.114 = f32[496,128]{1,0:T(8,128)S(1)} custom-call(f32[20,32,128]{2,1,0:T(8,128)} %bitcast.12, f32[20,32,128]{2,1,0:T(8,128)} %bitcast.15, f32[32,128]{1,0:T(8,128)} %t_ref.5), custom_call_target="tpu_custom_call" | custom-call | flops 1000 | bytes 1000 | tf_op jit(solution)/shard_map/pallas_call | solution.py:346
  1.8 8.8 %collective-permute-start.1 = (f32[496,128]{1,0:T(8,128)S(1)}, f32[496,128]{1,0:T(8,128)S(1)}, u32[]{:S(2)}, u32[]{:S(2)}) collective-permute-start(f32[496,128]{1,0:T(8,128)S(1)} %shard_map.114), channel_id=1, source_target_pairs={{1,2},{2,1},{3,4},{4,3},{5,6},{6,5},{7,8},{8,7},{9,10},{10,9},{11,... | collective-permute-start | bytes 761864 | tf_op jit(solution)/shard_map/ppermute | solution.py:352
  11.3 0.0 copy-start.5
  11.3 0.0 copy-start.6
  11.3 0.0 copy-done
  11.3 0.0 copy-done.1
  11.3 0.0 copy-done.2
  11.3 0.0 copy-done.3
  11.4 0.6 copy-done.5
  12.0 0.0 copy-done.6
  12.0 7.8 %shard_map.113 = (f32[496,128]{1,0:T(8,128)S(1)}, f32[512,128]{1,0:T(8,128)S(1)}, f32[48,128]{1,0:T(8,128)S(1)}, f32[11,20,8,128]{3,2,1,0:T(8,128)S(1)}, f32[20,8,128]{2,1,0:T(8,128)S(1)}) custom-call(s32[1,512]{1,0:T(1,128)} %bitcast.23, f32[16,512]{1,0:T(8,128)} %weight_ref.1, s32[1]{0:T(128)S(6)} %copy.14.count_ref, s32[16]{0:T(128)S(1)} %copy-done.6, ...), custom_call_target="tpu_custom_call" | custom-call | flops 400000000 | bytes 1000000 | tf_op jit(solution)/shard_map/pallas_call | solution.py:356
  19.7 1.9 %collective-permute-start = (f32[496,128]{1,0:T(8,128)S(1)}, f32[496,128]{1,0:T(8,128)S(1)}, u32[]{:S(2)}, u32[]{:S(2)}) collective-permute-start(f32[496,128]{1,0:T(8,128)S(1)} %get-tuple-element.9), channel_id=1, source_target_pairs={{0,1},{1,0},{2,3},{3,2},{4,5},{5,4},{6,7},{7,6},{8,9},{9,8},{10,11... | collective-permute-start | bytes 761864 | tf_op jit(solution)/shard_map/ppermute | solution.py:373
  21.7 0.0 collective-permute-done.1.far_ref
  21.7 1.5 %collective-permute-done.near_ref = f32[496,128]{1,0:T(8,128)S(1)} collective-permute-done((f32[496,128]{1,0:T(8,128)S(1)}, f32[496,128]{1,0:T(8,128)S(1)}, u32[]{:S(2)}, u32[]{:S(2)}) %collective-permute-start) | collective-permute-done | bytes 253984 | tf_op jit(solution)/shard_map/ppermute | solution.py:373
  23.2 7.5 %shard_map.115 = (f32[20,32,128]{2,1,0:T(8,128)}, f32[16,128]{1,0:T(8,128)S(1)}) custom-call(f32[5,5]{1,0:T(8,128)S(1)} %copy-done.3, f32[5,5]{1,0:T(8,128)S(1)} %copy-done.4, f32[2]{0:T(128)S(1)} %copy-done.5, f32[20,32,128]{2,1,0:T(8,128)S(1)} %bitcast.14, f32[20,32,128]{2,1,0:T(8,128)S(1)} %bitcast.17, f32[32,128]{1,0:T(8,128)S(1)} %copy-done.2, ...), custom_call_target="tpu_custom_call" | custom-call | flops 100000000 | bytes 2000000 | tf_op jit(solution)/shard_map/pallas_call | solution.py:375
  30.7 13.0 %all_to_all.22 = f32[16,1,128]{2,1,0:T(1,128)S(1)} all-to-all(f32[16,1,128]{2,1,0:T(1,128)S(1)} %bitcast.21), channel_id=1, replica_groups=mesh['x'=4,'yl'=4,'z'=8,'yh'=2,'core'=2] {'yl','yh','core'}, dimensions={0} | all-to-all | bytes 16384 | tf_op jit(solution)/shard_map/all_to_all | solution.py:382
  43.7 0.1 shard_map.116
  43.8 21.6 %all_to_all.23 = f32[32,1,128]{2,1,0:T(1,128)S(1)} all-to-all(f32[32,1,128]{2,1,0:T(1,128)S(1)} %bitcast.19), channel_id=1, replica_groups=mesh['x'=4,'yl'=4,'z'=8,'yh'=2,'core'=2] {'x','z'}, dimensions={0} | all-to-all | bytes 32768 | tf_op jit(solution)/shard_map/all_to_all | solution.py:384
  65.4 0.8 %shard_map.117 = f32[1,2,2,72]{3,2,1,0:T(2,128)} custom-call(f32[32,128]{1,0:T(8,128)S(1)} %bitcast.18, f32[48,128]{1,0:T(8,128)S(1)} %get-tuple-element.11.table_ref), custom_call_target="tpu_custom_call" | custom-call | flops 1000 | bytes 1000 | tf_op jit(solution)/shard_map/pallas_call | solution.py:385
  (1 shorter events, 0.0 us)
Async XLA Ops:
  0.6 10.7 %copy-start = (f32[1,2,2,5,32,128]{5,4,3,2,1,0:T(8,128)S(1)}, f32[1,2,2,5,32,128]{5,4,3,2,1,0:T(8,128)}, u32[]{:S(2)}) copy-start(f32[1,2,2,5,32,128]{5,4,3,2,1,0:T(8,128)} %param.10) | copy-start | bytes 983044
  0.6 10.7 %copy-start.1 = (f32[2,2,5,32,128]{4,3,2,1,0:T(8,128)S(1)}, f32[2,2,5,32,128]{4,3,2,1,0:T(8,128)}, u32[]{:S(2)}) copy-start(f32[2,2,5,32,128]{4,3,2,1,0:T(8,128)} %param.11) | copy-start | bytes 983044
  0.7 10.7 %copy-start.2 = (f32[32,128]{1,0:T(8,128)S(1)}, f32[32,128]{1,0:T(8,128)}, u32[]{:S(2)}) copy-start(f32[32,128]{1,0:T(8,128)} %t_ref.5) | copy-start | bytes 49156
  0.7 10.7 %copy-start.3 = (f32[5,5]{1,0:T(8,128)S(1)}, f32[5,5]{1,0:T(8,128)}, u32[]{:S(2)}) copy-start(f32[5,5]{1,0:T(8,128)} %ja_ref.3) | copy-start | bytes 304
  0.7 10.7 %copy-start.4 = (f32[5,5]{1,0:T(8,128)S(1)}, f32[5,5]{1,0:T(8,128)}, u32[]{:S(2)}) copy-start(f32[5,5]{1,0:T(8,128)} %jc_ref.3) | copy-start | bytes 304
  1.8 19.9 %collective-permute-start.1 = (f32[496,128]{1,0:T(8,128)S(1)}, f32[496,128]{1,0:T(8,128)S(1)}, u32[]{:S(2)}, u32[]{:S(2)}) collective-permute-start(f32[496,128]{1,0:T(8,128)S(1)} %shard_map.114), channel_id=1, source_target_pairs={{1,2},{2,1},{3,4},{4,3},{5,6},{6,5},{7,8},{8,7},{9,10},{10,9},{11,... | collective-permute-start | bytes 761864 | tf_op jit(solution)/shard_map/ppermute | solution.py:352
  11.3 0.7 copy-start.5
  11.3 0.7 %copy-start.6 = (s32[16]{0:T(128)S(1)}, s32[16]{0:T(128)}, u32[]{:S(2)}) copy-start(s32[16]{0:T(128)} %ids_ref.1) | copy-start | bytes 196
  19.7 3.4 %collective-permute-start = (f32[496,128]{1,0:T(8,128)S(1)}, f32[496,128]{1,0:T(8,128)S(1)}, u32[]{:S(2)}, u32[]{:S(2)}) collective-permute-start(f32[496,128]{1,0:T(8,128)S(1)} %get-tuple-element.9), channel_id=1, source_target_pairs={{0,1},{1,0},{2,3},{3,2},{4,5},{5,4},{6,7},{7,6},{8,9},{9,8},{10,11... | collective-permute-start | bytes 761864 | tf_op jit(solution)/shard_map/ppermute | solution.py:373

commit v4 on v3

--- a/solution.py
+++ b/solution.py
@@ -134,13 +134,18 @@
     live = lax.broadcasted_iota(jnp.int32, (1, faces), 1) < count_ref[0]
     weight = jnp.where(live, weight_ref[...], 0.0)
     in_row = lax.broadcasted_iota(jnp.int32, (ROWS, faces), 0) == row
-    in_col = (lax.broadcasted_iota(jnp.int32, (LANES, faces), 0) == col).astype(jnp.float32)
-    spread = jnp.concatenate(
-        [jnp.where(in_row, weight[m : m + 1, :], 0.0) for m in range(modes)], axis=0
-    )
-    moments_ref[...] = lax.dot_general(
-        spread, in_col, (((1,), (1,)), ((), ())), precision=HIGH, preferred_element_type=jnp.float32
-    )
+    in_col = (lax.broadcasted_iota(jnp.int32, (LANES, faces), 0) == col).astype(jnp.bfloat16)
+    total = None
+    for _ in range(3):
+        part = weight.astype(jnp.bfloat16)
+        weight = weight - part.astype(jnp.float32)
+        wide = part.astype(jnp.float32)
+        spread = jnp.concatenate(
+            [jnp.where(in_row, wide[m : m + 1, :], 0.0) for m in range(modes)], axis=0
+        ).astype(jnp.bfloat16)
+        term = lax.dot_general(spread, in_col, (((1,), (1,)), ((), ())), preferred_element_type=jnp.float32)
+        total = term if total is None else total + term
+    moments_ref[...] = total
 
 
 def make_tables(ids_ref, table_ref):
@@ -161,19 +166,25 @@
     table_ref[2 * n + 8 : 2 * n + 16, :] = jnp.sin(sigma)
 
 
-def inner_kernel(
-    cell_ref, weight_ref, count_ref, ids_ref, ja_ref, jc_ref, omega_ref, q_ref, s_ref, t_ref,
-    near_ref, moments_ref, table_ref, rim_ref, core_ref,
-    base, first, second, forced, step, coef, cell, weight, sems,
-):
+def prep_kernel(cell_ref, weight_ref, ids_ref, count_ref, q_ref, s_ref, t_ref, near_ref, moments_ref, table_ref, cell, weight, ids, sems):
     copies = [
         pltpu.make_async_copy(cell_ref, cell, sems.at[0]),
         pltpu.make_async_copy(weight_ref, weight, sems.at[1]),
+        pltpu.make_async_copy(ids_ref, ids, sems.at[2]),
     ]
     for copy in copies:
         copy.start()
     fill_message(near_ref, pl.ds((1 - lax.axis_index("core")) * (ROWS - HALO), HALO), q_ref, s_ref, t_ref)
-    make_tables(ids_ref, table_ref)
+    for copy in copies:
+        copy.wait()
+    make_tables(ids, table_ref)
+    make_moments(cell, weight, count_ref, moments_ref)
+
+
+def inner_kernel(
+    ja_ref, jc_ref, omega_ref, q_ref, s_ref, t_ref, table_ref, rim_ref, core_ref,
+    base, first, second, forced, step, coef,
+):
     coefficients(ja_ref, jc_ref, coef)
     phase = phases(table_ref)
     own = pl.ds(OWN, ROWS)
@@ -181,9 +192,6 @@
         base[i, own, :] = q_ref[i]
         forced[i, own, :] = s_ref[i] * 5.0
     step[own, :] = t_ref[...]
-    for copy in copies:
-        copy.wait()
-    make_moments(cell, weight, count_ref, moments_ref)
 
     bufs = (base, first, second, first, base)
     for t in range(1, LEVELS + 1):
@@ -192,12 +200,8 @@
         valid = ROWS - 2 * t
         tiles = (valid + TILE - 1) // TILE
 
-        def body(j, carry, cur=cur, new=new, alpha=ALPHAS[k], t=t, valid=valid, tiles=tiles):
-            row = OWN + t + j * TILE
-            tile_update(cur, base, new, forced, step, coef, omega_ref, phase, alpha, row)
-            return carry
-
-        lax.fori_loop(0, tiles, body, 0)
+        for j in range(tiles):
+            tile_update(cur, base, new, forced, step, coef, omega_ref, phase, ALPHAS[k], OWN + t + j * TILE)
         if t < LEVELS:
             for i in range(PLANES):
                 rim_ref[t - 1, i, 0:4, :] = new[i, OWN + t : OWN + t + 4, :]
@@ -209,7 +213,7 @@
 
 def rim_kernel(
     ja_ref, jc_ref, omega_ref, q_ref, s_ref, t_ref, near_ref, far_ref, moments_ref, table_ref, rim_ref, core_ref,
-    out_ref, force_ref, base, other, first, second, forced, step, coef,
+    out_ref, force_ref, base, other, first, second, forced, step, coef, result, sem,
 ):
     even = lax.axis_index("core") == 0
     coefficients(ja_ref, jc_ref, coef)
@@ -247,9 +251,11 @@
                     new[i, 16 + t : 20 + t, :] = rim_ref[t - 1, i, 0:4, :]
                     new[i, PART + 12 - t : PART + 16 - t, :] = rim_ref[t - 1, i, 4:8, :]
     for i in range(PLANES):
-        out_ref[i, 0:HALO, :] = end[i, 16 : 16 + HALO, :]
-        out_ref[i, HALO : ROWS - HALO, :] = core_ref[i]
-        out_ref[i, ROWS - HALO : ROWS, :] = end[i, PART + 4 : PART + 16, :]
+        result[i, 0:HALO, :] = end[i, 16 : 16 + HALO, :]
+        result[i, HALO : ROWS - HALO, :] = core_ref[i]
+        result[i, ROWS - HALO : ROWS, :] = end[i, PART + 4 : PART + 16, :]
+    copy = pltpu.make_async_copy(result, out_ref, sem)
+    copy.start()
 
     sums = []
     modes = moments_ref.shape[0] // ROWS
@@ -257,7 +263,7 @@
         for ec in range(4):
             acc = None
             for r in range(0, ROWS, TILE):
-                term = moments_ref[m * ROWS + r : m * ROWS + r + TILE, :] * out_ref[ec * 5 + 4, r : r + TILE, :]
+                term = moments_ref[m * ROWS + r : m * ROWS + r + TILE, :] * result[ec * 5 + 4, r : r + TILE, :]
                 acc = term if acc is None else acc + term
             sums.append(acc)
     stacked = jnp.concatenate(sums, axis=0)
@@ -269,6 +275,7 @@
     force_ref[...] = lax.dot_general(
         ones, by_lane, (((1,), (1,)), ((), ())), precision=HIGH, preferred_element_type=jnp.float32
     )
+    copy.wait()
 
 
 def middle_kernel(in_ref, out_ref):
@@ -321,12 +328,12 @@
 ANY = pl.BlockSpec(memory_space=pltpu.HBM)
 
 
-def call(kernel, out_shape, in_specs, scratch=(), cost=(1000, 1000)):
+def call(kernel, out_shape, in_specs, scratch=(), cost=(1000, 1000), out_specs=None):
     return pl.pallas_call(
         kernel,
         out_shape=out_shape,
         in_specs=in_specs,
-        out_specs=jax.tree.map(lambda _: VMEM, out_shape),
+        out_specs=out_specs or jax.tree.map(lambda _: VMEM, out_shape),
         scratch_shapes=list(scratch),
         compiler_params=pltpu.CompilerParams(vmem_limit_bytes=32 * 1024 * 1024),
         cost_estimate=pl.CostEstimate(flops=cost[0], bytes_accessed=cost[1], transcendentals=0),
@@ -353,31 +360,32 @@
     coef = pltpu.VMEM((50, TILE, LANES), jnp.float32)
     big = pltpu.VMEM((PLANES, ROWS + 16, LANES), jnp.float32)
     faces = surf_cell.shape[0]
-    near, moments, table, rim, core = call(
+    near, moments, table = call(
+        prep_kernel,
+        (shape(MSG, LANES), shape(16 * ROWS, LANES), shape(48, LANES)),
+        [ANY] * 3 + [SMEM] + [VMEM] * 3,
+        [pltpu.VMEM((1, faces), jnp.int32), pltpu.VMEM((16, faces), jnp.float32)]
+        + [pltpu.SMEM(diam_ids.shape, jnp.int32), pltpu.SemaphoreType.DMA((3,))],
+        cost=(400_000_000, 1_000_000),
+    )(*map(in_hbm, (surf_cell.reshape(1, -1), surf_weight, diam_ids)), face_count, q, src, time_step)
+    near = lax.ppermute(near, AXES, swap_pairs(True))
+    rim, core = call(
         inner_kernel,
-        (
-            shape(MSG, LANES),
-            shape(16 * ROWS, LANES),
-            shape(48, LANES),
-            shape(LEVELS - 1, PLANES, TILE, LANES),
-            shape(PLANES, TILE, LANES),
-        ),
-        [ANY, ANY] + [SMEM] * 5 + [VMEM] * 3,
-        [big, big, big, big, pltpu.VMEM((ROWS + 16, LANES), jnp.float32), coef]
-        + [pltpu.VMEM((1, faces), jnp.int32), pltpu.VMEM((16, faces), jnp.float32), pltpu.SemaphoreType.DMA((2,))],
+        (shape(LEVELS - 1, PLANES, TILE, LANES), shape(PLANES, TILE, LANES)),
+        [SMEM] * 3 + [VMEM] * 4,
+        [big, big, big, big, pltpu.VMEM((ROWS + 16, LANES), jnp.float32), coef],
         cost=(400_000_000, 1_000_000),
-    )(
-        in_hbm(surf_cell.reshape(1, -1)), in_hbm(surf_weight), face_count, diam_ids,
-        jac_axial, jac_circ, omega, q, src, time_step,
-    )
-    near = lax.ppermute(near, AXES, swap_pairs(True))
+    )(jac_axial, jac_circ, omega, q, src, time_step, table)
     big = pltpu.VMEM((PLANES, 2 * PART, LANES), jnp.float32)
     result, force = call(
         rim_kernel,
         (shape(PLANES, ROWS, LANES), shape(16, LANES)),
         [SMEM] * 3 + [VMEM] * 9,
-        [big] * 5 + [pltpu.VMEM((2 * PART, LANES), jnp.float32), coef],
+        [big] * 5
+        + [pltpu.VMEM((2 * PART, LANES), jnp.float32), coef, pltpu.VMEM((PLANES, ROWS, LANES), jnp.float32)]
+        + [pltpu.SemaphoreType.DMA],
         cost=(100_000_000, 2_000_000),
+        out_specs=(ANY, VMEM),
     )(jac_axial, jac_circ, omega, q, src, time_step, near, far, moments, table, rim, core)
     got = lax.all_to_all(force, ("yl", "yh", "core"), 0, 0, tiled=True)
     middle = call(middle_kernel, shape(32, LANES), [VMEM])(got)

time: 66.5 us -> 66.5 us (level)
  blocking collectives: 34.6 us -> 38.6 us
  Pallas kernels: 17.3 us -> 15.3 us
  waiting for transfers between devices: 1.48 us -> 0.01 us
    all_to_all x1, blocking collectives: 13 us -> 17 us  [per_device(): got = lax.all_to_all(force, ('yl', 'yh', 'core'), 0, 0, tiled=True)]
    pallas_call x1 -> x2, Pallas kernels: 7.76 us -> 5.77 us  [the longest x1 4.34 us: per_device(): call(inner_kernel, (shape(LEVELS - 1, PLANES, TILE, LANES), shape(PLANES,...]
    ppermute x1, waiting for transfers between devices: 1.48 us -> 0.01 us  [per_device(): near = lax.ppermute(near, AXES, swap_pairs(True))]
  transfers between devices with their start and end apart: 2 -> 2, of which waited for: 1 -> 0; matrix products, arithmetic and copies ran while one was open for 0% -> 0% of each run, Pallas kernels for 12% -> 9%
where the time goes in v4:
time: 66.5 us; the launch traced here: 66.2 us
  blocking collectives  38.6 us (58%)
  Pallas kernels  15.3 us (23%)
  starting transfers between devices  10.8 us (16%)
  between operations  1.44 us (2%)
    all_to_all x1, blocking collectives, per_device(): got = lax.all_to_all(middle, ('x', 'z'), 0, 0, tiled=True)  21.6 us
    all_to_all x1, blocking collectives, per_device(): got = lax.all_to_all(force, ('yl', 'yh', 'core'), 0, 0, tiled=True)  17 us
    ppermute x1, starting transfers between devices, per_device(): far = lax.ppermute(far, AXES, swap_pairs(False))  8.84 us
    pallas_call x1, Pallas kernels, per_device(): call(rim_kernel, (shape(PLANES, ROWS, LANES), shape(16, LANES)), [SMEM] *...  7.55 us
    pallas_call x1, Pallas kernels, per_device(): call(inner_kernel, (shape(LEVELS - 1, PLANES, TILE, LANES), shape(PLANES,...  4.34 us
    ppermute x1, starting transfers between devices, per_device(): near = lax.ppermute(near, AXES, swap_pairs(True))  1.92 us
    pallas_call x1, Pallas kernels, per_device(): call(prep_kernel, (shape(MSG, LANES), shape(16 * ROWS, LANES), shape(48,...  1.43 us
  transfers between devices with their start and end apart: 2, of which 0 were waited for; matrix products, arithmetic and copies ran while one was open for 0% of the time, Pallas kernels for 9%

profile of v4, /device:TPU:1, one launch (start us, length us, event | category | flops | bytes accessed | tf_op | source)
XLA Modules:
  0.0 66.2 jit_solution(1104925991961459458)
XLA Ops:
  0.6 0.0 copy-start
  0.6 0.0 copy-start.1
  0.6 0.0 copy-start.2
  0.7 1.1 %shard_map.114 = f32[496,128]{1,0:T(8,128)S(1)} custom-call(f32[20,32,128]{2,1,0:T(8,128)} %bitcast.12, f32[20,32,128]{2,1,0:T(8,128)} %bitcast.16, f32[32,128]{1,0:T(8,128)} %t_ref.7), custom_call_target="tpu_custom_call" | custom-call | flops 1000 | bytes 1000 | tf_op jit(solution)/shard_map/pallas_call | solution.py:353
  1.8 8.8 %collective-permute-start.1 = (f32[496,128]{1,0:T(8,128)S(1)}, f32[496,128]{1,0:T(8,128)S(1)}, u32[]{:S(2)}, u32[]{:S(2)}) collective-permute-start(f32[496,128]{1,0:T(8,128)S(1)} %shard_map.114), channel_id=1, source_target_pairs={{1,2},{2,1},{3,4},{4,3},{5,6},{6,5},{7,8},{8,7},{9,10},{10,9},{11,... | collective-permute-start | bytes 761864 | tf_op jit(solution)/shard_map/ppermute | solution.py:359
  11.3 0.0 copy-done
  11.3 0.0 copy-done.1
  11.3 0.0 copy-done.2
  11.3 0.0 copy-start.3
  11.3 0.0 copy-start.4
  11.3 1.4 %shard_map.113 = (f32[496,128]{1,0:T(8,128)S(1)}, f32[512,128]{1,0:T(8,128)S(1)}, f32[48,128]{1,0:T(8,128)S(1)}) custom-call(s32[1,512]{1,0:T(1,128)} %bitcast.25, f32[16,512]{1,0:T(8,128)} %weight_ref.1, s32[16]{0:T(128)} %ids_ref.1, s32[1]{0:T(128)S(6)} %copy.14.count_ref, f32[20,32,128]{2,1,0:T(8,128)S(1)} %bitcast.13, f32[20,32,128]{2,1,0:T(8,128)S(1)} %bitcast.17, ...), custom_call_target="tpu_custom_call" | custom-call | flops 400000000 | bytes 1000000 | tf_op jit(solution)/shard_map/pallas_call | solution.py:363
  12.8 0.0 copy-start.5
  12.8 1.9 %collective-permute-start = (f32[496,128]{1,0:T(8,128)S(1)}, f32[496,128]{1,0:T(8,128)S(1)}, u32[]{:S(2)}, u32[]{:S(2)}) collective-permute-start(f32[496,128]{1,0:T(8,128)S(1)} %get-tuple-element.9), channel_id=1, source_target_pairs={{0,1},{1,0},{2,3},{3,2},{4,5},{5,4},{6,7},{7,6},{8,9},{9,8},{10,11... | collective-permute-start | bytes 761864 | tf_op jit(solution)/shard_map/ppermute | solution.py:371
  14.7 0.0 copy-done.3
  14.7 0.0 copy-done.4
  14.7 0.0 copy-done.5
  14.7 4.3 %shard_map.115 = (f32[11,20,8,128]{3,2,1,0:T(8,128)S(1)}, f32[20,8,128]{2,1,0:T(8,128)S(1)}) custom-call(f32[5,5]{1,0:T(8,128)S(1)} %copy-done.3, f32[5,5]{1,0:T(8,128)S(1)} %copy-done.4, f32[2]{0:T(128)S(1)} %copy-done.5, f32[20,32,128]{2,1,0:T(8,128)S(1)} %bitcast.14, f32[20,32,128]{2,1,0:T(8,128)S(1)} %bitcast.18, f32[32,128]{1,0:T(8,128)S(1)} %copy-done.2, ...), custom_call_target="tpu_custom_call" | custom-call | flops 400000000 | bytes 1000000 | tf_op jit(solution)/shard_map/pallas_call | solution.py:372
  19.1 0.0 collective-permute-done.1.far_ref
  19.1 0.0 collective-permute-done.near_ref
  19.1 7.5 %shard_map.116 = (f32[20,32,128]{2,1,0:T(8,128)}, f32[16,128]{1,0:T(8,128)S(1)}) custom-call(f32[5,5]{1,0:T(8,128)S(1)} %copy-done.3, f32[5,5]{1,0:T(8,128)S(1)} %copy-done.4, f32[2]{0:T(128)S(1)} %copy-done.5, f32[20,32,128]{2,1,0:T(8,128)S(1)} %bitcast.15, f32[20,32,128]{2,1,0:T(8,128)S(1)} %bitcast.19, f32[32,128]{1,0:T(8,128)S(1)} %copy-done.2, ...), custom_call_target="tpu_custom_call" | custom-call | flops 100000000 | bytes 2000000 | tf_op jit(solution)/shard_map/pallas_call | solution.py:380
  26.7 17.0 %all_to_all.22 = f32[16,1,128]{2,1,0:T(1,128)S(1)} all-to-all(f32[16,1,128]{2,1,0:T(1,128)S(1)} %bitcast.23), channel_id=1, replica_groups=mesh['x'=4,'yl'=4,'z'=8,'yh'=2,'core'=2] {'yl','yh','core'}, dimensions={0} | all-to-all | bytes 16384 | tf_op jit(solution)/shard_map/all_to_all | solution.py:390
  43.7 0.1 shard_map.117
  43.8 21.6 %all_to_all.23 = f32[32,1,128]{2,1,0:T(1,128)S(1)} all-to-all(f32[32,1,128]{2,1,0:T(1,128)S(1)} %bitcast.21), channel_id=1, replica_groups=mesh['x'=4,'yl'=4,'z'=8,'yh'=2,'core'=2] {'x','z'}, dimensions={0} | all-to-all | bytes 32768 | tf_op jit(solution)/shard_map/all_to_all | solution.py:392
  65.4 0.8 %shard_map.118 = f32[1,2,2,72]{3,2,1,0:T(2,128)} custom-call(f32[32,128]{1,0:T(8,128)S(1)} %bitcast.20, f32[48,128]{1,0:T(8,128)S(1)} %get-tuple-element.11.table_ref), custom_call_target="tpu_custom_call" | custom-call | flops 1000 | bytes 1000 | tf_op jit(solution)/shard_map/pallas_call | solution.py:393
Async XLA Ops:
  0.6 10.6 %copy-start = (f32[1,2,2,5,32,128]{5,4,3,2,1,0:T(8,128)S(1)}, f32[1,2,2,5,32,128]{5,4,3,2,1,0:T(8,128)}, u32[]{:S(2)}) copy-start(f32[1,2,2,5,32,128]{5,4,3,2,1,0:T(8,128)} %param.10) | copy-start | bytes 983044
  0.6 10.6 %copy-start.1 = (f32[2,2,5,32,128]{4,3,2,1,0:T(8,128)S(1)}, f32[2,2,5,32,128]{4,3,2,1,0:T(8,128)}, u32[]{:S(2)}) copy-start(f32[2,2,5,32,128]{4,3,2,1,0:T(8,128)} %param.11) | copy-start | bytes 983044
  0.6 10.6 %copy-start.2 = (f32[32,128]{1,0:T(8,128)S(1)}, f32[32,128]{1,0:T(8,128)}, u32[]{:S(2)}) copy-start(f32[32,128]{1,0:T(8,128)} %t_ref.7) | copy-start | bytes 49156
  1.8 17.3 %collective-permute-start.1 = (f32[496,128]{1,0:T(8,128)S(1)}, f32[496,128]{1,0:T(8,128)S(1)}, u32[]{:S(2)}, u32[]{:S(2)}) collective-permute-start(f32[496,128]{1,0:T(8,128)S(1)} %shard_map.114), channel_id=1, source_target_pairs={{1,2},{2,1},{3,4},{4,3},{5,6},{6,5},{7,8},{8,7},{9,10},{10,9},{11,... | collective-permute-start | bytes 761864 | tf_op jit(solution)/shard_map/ppermute | solution.py:359
  11.3 3.4 %copy-start.3 = (f32[5,5]{1,0:T(8,128)S(1)}, f32[5,5]{1,0:T(8,128)}, u32[]{:S(2)}) copy-start(f32[5,5]{1,0:T(8,128)} %ja_ref.3) | copy-start | bytes 304
  11.3 3.4 %copy-start.4 = (f32[5,5]{1,0:T(8,128)S(1)}, f32[5,5]{1,0:T(8,128)}, u32[]{:S(2)}) copy-start(f32[5,5]{1,0:T(8,128)} %jc_ref.3) | copy-start | bytes 304
  12.8 2.0 %copy-start.5 = (f32[2]{0:T(128)S(1)}, f32[2]{0:T(128)}, u32[]{:S(2)}) copy-start(f32[2]{0:T(128)} %omega_ref.3) | copy-start | bytes 28
  12.8 6.3 %collective-permute-start = (f32[496,128]{1,0:T(8,128)S(1)}, f32[496,128]{1,0:T(8,128)S(1)}, u32[]{:S(2)}, u32[]{:S(2)}) collective-permute-start(f32[496,128]{1,0:T(8,128)S(1)} %get-tuple-element.9), channel_id=1, source_target_pairs={{0,1},{1,0},{2,3},{3,2},{4,5},{5,4},{6,7},{7,6},{8,9},{9,8},{10,11... | collective-permute-start | bytes 761864 | tf_op jit(solution)/shard_map/ppermute | solution.py:371

commit v5 on v4

--- a/solution.py
+++ b/solution.py
@@ -19,7 +19,10 @@
 PLANES = 20
 ROWS = 32
 LANES = 128
-MSG = 2 * PLANES * HALO + 16
+SOURCE_AT = PLANES * HALO
+STEP_AT = SOURCE_AT + PLANES * (HALO - 1)
+MSG = STEP_AT + HALO
+FAR_MSG = MSG + 8
 LEVELS = HALO
 OWN = 8
 PART = 32
@@ -47,13 +50,16 @@
     return pairs
 
 
-def fill_message(out, rows, q_buf, s_buf, t_buf):
+def fill_message(out, first, last_end, q_buf, s_buf, t_buf):
+    rows = pl.ds(first, HALO)
+    fewer = pl.ds(first + last_end, HALO - 1)
     for i in range(PLANES):
         out[i * HALO : (i + 1) * HALO, :] = q_buf[i, rows, :]
-        out[(PLANES + i) * HALO : (PLANES + i + 1) * HALO, :] = s_buf[i, rows, :]
-    at = 2 * PLANES * HALO
-    out[at : at + HALO, :] = t_buf[rows, :]
-    out[at + HALO :, :] = jnp.zeros((MSG - at - HALO, LANES), jnp.float32)
+        at = SOURCE_AT + i * (HALO - 1)
+        out[at : at + HALO - 1, :] = s_buf[i, fewer, :]
+    out[STEP_AT : STEP_AT + HALO - 1, :] = t_buf[fewer, :]
+    at = MSG - 1
+    out[at:, :] = jnp.zeros((out.shape[0] - at, LANES), jnp.float32)
 
 
 def far_kernel(q_ref, s_ref, t_ref, out_ref, q_buf, s_buf, t_buf, sems):
@@ -69,7 +75,7 @@
         copy.start()
     for copy in copies:
         copy.wait()
-    fill_message(out_ref, pl.ds(core * (wide - HALO), HALO), q_buf, s_buf, t_buf)
+    fill_message(out_ref, core * (wide - HALO), core, q_buf, s_buf, t_buf)
 
 
 def coefficients(ja_ref, jc_ref, coef):
@@ -166,7 +172,10 @@
     table_ref[2 * n + 8 : 2 * n + 16, :] = jnp.sin(sigma)
 
 
-def prep_kernel(cell_ref, weight_ref, ids_ref, count_ref, q_ref, s_ref, t_ref, near_ref, moments_ref, table_ref, cell, weight, ids, sems):
+def prep_kernel(
+    cell_ref, weight_ref, ids_ref, _, count_ref, q_ref, s_ref, t_ref, near_ref,
+    moments_ref, table_ref, cell, weight, ids, sems,
+):
     copies = [
         pltpu.make_async_copy(cell_ref, cell, sems.at[0]),
         pltpu.make_async_copy(weight_ref, weight, sems.at[1]),
@@ -174,7 +183,8 @@
     ]
     for copy in copies:
         copy.start()
-    fill_message(near_ref, pl.ds((1 - lax.axis_index("core")) * (ROWS - HALO), HALO), q_ref, s_ref, t_ref)
+    last_end = 1 - lax.axis_index("core")
+    fill_message(near_ref, last_end * (ROWS - HALO), last_end, q_ref, s_ref, t_ref)
     for copy in copies:
         copy.wait()
     make_tables(ids, table_ref)
@@ -211,32 +221,23 @@
                 core_ref[i] = new[i, OWN + t : OWN + ROWS - t, :]
 
 
-def rim_kernel(
-    ja_ref, jc_ref, omega_ref, q_ref, s_ref, t_ref, near_ref, far_ref, moments_ref, table_ref, rim_ref, core_ref,
-    out_ref, force_ref, base, other, first, second, forced, step, coef, result, sem,
-):
-    even = lax.axis_index("core") == 0
+def rim_sections(last_end, halo_ref, q_ref, s_ref, t_ref, rim_ref, table_ref, ja_ref, jc_ref, omega_ref, scratch):
+    base, other, first, second, forced, step, coef = scratch
     coefficients(ja_ref, jc_ref, coef)
     phase = phases(table_ref)
-    edge = jnp.zeros((4, LANES), jnp.float32)
-
-    def put(buf, at, top, low, scale):
-        near = near_ref[pl.ds(at, HALO), :]
-        far = far_ref[pl.ds(at, HALO), :]
-        buf[0:4, :] = edge
-        buf[4:16, :] = jnp.where(even, far, near) * scale
-        buf[16:PART, :] = top * scale
-        buf[PART : PART + 16, :] = low * scale
-        buf[PART + 16 : PART + 28, :] = jnp.where(even, near, far) * scale
-        buf[PART + 28 : PART + 32, :] = edge
-
-    for i in range(PLANES):
-        put(base.at[i], i * HALO, q_ref[i, 0:16, :], q_ref[i, 16:32, :], 1.0)
-        put(forced.at[i], (PLANES + i) * HALO, s_ref[i, 0:16, :], s_ref[i, 16:32, :], 5.0)
-        for buf in (other, first, second):
-            buf[i, 0:8, :] = jnp.zeros((8, LANES), jnp.float32)
-            buf[i, PART + 24 : PART + 32, :] = jnp.zeros((8, LANES), jnp.float32)
-    put(step, 2 * PLANES * HALO, t_ref[0:16, :], t_ref[16:32, :], 1.0)
+    half = PART // 2
+    taken = pl.ds(pl.multiple_of(last_end * half, half), half)
+    own = pl.ds(pl.multiple_of((1 - last_end) * half, half), half)
+    halo = pl.ds(jnp.where(last_end == 1, half, half - HALO), HALO)
+    fewer = pl.ds(jnp.where(last_end == 1, half, half - HALO + 1), HALO - 1)
+    for i in range(PLANES):
+        base[i, own, :] = q_ref[i, taken, :]
+        base[i, halo, :] = halo_ref[i * HALO : (i + 1) * HALO, :]
+        at = SOURCE_AT + i * (HALO - 1)
+        forced[i, own, :] = s_ref[i, taken, :] * 5.0
+        forced[i, fewer, :] = halo_ref[at : at + HALO - 1, :] * 5.0
+    step[own, :] = t_ref[taken, :]
+    step[fewer, :] = halo_ref[STEP_AT : STEP_AT + HALO - 1, :]
 
     for it in range(ITERS):
         start, end = (base, other) if it % 2 == 0 else (other, base)
@@ -244,26 +245,63 @@
         for k in range(SECTIONS):
             t = it * SECTIONS + k + 1
             cur, new = bufs[k], bufs[k + 1]
-            for row in (4 + t, 8 + t, PART + 16 - t, PART + 20 - t):
-                tile_update(cur, start, new, forced, step, coef, omega_ref, phase, ALPHAS[k], row)
+            row = jnp.where(last_end == 1, half - t, half - HALO + t)
+            for shift in (0, HALO - TILE):
+                tile_update(cur, start, new, forced, step, coef, omega_ref, phase, ALPHAS[k], row + shift)
             if t < LEVELS:
+                kept = pl.ds(last_end * 4, 4)
+                place = pl.ds(jnp.where(last_end == 1, half - 4 - t, half + t), 4)
                 for i in range(PLANES):
-                    new[i, 16 + t : 20 + t, :] = rim_ref[t - 1, i, 0:4, :]
-                    new[i, PART + 12 - t : PART + 16 - t, :] = rim_ref[t - 1, i, 4:8, :]
-    for i in range(PLANES):
-        result[i, 0:HALO, :] = end[i, 16 : 16 + HALO, :]
+                    new[i, place, :] = rim_ref[t - 1, i, kept, :]
+    return end, jnp.where(last_end == 1, half - HALO, half)
+
+
+def near_rim_kernel(
+    ja_ref, jc_ref, omega_ref, q_ref, s_ref, t_ref, halo_ref, table_ref, rim_ref, core_ref,
+    half_ref, out_ref, result, sem, *scratch,
+):
+    last_end = 1 - lax.axis_index("core")
+    end, at = rim_sections(last_end, halo_ref, q_ref, s_ref, t_ref, rim_ref, table_ref, ja_ref, jc_ref, omega_ref, scratch)
+    for i in range(PLANES):
+        result[i, pl.ds(last_end * (ROWS - HALO), HALO), :] = end[i, pl.ds(at, HALO), :]
         result[i, HALO : ROWS - HALO, :] = core_ref[i]
-        result[i, ROWS - HALO : ROWS, :] = end[i, PART + 4 : PART + 16, :]
-    copy = pltpu.make_async_copy(result, out_ref, sem)
+    half = ROWS // 2
+    mine = pl.ds(pl.multiple_of(last_end * half, half), half)
+    copy = pltpu.make_async_copy(result.at[:, mine, :], out_ref.at[:, mine, :], sem)
     copy.start()
-
+    for i in range(PLANES):
+        half_ref[i] = result[i, mine, :]
+    copy.wait()
+
+
+def far_rim_kernel(
+    ja_ref, jc_ref, omega_ref, q_ref, s_ref, t_ref, halo_ref, moments_ref, table_ref, rim_ref, core_ref, half_ref, _,
+    out_ref, force_ref, result, sem, *scratch,
+):
+    last_end = lax.axis_index("core")
+    end, at = rim_sections(last_end, halo_ref, q_ref, s_ref, t_ref, rim_ref, table_ref, ja_ref, jc_ref, omega_ref, scratch)
+    half = ROWS // 2
+    mine = pl.ds(pl.multiple_of(last_end * half, half), half)
+    for i in range(PLANES):
+        result[i, HALO : ROWS - HALO, :] = core_ref[i]
+        result[i, pl.ds(last_end * (ROWS - HALO), HALO), :] = end[i, pl.ds(at, HALO), :]
+    copy = pltpu.make_async_copy(result.at[:, mine, :], out_ref.at[:, mine, :], sem)
+    copy.start()
+
+    pressure = []
+    for ec in range(4):
+        i = ec * 5 + 4
+        far = [result[i, pl.ds(last_end * half + r, TILE), :] for r in (0, TILE)]
+        near = [half_ref[i, r : r + TILE, :] for r in (0, TILE)]
+        pressure.append([jnp.where(last_end == 1, n, f) for f, n in zip(far, near)]
+                        + [jnp.where(last_end == 1, f, n) for f, n in zip(far, near)])
     sums = []
     modes = moments_ref.shape[0] // ROWS
     for m in range(modes):
         for ec in range(4):
             acc = None
             for r in range(0, ROWS, TILE):
-                term = moments_ref[m * ROWS + r : m * ROWS + r + TILE, :] * result[ec * 5 + 4, r : r + TILE, :]
+                term = moments_ref[m * ROWS + r : m * ROWS + r + TILE, :] * pressure[ec][r // TILE]
                 acc = term if acc is None else acc + term
             sums.append(acc)
     stacked = jnp.concatenate(sums, axis=0)
@@ -328,13 +366,14 @@
 ANY = pl.BlockSpec(memory_space=pltpu.HBM)
 
 
-def call(kernel, out_shape, in_specs, scratch=(), cost=(1000, 1000), out_specs=None):
+def call(kernel, out_shape, in_specs, scratch=(), cost=(1000, 1000), out_specs=None, aliases=()):
     return pl.pallas_call(
         kernel,
         out_shape=out_shape,
         in_specs=in_specs,
         out_specs=out_specs or jax.tree.map(lambda _: VMEM, out_shape),
         scratch_shapes=list(scratch),
+        input_output_aliases=dict(aliases),
         compiler_params=pltpu.CompilerParams(vmem_limit_bytes=32 * 1024 * 1024),
         cost_estimate=pl.CostEstimate(flops=cost[0], bytes_accessed=cost[1], transcendentals=0),
     )
@@ -352,41 +391,46 @@
     edge = pltpu.VMEM((PLANES, 16, LANES), jnp.float32)
     far = call(
         far_kernel,
-        shape(MSG, LANES),
+        shape(FAR_MSG, LANES),
         [ANY] * 3,
         [edge, edge, pltpu.VMEM((16, LANES), jnp.float32), pltpu.SemaphoreType.DMA((3,))],
     )(*map(in_hbm, (q, src, time_step)))
-    far = lax.ppermute(far, AXES, swap_pairs(False))
     coef = pltpu.VMEM((50, TILE, LANES), jnp.float32)
     big = pltpu.VMEM((PLANES, ROWS + 16, LANES), jnp.float32)
     faces = surf_cell.shape[0]
     near, moments, table = call(
         prep_kernel,
         (shape(MSG, LANES), shape(16 * ROWS, LANES), shape(48, LANES)),
-        [ANY] * 3 + [SMEM] + [VMEM] * 3,
+        [ANY] * 4 + [SMEM] + [VMEM] * 3,
         [pltpu.VMEM((1, faces), jnp.int32), pltpu.VMEM((16, faces), jnp.float32)]
         + [pltpu.SMEM(diam_ids.shape, jnp.int32), pltpu.SemaphoreType.DMA((3,))],
-        cost=(400_000_000, 1_000_000),
-    )(*map(in_hbm, (surf_cell.reshape(1, -1), surf_weight, diam_ids)), face_count, q, src, time_step)
+    )(*map(in_hbm, (surf_cell.reshape(1, -1), surf_weight, diam_ids)), far, face_count, q, src, time_step)
+    far = lax.ppermute(far, AXES, swap_pairs(False))
     near = lax.ppermute(near, AXES, swap_pairs(True))
     rim, core = call(
         inner_kernel,
         (shape(LEVELS - 1, PLANES, TILE, LANES), shape(PLANES, TILE, LANES)),
         [SMEM] * 3 + [VMEM] * 4,
         [big, big, big, big, pltpu.VMEM((ROWS + 16, LANES), jnp.float32), coef],
-        cost=(400_000_000, 1_000_000),
     )(jac_axial, jac_circ, omega, q, src, time_step, table)
-    big = pltpu.VMEM((PLANES, 2 * PART, LANES), jnp.float32)
+    big = pltpu.VMEM((PLANES, PART, LANES), jnp.float32)
+    scratch = [pltpu.VMEM((PLANES, ROWS, LANES), jnp.float32), pltpu.SemaphoreType.DMA]
+    scratch += [big] * 5 + [pltpu.VMEM((PART, LANES), jnp.float32), coef]
+    half, result = call(
+        near_rim_kernel,
+        (shape(PLANES, ROWS // 2, LANES), shape(PLANES, ROWS, LANES)),
+        [SMEM] * 3 + [VMEM] * 7,
+        scratch,
+        out_specs=(VMEM, ANY),
+    )(jac_axial, jac_circ, omega, q, src, time_step, near, table, rim, core)
     result, force = call(
-        rim_kernel,
+        far_rim_kernel,
         (shape(PLANES, ROWS, LANES), shape(16, LANES)),
-        [SMEM] * 3 + [VMEM] * 9,
-        [big] * 5
-        + [pltpu.VMEM((2 * PART, LANES), jnp.float32), coef, pltpu.VMEM((PLANES, ROWS, LANES), jnp.float32)]
-        + [pltpu.SemaphoreType.DMA],
-        cost=(100_000_000, 2_000_000),
+        [SMEM] * 3 + [VMEM] * 9 + [ANY],
+        scratch,
         out_specs=(ANY, VMEM),
-    )(jac_axial, jac_circ, omega, q, src, time_step, near, far, moments, table, rim, core)
+        aliases={12: 0},
+    )(jac_axial, jac_circ, omega, q, src, time_step, far, moments, table, rim, core, half, result)
     got = lax.all_to_all(force, ("yl", "yh", "core"), 0, 0, tiled=True)
     middle = call(middle_kernel, shape(32, LANES), [VMEM])(got)
     got = lax.all_to_all(middle, ("x", "z"), 0, 0, tiled=True)

time: 66.5 us -> 63.4 us (0.953)
  blocking collectives: 38.6 us -> 33.5 us
  Pallas kernels: 15.3 us -> 17.3 us
    all_to_all x1, blocking collectives: 17 us -> 10.8 us  [per_device(): got = lax.all_to_all(force, ('yl', 'yh', 'core'), 0, 0, tiled=True)]
    pallas_call x2 -> x3, Pallas kernels: 8.66 us -> 10.7 us  [the longest x1 4.79 us: per_device(): call(far_rim_kernel, (shape(PLANES, ROWS, LANES), shape(16, LANES)), [SME...]
    all_to_all x1, blocking collectives: 21.6 us -> 22.7 us  [per_device(): got = lax.all_to_all(middle, ('x', 'z'), 0, 0, tiled=True)]
  transfers between devices with their start and end apart: 2 -> 2, of which waited for: 0 -> 0; matrix products, arithmetic and copies ran while one was open for 0% -> 0% of each run, Pallas kernels for 9% -> 17%
where the time goes in v5:
time: 63.4 us; the launch traced here: 63.1 us
  blocking collectives  33.5 us (53%)
  Pallas kernels  17.3 us (27%)
  starting transfers between devices  10.8 us (17%)
  between operations  1.44 us (2%)
    all_to_all x1, blocking collectives, per_device(): got = lax.all_to_all(middle, ('x', 'z'), 0, 0, tiled=True)  22.7 us
    all_to_all x1, blocking collectives, per_device(): got = lax.all_to_all(force, ('yl', 'yh', 'core'), 0, 0, tiled=True)  10.8 us
    ppermute x1, starting transfers between devices, per_device(): far = lax.ppermute(far, AXES, swap_pairs(False))  8.83 us
    pallas_call x1, Pallas kernels, per_device(): call(far_rim_kernel, (shape(PLANES, ROWS, LANES), shape(16, LANES)), [SME...  4.79 us
    pallas_call x1, Pallas kernels, per_device(): call(near_rim_kernel, (shape(PLANES, ROWS // 2, LANES), shape(PLANES, ROW...  4.75 us
    pallas_call x1, Pallas kernels, per_device(): call(inner_kernel, (shape(LEVELS - 1, PLANES, TILE, LANES), shape(PLANES,...  4.34 us
    ppermute x1, starting transfers between devices, per_device(): near = lax.ppermute(near, AXES, swap_pairs(True))  1.92 us
    pallas_call x1, Pallas kernels, per_device(): call(prep_kernel, (shape(MSG, LANES), shape(16 * ROWS, LANES), shape(48,...  1.43 us
  transfers between devices with their start and end apart: 2, of which 0 were waited for; matrix products, arithmetic and copies ran while one was open for 0% of the time, Pallas kernels for 17%

profile of v5, /device:TPU:1, one launch (start us, length us, event | category | flops | bytes accessed | tf_op | source)
XLA Modules:
  0.0 63.1 jit_solution(2397349933659800499)
XLA Ops:
  0.6 0.0 copy-start
  0.6 0.0 copy-start.1
  0.6 0.0 copy-start.2
  0.7 1.1 %shard_map.113._ = f32[480,128]{1,0:T(8,128)S(1)} custom-call(f32[20,32,128]{2,1,0:T(8,128)} %bitcast.12, f32[20,32,128]{2,1,0:T(8,128)} %bitcast.17, f32[32,128]{1,0:T(8,128)} %t_ref.9), custom_call_target="tpu_custom_call" | custom-call | flops 1000 | bytes 1000 | tf_op jit(solution)/shard_map/pallas_call | solution.py:392
  1.8 8.8 %collective-permute-start = (f32[480,128]{1,0:T(8,128)S(1)}, f32[480,128]{1,0:T(8,128)S(1)}, u32[]{:S(2)}, u32[]{:S(2)}) collective-permute-start(f32[480,128]{1,0:T(8,128)S(1)} %shard_map.113._), channel_id=1, source_target_pairs={{1,2},{2,1},{3,4},{4,3},{5,6},{6,5},{7,8},{8,7},{9,10},{10,9},{11,... | collective-permute-start | bytes 737288 | tf_op jit(solution)/shard_map/ppermute | solution.py:408
  11.3 0.0 copy-done
  11.3 0.0 copy-done.1
  11.3 0.0 copy-done.2
  11.3 0.0 copy-start.3
  11.3 0.0 copy-start.4
  11.3 1.4 %shard_map.114 = (f32[472,128]{1,0:T(8,128)S(1)}, f32[512,128]{1,0:T(8,128)S(1)}, f32[48,128]{1,0:T(8,128)S(1)}) custom-call(s32[1,512]{1,0:T(1,128)} %bitcast.27, f32[16,512]{1,0:T(8,128)} %weight_ref.1, s32[16]{0:T(128)} %ids_ref.1, f32[480,128]{1,0:T(8,128)S(1)} %shard_map.113._, s32[1]{0:T(128)S(6)} %copy.16.count_ref, f32[20,32,128]{2,1,0:T(8,128)S(1)} %bitcast.13, ...), custom_call_target="tpu_custom_call" | custom-call | flops 1000 | bytes 1000 | tf_op jit(solution)/shard_map/pallas_call | solution.py:401
  12.8 0.0 copy-start.5
  12.8 1.9 %collective-permute-start.1 = (f32[472,128]{1,0:T(8,128)S(1)}, f32[472,128]{1,0:T(8,128)S(1)}, u32[]{:S(2)}, u32[]{:S(2)}) collective-permute-start(f32[472,128]{1,0:T(8,128)S(1)} %get-tuple-element.15), channel_id=1, source_target_pairs={{0,1},{1,0},{2,3},{3,2},{4,5},{5,4},{6,7},{7,6},{8,9},{9,8},{10,11... | collective-permute-start | bytes 725000 | tf_op jit(solution)/shard_map/ppermute | solution.py:409
  14.7 0.0 copy-done.3
  14.7 0.0 copy-done.4
  14.7 4.3 %shard_map.115 = (f32[11,20,8,128]{3,2,1,0:T(8,128)S(1)}, f32[20,8,128]{2,1,0:T(8,128)S(1)}) custom-call(f32[5,5]{1,0:T(8,128)S(1)} %copy-done.3, f32[5,5]{1,0:T(8,128)S(1)} %copy-done.4, f32[2]{0:T(128)S(1)} %copy-done.5, f32[20,32,128]{2,1,0:T(8,128)S(1)} %bitcast.14, f32[20,32,128]{2,1,0:T(8,128)S(1)} %bitcast.19, f32[32,128]{1,0:T(8,128)S(1)} %copy-done.2, ...), custom_call_target="tpu_custom_call" | custom-call | flops 1000 | bytes 1000 | tf_op jit(solution)/shard_map/pallas_call | solution.py:410
  19.1 0.0 collective-permute-done.1.halo_ref
  19.1 4.8 %shard_map.116 = (f32[20,16,128]{2,1,0:T(8,128)S(1)}, f32[20,32,128]{2,1,0:T(8,128)}) custom-call(f32[5,5]{1,0:T(8,128)S(1)} %copy-done.3, f32[5,5]{1,0:T(8,128)S(1)} %copy-done.4, f32[2]{0:T(128)S(1)} %copy-done.5, f32[20,32,128]{2,1,0:T(8,128)S(1)} %bitcast.15, f32[20,32,128]{2,1,0:T(8,128)S(1)} %bitcast.20, f32[32,128]{1,0:T(8,128)S(1)} %copy-done.2, ...), custom_call_target="tpu_custom_call" | custom-call | flops 1000 | bytes 1000 | tf_op jit(solution)/shard_map/pallas_call | solution.py:419
  23.9 0.0 collective-permute-done.halo_ref
  23.9 4.8 %shard_map.117 = (f32[20,32,128]{2,1,0:T(8,128)}, f32[16,128]{1,0:T(8,128)S(1)}) custom-call(f32[5,5]{1,0:T(8,128)S(1)} %copy-done.3, f32[5,5]{1,0:T(8,128)S(1)} %copy-done.4, f32[2]{0:T(128)S(1)} %copy-done.5, f32[20,32,128]{2,1,0:T(8,128)S(1)} %bitcast.16, f32[20,32,128]{2,1,0:T(8,128)S(1)} %bitcast.21, ...), custom_call_target="tpu_custom_call", output_to_operand_aliasing={{0}: (12, {})} | custom-call | flops 1000 | bytes 1000 | tf_op jit(solution)/shard_map/pallas_call | solution.py:426
  28.7 10.8 %all_to_all.22 = f32[16,1,128]{2,1,0:T(1,128)S(1)} all-to-all(f32[16,1,128]{2,1,0:T(1,128)S(1)} %bitcast.25), channel_id=1, replica_groups=mesh['x'=4,'yl'=4,'z'=8,'yh'=2,'core'=2] {'yl','yh','core'}, dimensions={0} | all-to-all | bytes 16384 | tf_op jit(solution)/shard_map/all_to_all | solution.py:434
  39.5 0.1 shard_map.118
  39.7 22.7 %all_to_all.23 = f32[32,1,128]{2,1,0:T(1,128)S(1)} all-to-all(f32[32,1,128]{2,1,0:T(1,128)S(1)} %bitcast.23), channel_id=1, replica_groups=mesh['x'=4,'yl'=4,'z'=8,'yh'=2,'core'=2] {'x','z'}, dimensions={0} | all-to-all | bytes 32768 | tf_op jit(solution)/shard_map/all_to_all | solution.py:436
  62.3 0.8 %shard_map.119 = f32[1,2,2,72]{3,2,1,0:T(2,128)} custom-call(f32[32,128]{1,0:T(8,128)S(1)} %bitcast.22, f32[48,128]{1,0:T(8,128)S(1)} %get-tuple-element.12.table_ref), custom_call_target="tpu_custom_call" | custom-call | flops 1000 | bytes 1000 | tf_op jit(solution)/shard_map/pallas_call | solution.py:437
  (1 shorter events, 0.0 us)
Async XLA Ops:
  0.6 10.6 %copy-start = (f32[1,2,2,5,32,128]{5,4,3,2,1,0:T(8,128)S(1)}, f32[1,2,2,5,32,128]{5,4,3,2,1,0:T(8,128)}, u32[]{:S(2)}) copy-start(f32[1,2,2,5,32,128]{5,4,3,2,1,0:T(8,128)} %param.10) | copy-start | bytes 983044
  0.6 10.6 %copy-start.1 = (f32[2,2,5,32,128]{4,3,2,1,0:T(8,128)S(1)}, f32[2,2,5,32,128]{4,3,2,1,0:T(8,128)}, u32[]{:S(2)}) copy-start(f32[2,2,5,32,128]{4,3,2,1,0:T(8,128)} %param.11) | copy-start | bytes 983044
  0.6 10.6 %copy-start.2 = (f32[32,128]{1,0:T(8,128)S(1)}, f32[32,128]{1,0:T(8,128)}, u32[]{:S(2)}) copy-start(f32[32,128]{1,0:T(8,128)} %t_ref.9) | copy-start | bytes 49156
  1.8 22.1 %collective-permute-start = (f32[480,128]{1,0:T(8,128)S(1)}, f32[480,128]{1,0:T(8,128)S(1)}, u32[]{:S(2)}, u32[]{:S(2)}) collective-permute-start(f32[480,128]{1,0:T(8,128)S(1)} %shard_map.113._), channel_id=1, source_target_pairs={{1,2},{2,1},{3,4},{4,3},{5,6},{6,5},{7,8},{8,7},{9,10},{10,9},{11,... | collective-permute-start | bytes 737288 | tf_op jit(solution)/shard_map/ppermute | solution.py:408
  11.3 3.4 %copy-start.3 = (f32[5,5]{1,0:T(8,128)S(1)}, f32[5,5]{1,0:T(8,128)}, u32[]{:S(2)}) copy-start(f32[5,5]{1,0:T(8,128)} %ja_ref.5) | copy-start | bytes 304
  11.3 3.4 %copy-start.4 = (f32[5,5]{1,0:T(8,128)S(1)}, f32[5,5]{1,0:T(8,128)}, u32[]{:S(2)}) copy-start(f32[5,5]{1,0:T(8,128)} %jc_ref.5) | copy-start | bytes 304
  12.8 2.0 %copy-start.5 = (f32[2]{0:T(128)S(1)}, f32[2]{0:T(128)}, u32[]{:S(2)}) copy-start(f32[2]{0:T(128)} %omega_ref.5) | copy-start | bytes 28
  12.8 6.3 %collective-permute-start.1 = (f32[472,128]{1,0:T(8,128)S(1)}, f32[472,128]{1,0:T(8,128)S(1)}, u32[]{:S(2)}, u32[]{:S(2)}) collective-permute-start(f32[472,128]{1,0:T(8,128)S(1)} %get-tuple-element.15), channel_id=1, source_target_pairs={{0,1},{1,0},{2,3},{3,2},{4,5},{5,4},{6,7},{7,6},{8,9},{9,8},{10,11... | collective-permute-start | bytes 725000 | tf_op jit(solution)/shard_map/ppermute | solution.py:409

commit v6 on v5

--- a/solution.py
+++ b/solution.py
@@ -78,11 +78,16 @@
     fill_message(out_ref, core * (wide - HALO), core, q_buf, s_buf, t_buf)
 
 
-def coefficients(ja_ref, jc_ref, coef):
+def make_coefficients(ja, jc, omega, coef_ref):
+    def put(at, value):
+        coef_ref[at] = jnp.broadcast_to(value, (TILE, LANES))
+
     for u in range(5):
         for v in range(5):
-            coef[u * 5 + v] = jnp.full((TILE, LANES), ja_ref[u, v] * 2.5, jnp.float32)
-            coef[25 + u * 5 + v] = jnp.full((TILE, LANES), jc_ref[u, v] * 2.5, jnp.float32)
+            put(u * 5 + v, ja[u : u + 1, v : v + 1] * 2.5)
+            put(25 + u * 5 + v, jc[u : u + 1, v : v + 1] * 2.5)
+    for e in range(2):
+        put(50 + e, omega[:, e : e + 1] * 5.0)
 
 
 def phases(table_ref):
@@ -95,7 +100,7 @@
     return is_first, is_last, turn_c, turn_s
 
 
-def tile_update(cur, base, new, forced, step, coef, omega_ref, phase, alpha, row):
+def tile_update(cur, base, new, forced, step, coef, phase, alpha, row):
     is_first, is_last, turn_c, turn_s = phase
     here = pl.ds(row, TILE)
     dt = step[here, :] * (alpha * 0.2)
@@ -116,7 +121,7 @@
                 axial.append(up - down)
                 circ.append(right - left)
                 total.append((up + down) + (right + left))
-        freq = omega_ref[e] * 5.0
+        freq = coef[50 + e]
         for c in range(2):
             for u in range(5):
                 i = e * 10 + c * 5 + u
@@ -173,29 +178,25 @@
 
 
 def prep_kernel(
-    cell_ref, weight_ref, ids_ref, _, count_ref, q_ref, s_ref, t_ref, near_ref,
-    moments_ref, table_ref, cell, weight, ids, sems,
+    cell_ref, weight_ref, ids_ref, ja_ref, jc_ref, omega_ref, _, count_ref, q_ref, s_ref, t_ref, near_ref,
+    moments_ref, table_ref, coef_ref, cell, weight, ids, ja, jc, omega, sems,
 ):
-    copies = [
-        pltpu.make_async_copy(cell_ref, cell, sems.at[0]),
-        pltpu.make_async_copy(weight_ref, weight, sems.at[1]),
-        pltpu.make_async_copy(ids_ref, ids, sems.at[2]),
-    ]
+    pairs = ((cell_ref, cell), (weight_ref, weight), (ids_ref, ids), (ja_ref, ja), (jc_ref, jc), (omega_ref, omega))
+    copies = [pltpu.make_async_copy(a, b, sems.at[i]) for i, (a, b) in enumerate(pairs)]
     for copy in copies:
         copy.start()
     last_end = 1 - lax.axis_index("core")
     fill_message(near_ref, last_end * (ROWS - HALO), last_end, q_ref, s_ref, t_ref)
     for copy in copies:
         copy.wait()
+    make_coefficients(ja, jc, omega, coef_ref)
     make_tables(ids, table_ref)
     make_moments(cell, weight, count_ref, moments_ref)
 
 
 def inner_kernel(
-    ja_ref, jc_ref, omega_ref, q_ref, s_ref, t_ref, table_ref, rim_ref, core_ref,
-    base, first, second, forced, step, coef,
+    coef, q_ref, s_ref, t_ref, table_ref, rim_ref, core_ref, base, first, second, forced, step,
 ):
-    coefficients(ja_ref, jc_ref, coef)
     phase = phases(table_ref)
     own = pl.ds(OWN, ROWS)
     for i in range(PLANES):
@@ -211,7 +212,7 @@
         tiles = (valid + TILE - 1) // TILE
 
         for j in range(tiles):
-            tile_update(cur, base, new, forced, step, coef, omega_ref, phase, ALPHAS[k], OWN + t + j * TILE)
+            tile_update(cur, base, new, forced, step, coef, phase, ALPHAS[k], OWN + t + j * TILE)
         if t < LEVELS:
             for i in range(PLANES):
                 rim_ref[t - 1, i, 0:4, :] = new[i, OWN + t : OWN + t + 4, :]
@@ -221,9 +222,8 @@
                 core_ref[i] = new[i, OWN + t : OWN + ROWS - t, :]
 
 
-def rim_sections(last_end, halo_ref, q_ref, s_ref, t_ref, rim_ref, table_ref, ja_ref, jc_ref, omega_ref, scratch):
-    base, other, first, second, forced, step, coef = scratch
-    coefficients(ja_ref, jc_ref, coef)
+def rim_sections(last_end, halo_ref, q_ref, s_ref, t_ref, rim_ref, table_ref, coef, scratch):
+    base, other, first, second, forced, step = scratch
     phase = phases(table_ref)
     half = PART // 2
     taken = pl.ds(pl.multiple_of(last_end * half, half), half)
@@ -247,7 +247,7 @@
             cur, new = bufs[k], bufs[k + 1]
             row = jnp.where(last_end == 1, half - t, half - HALO + t)
             for shift in (0, HALO - TILE):
-                tile_update(cur, start, new, forced, step, coef, omega_ref, phase, ALPHAS[k], row + shift)
+                tile_update(cur, start, new, forced, step, coef, phase, ALPHAS[k], row + shift)
             if t < LEVELS:
                 kept = pl.ds(last_end * 4, 4)
                 place = pl.ds(jnp.where(last_end == 1, half - 4 - t, half + t), 4)
@@ -256,63 +256,70 @@
     return end, jnp.where(last_end == 1, half - HALO, half)
 
 
-def near_rim_kernel(
-    ja_ref, jc_ref, omega_ref, q_ref, s_ref, t_ref, halo_ref, table_ref, rim_ref, core_ref,
-    half_ref, out_ref, result, sem, *scratch,
-):
+def reduce_to_lanes(items):
+    sublane = lax.broadcasted_iota(jnp.int32, (TILE, LANES), 0)
+    lane = lax.broadcasted_iota(jnp.int32, (TILE, LANES), 1)
+    for axis, index, shifts in ((0, sublane, (4, 2, 1)), (1, lane, (64, 32, 16))):
+        size = (TILE, LANES)[axis]
+        for shift in shifts:
+            low = jnp.bitwise_and(index, shift) == 0
+            n = len(items) // 2
+            items = [
+                jnp.where(low, a + pltpu.roll(a, size - shift, axis), b + pltpu.roll(b, shift, axis))
+                for a, b in zip(items[:n], items[n:])
+            ]
+    total = items[0]
+    for shift in (8, 4, 2, 1):
+        low = jnp.bitwise_and(lane, shift) == 0
+        total = total + jnp.where(low, pltpu.roll(total, LANES - shift, 1), pltpu.roll(total, shift, 1))
+    kept = jnp.where(jnp.bitwise_and(lane, 15) == sublane, total, 0.0)
+    return jnp.sum(kept, axis=0, keepdims=True)
+
+
+def near_rim_kernel(coef, q_ref, s_ref, t_ref, halo_ref, table_ref, rim_ref, core_ref, half_ref, *scratch):
     last_end = 1 - lax.axis_index("core")
-    end, at = rim_sections(last_end, halo_ref, q_ref, s_ref, t_ref, rim_ref, table_ref, ja_ref, jc_ref, omega_ref, scratch)
+    end, at = rim_sections(last_end, halo_ref, q_ref, s_ref, t_ref, rim_ref, table_ref, coef, scratch)
+    fill_half(last_end, end, at, core_ref, half_ref)
+
+
+def fill_half(last_end, end, at, core_ref, half_ref):
     for i in range(PLANES):
-        result[i, pl.ds(last_end * (ROWS - HALO), HALO), :] = end[i, pl.ds(at, HALO), :]
-        result[i, HALO : ROWS - HALO, :] = core_ref[i]
+        half_ref[i, pl.ds(last_end * 4, HALO), :] = end[i, pl.ds(at, HALO), :]
+        half_ref[i, pl.ds((1 - last_end) * HALO, 4), :] = core_ref[i, pl.ds(last_end * 4, 4), :]
+
+
+def half_of(ref, last_end):
     half = ROWS // 2
-    mine = pl.ds(pl.multiple_of(last_end * half, half), half)
-    copy = pltpu.make_async_copy(result.at[:, mine, :], out_ref.at[:, mine, :], sem)
-    copy.start()
-    for i in range(PLANES):
-        half_ref[i] = result[i, mine, :]
-    copy.wait()
+    return ref.at[:, pl.ds(pl.multiple_of(last_end * half, half), half), :]
 
 
 def far_rim_kernel(
-    ja_ref, jc_ref, omega_ref, q_ref, s_ref, t_ref, halo_ref, moments_ref, table_ref, rim_ref, core_ref, half_ref, _,
-    out_ref, force_ref, result, sem, *scratch,
+    coef, q_ref, s_ref, t_ref, halo_ref, moments_ref, table_ref, rim_ref, core_ref, near_ref,
+    out_ref, half_ref, force_ref, sem, *scratch,
 ):
     last_end = lax.axis_index("core")
-    end, at = rim_sections(last_end, halo_ref, q_ref, s_ref, t_ref, rim_ref, table_ref, ja_ref, jc_ref, omega_ref, scratch)
-    half = ROWS // 2
-    mine = pl.ds(pl.multiple_of(last_end * half, half), half)
-    for i in range(PLANES):
-        result[i, HALO : ROWS - HALO, :] = core_ref[i]
-        result[i, pl.ds(last_end * (ROWS - HALO), HALO), :] = end[i, pl.ds(at, HALO), :]
-    copy = pltpu.make_async_copy(result.at[:, mine, :], out_ref.at[:, mine, :], sem)
+    copy = pltpu.make_async_copy(near_ref, half_of(out_ref, 1 - last_end), sem)
     copy.start()
+    end, at = rim_sections(last_end, halo_ref, q_ref, s_ref, t_ref, rim_ref, table_ref, coef, scratch)
+    fill_half(last_end, end, at, core_ref, half_ref)
 
     pressure = []
     for ec in range(4):
         i = ec * 5 + 4
-        far = [result[i, pl.ds(last_end * half + r, TILE), :] for r in (0, TILE)]
-        near = [half_ref[i, r : r + TILE, :] for r in (0, TILE)]
+        far = [half_ref[i, r : r + TILE, :] for r in (0, TILE)]
+        near = [near_ref[i, r : r + TILE, :] for r in (0, TILE)]
         pressure.append([jnp.where(last_end == 1, n, f) for f, n in zip(far, near)]
                         + [jnp.where(last_end == 1, f, n) for f, n in zip(far, near)])
-    sums = []
-    modes = moments_ref.shape[0] // ROWS
-    for m in range(modes):
-        for ec in range(4):
-            acc = None
-            for r in range(0, ROWS, TILE):
-                term = moments_ref[m * ROWS + r : m * ROWS + r + TILE, :] * pressure[ec][r // TILE]
-                acc = term if acc is None else acc + term
-            sums.append(acc)
-    stacked = jnp.concatenate(sums, axis=0)
-    count = len(sums)
-    pick = lax.broadcasted_iota(jnp.int32, (LANES, count * TILE), 1) // TILE
-    pick = (pick == lax.broadcasted_iota(jnp.int32, (LANES, count * TILE), 0)).astype(jnp.float32)
-    by_lane = jnp.dot(pick, stacked, precision=HIGH, preferred_element_type=jnp.float32)
-    ones = jnp.ones(force_ref.shape, jnp.float32)
-    force_ref[...] = lax.dot_general(
-        ones, by_lane, (((1,), (1,)), ((), ())), precision=HIGH, preferred_element_type=jnp.float32
-    )
+    items = []
+    for at in range(64):
+        g, ec, odd = at % 8, at // 8 % 4, at // 32
+        m = g // 2 * 4 + g % 2 * 2 + odd
+        acc = None
+        for r in range(0, ROWS, TILE):
+            term = moments_ref[m * ROWS + r : m * ROWS + r + TILE, :] * pressure[ec][r // TILE]
+            acc = term if acc is None else acc + term
+        items.append(acc)
+    force_ref[...] = jnp.broadcast_to(reduce_to_lanes(items), force_ref.shape)
     copy.wait()
 
 
@@ -320,11 +327,12 @@
     got = in_ref[...]
     mine = lax.axis_index("yl")
     lane = lax.broadcasted_iota(jnp.int32, (1, LANES), 1)
-    keep = (lane % 16 < 4) & (lane < 64)
+    keep = lane % 32 < 4
+    at = mine // 2 * 16 + mine % 2 * 4
     total = None
     for yl in range(SIZES[1]):
         part = jnp.sum(got[yl * 4 : yl * 4 + 4, :], axis=0, keepdims=True)
-        part = pltpu.roll(part, (LANES - 4 * mine) % LANES, 1)
+        part = pltpu.roll(part, (LANES - at) % LANES, 1)
         part = jnp.where(keep, part, 0.0)
         if yl:
             part = pltpu.roll(part, 4 * yl, 1)
@@ -332,13 +340,15 @@
     out_ref[...] = jnp.broadcast_to(total, out_ref.shape)
 
 
-def final_kernel(in_ref, table_ref, out_ref):
+def final_kernel(in_ref, table_ref, half_ref, _, out_ref, result_ref, sem):
+    copy = pltpu.make_async_copy(half_ref, half_of(result_ref, lax.axis_index("core")), sem)
+    copy.start()
     mine = lax.axis_index("x")
     depth = SIZES[2]
     parts = [
         jnp.sum(in_ref[x * depth : (x + 1) * depth, :], axis=0, keepdims=True) for x in range(SIZES[0])
     ]
-    force = pltpu.roll(jnp.concatenate(parts, axis=0), (LANES - 16 * mine) % LANES, 1)
+    force = pltpu.roll(jnp.concatenate(parts, axis=0), (LANES - 32 * mine) % LANES, 1)
     n = SIZES[0] * SIZES[1]
     for e in range(2):
         real, imag = None, None
@@ -355,6 +365,7 @@
         scale = 1.0 / BLADES
         out_ref[0, 0, e : e + 1, :] = (jnp.sum(real, axis=0, keepdims=True) * scale)[:, :BLADES]
         out_ref[0, 1, e : e + 1, :] = (jnp.sum(imag, axis=0, keepdims=True) * scale)[:, :BLADES]
+    copy.wait()
 
 
 def shape(*dims):
@@ -395,46 +406,49 @@
         [ANY] * 3,
         [edge, edge, pltpu.VMEM((16, LANES), jnp.float32), pltpu.SemaphoreType.DMA((3,))],
     )(*map(in_hbm, (q, src, time_step)))
-    coef = pltpu.VMEM((50, TILE, LANES), jnp.float32)
     big = pltpu.VMEM((PLANES, ROWS + 16, LANES), jnp.float32)
     faces = surf_cell.shape[0]
-    near, moments, table = call(
+    near, moments, table, coef = call(
         prep_kernel,
-        (shape(MSG, LANES), shape(16 * ROWS, LANES), shape(48, LANES)),
-        [ANY] * 4 + [SMEM] + [VMEM] * 3,
+        (shape(MSG, LANES), shape(16 * ROWS, LANES), shape(48, LANES), shape(52, TILE, LANES)),
+        [ANY] * 7 + [SMEM] + [VMEM] * 3,
         [pltpu.VMEM((1, faces), jnp.int32), pltpu.VMEM((16, faces), jnp.float32)]
-        + [pltpu.SMEM(diam_ids.shape, jnp.int32), pltpu.SemaphoreType.DMA((3,))],
-    )(*map(in_hbm, (surf_cell.reshape(1, -1), surf_weight, diam_ids)), far, face_count, q, src, time_step)
+        + [pltpu.SMEM(diam_ids.shape, jnp.int32), pltpu.VMEM((5, 5), jnp.float32), pltpu.VMEM((5, 5), jnp.float32)]
+        + [pltpu.VMEM((1, 2), jnp.float32), pltpu.SemaphoreType.DMA((6,))],
+    )(
+        *map(in_hbm, (surf_cell.reshape(1, -1), surf_weight, diam_ids, jac_axial, jac_circ, omega.reshape(1, 2))),
+        far, face_count, q, src, time_step,
+    )
     far = lax.ppermute(far, AXES, swap_pairs(False))
     near = lax.ppermute(near, AXES, swap_pairs(True))
     rim, core = call(
         inner_kernel,
         (shape(LEVELS - 1, PLANES, TILE, LANES), shape(PLANES, TILE, LANES)),
-        [SMEM] * 3 + [VMEM] * 4,
-        [big, big, big, big, pltpu.VMEM((ROWS + 16, LANES), jnp.float32), coef],
-    )(jac_axial, jac_circ, omega, q, src, time_step, table)
+        [VMEM] * 5,
+        [big, big, big, big, pltpu.VMEM((ROWS + 16, LANES), jnp.float32)],
+    )(coef, q, src, time_step, table)
     big = pltpu.VMEM((PLANES, PART, LANES), jnp.float32)
-    scratch = [pltpu.VMEM((PLANES, ROWS, LANES), jnp.float32), pltpu.SemaphoreType.DMA]
-    scratch += [big] * 5 + [pltpu.VMEM((PART, LANES), jnp.float32), coef]
-    half, result = call(
-        near_rim_kernel,
-        (shape(PLANES, ROWS // 2, LANES), shape(PLANES, ROWS, LANES)),
-        [SMEM] * 3 + [VMEM] * 7,
-        scratch,
-        out_specs=(VMEM, ANY),
-    )(jac_axial, jac_circ, omega, q, src, time_step, near, table, rim, core)
-    result, force = call(
+    scratch = [big] * 5 + [pltpu.VMEM((PART, LANES), jnp.float32)]
+    half = shape(PLANES, ROWS // 2, LANES)
+    near_half = call(near_rim_kernel, half, [VMEM] * 8, scratch)(coef, q, src, time_step, near, table, rim, core)
+    result, far_half, force = call(
         far_rim_kernel,
-        (shape(PLANES, ROWS, LANES), shape(16, LANES)),
-        [SMEM] * 3 + [VMEM] * 9 + [ANY],
-        scratch,
-        out_specs=(ANY, VMEM),
-        aliases={12: 0},
-    )(jac_axial, jac_circ, omega, q, src, time_step, far, moments, table, rim, core, half, result)
+        (shape(PLANES, ROWS, LANES), half, shape(16, LANES)),
+        [VMEM] * 10,
+        [pltpu.SemaphoreType.DMA] + scratch,
+        out_specs=(ANY, VMEM, VMEM),
+    )(coef, q, src, time_step, far, moments, table, rim, core, near_half)
     got = lax.all_to_all(force, ("yl", "yh", "core"), 0, 0, tiled=True)
     middle = call(middle_kernel, shape(32, LANES), [VMEM])(got)
     got = lax.all_to_all(middle, ("x", "z"), 0, 0, tiled=True)
-    influence = call(final_kernel, shape(1, 2, 2, BLADES), [VMEM, VMEM])(got, table)
+    influence, result = call(
+        final_kernel,
+        (shape(1, 2, 2, BLADES), shape(PLANES, ROWS, LANES)),
+        [VMEM] * 3 + [ANY],
+        [pltpu.SemaphoreType.DMA],
+        out_specs=(VMEM, ANY),
+        aliases={3: 1},
+    )(got, table, far_half, result)
     return result.reshape(perturbation.shape), influence
 
 

time: 63.4 us -> 62.9 us (level)
  Pallas kernels: 17.3 us -> 15.3 us
  blocking collectives: 33.5 us -> 35.1 us
    pallas_call x3, Pallas kernels: 10.3 us -> 8.55 us  [the longest x1 3.81 us: per_device(): call(far_rim_kernel, (shape(PLANES, ROWS, LANES), half, shape(16, LANES))...]
    all_to_all x1, blocking collectives: 10.8 us -> 12.2 us  [per_device(): got = lax.all_to_all(force, ('yl', 'yh', 'core'), 0, 0, tiled=True)]
  transfers between devices with their start and end apart: 2 -> 2, of which waited for: 0 -> 0; matrix products, arithmetic and copies ran while one was open for 0% -> 0% of each run, Pallas kernels for 17% -> 14%
where the time goes in v6:
time: 62.9 us; the launch traced here: 62.6 us
  blocking collectives  35.1 us (56%)
  Pallas kernels  15.3 us (24%)
  starting transfers between devices  10.8 us (17%)
  between operations  1.39 us (2%)
    all_to_all x1, blocking collectives, per_device(): got = lax.all_to_all(middle, ('x', 'z'), 0, 0, tiled=True)  22.9 us
    all_to_all x1, blocking collectives, per_device(): got = lax.all_to_all(force, ('yl', 'yh', 'core'), 0, 0, tiled=True)  12.2 us
    ppermute x1, starting transfers between devices, per_device(): far = lax.ppermute(far, AXES, swap_pairs(False))  8.83 us
    pallas_call x1, Pallas kernels, per_device(): call(inner_kernel, (shape(LEVELS - 1, PLANES, TILE, LANES), shape(PLANES,...  4 us
    pallas_call x1, Pallas kernels, per_device(): call(far_rim_kernel, (shape(PLANES, ROWS, LANES), half, shape(16, LANES))...  3.81 us
    pallas_call x1, Pallas kernels, per_device(): call(near_rim_kernel, half, [VMEM] * 8, scratch)  3.49 us
    ppermute x1, starting transfers between devices, per_device(): near = lax.ppermute(near, AXES, swap_pairs(True))  1.92 us
    pallas_call x1, Pallas kernels, per_device(): call(prep_kernel, (shape(MSG, LANES), shape(16 * ROWS, LANES), shape(48,...  1.5 us
  transfers between devices with their start and end apart: 2, of which 0 were waited for; matrix products, arithmetic and copies ran while one was open for 0% of the time, Pallas kernels for 14%

profile of v6, /device:TPU:1, one launch (start us, length us, event | category | flops | bytes accessed | tf_op | source)
XLA Modules:
  0.0 62.6 jit_solution(7497321930064749831)
XLA Ops:
  0.6 0.0 copy-start
  0.6 0.0 copy-start.1
  0.6 0.0 copy-start.2
  0.7 1.1 %shard_map.113._ = f32[480,128]{1,0:T(8,128)S(1)} custom-call(f32[20,32,128]{2,1,0:T(8,128)} %bitcast.13, f32[20,32,128]{2,1,0:T(8,128)} %bitcast.18, f32[32,128]{1,0:T(8,128)} %t_ref.9), custom_call_target="tpu_custom_call" | custom-call | flops 1000 | bytes 1000 | tf_op jit(solution)/shard_map/pallas_call | solution.py:403
  1.8 8.8 %collective-permute-start = (f32[480,128]{1,0:T(8,128)S(1)}, f32[480,128]{1,0:T(8,128)S(1)}, u32[]{:S(2)}, u32[]{:S(2)}) collective-permute-start(f32[480,128]{1,0:T(8,128)S(1)} %shard_map.113._), channel_id=1, source_target_pairs={{1,2},{2,1},{3,4},{4,3},{5,6},{6,5},{7,8},{8,7},{9,10},{10,9},{11,... | collective-permute-start | bytes 737288 | tf_op jit(solution)/shard_map/ppermute | solution.py:422
  11.3 0.0 copy-done
  11.3 0.0 copy-done.1
  11.3 0.0 copy-done.2
  11.3 1.5 %shard_map.114 = (f32[472,128]{1,0:T(8,128)S(1)}, f32[512,128]{1,0:T(8,128)S(1)}, f32[48,128]{1,0:T(8,128)S(1)}, f32[52,8,128]{2,1,0:T(8,128)S(1)}) custom-call(s32[1,512]{1,0:T(1,128)} %bitcast.28, f32[16,512]{1,0:T(8,128)} %weight_ref.1, s32[16]{0:T(128)} %ids_ref.1, f32[5,5]{1,0:T(8,128)} %ja_ref.1, f32[5,5]{1,0:T(8,128)} %jc_ref.1, f32[1,2]{1,0:T(1,128)} %bitcast.29, ...), custom_call_target="tpu_custom_call" | custom-call | flops 1000 | bytes 1000 | tf_op jit(solution)/shard_map/pallas_call | solution.py:411
  12.8 1.9 %collective-permute-start.1 = (f32[472,128]{1,0:T(8,128)S(1)}, f32[472,128]{1,0:T(8,128)S(1)}, u32[]{:S(2)}, u32[]{:S(2)}) collective-permute-start(f32[472,128]{1,0:T(8,128)S(1)} %get-tuple-element.18), channel_id=1, source_target_pairs={{0,1},{1,0},{2,3},{3,2},{4,5},{5,4},{6,7},{7,6},{8,9},{9,8},{10,11... | collective-permute-start | bytes 725000 | tf_op jit(solution)/shard_map/ppermute | solution.py:423
  14.7 4.0 %shard_map.115 = (f32[11,20,8,128]{3,2,1,0:T(8,128)S(1)}, f32[20,8,128]{2,1,0:T(8,128)S(1)}) custom-call(f32[52,8,128]{2,1,0:T(8,128)S(1)} %get-tuple-element.13.coef, f32[20,32,128]{2,1,0:T(8,128)S(1)} %bitcast.15, f32[20,32,128]{2,1,0:T(8,128)S(1)} %bitcast.20, f32[32,128]{1,0:T(8,128)S(1)} %copy-done.2, f32[48,128]{1,0:T(8,128)S(1)} %get-tuple-element.15.table_ref), custom_call_target="tpu_custom_call" | custom-call | flops 1000 | bytes 1000 | tf_op jit(solution)/shard_map/pallas_call | solution.py:424
  18.7 0.0 collective-permute-done.1.halo_ref
  18.8 3.5 %shard_map.116.near_ref = f32[20,16,128]{2,1,0:T(8,128)S(1)} custom-call(f32[52,8,128]{2,1,0:T(8,128)S(1)} %get-tuple-element.13.coef, f32[20,32,128]{2,1,0:T(8,128)S(1)} %bitcast.16, f32[20,32,128]{2,1,0:T(8,128)S(1)} %bitcast.21, f32[32,128]{1,0:T(8,128)S(1)} %copy-done.2, f32[472,128]{1,0:T(8,128)S(1)} %collective-permute-done.1.halo_ref, ...), custom_call_target="tpu_custom_call" | custom-call | flops 1000 | bytes 1000 | tf_op jit(solution)/shard_map/pallas_call | solution.py:433
  22.2 0.0 collective-permute-done.halo_ref
  22.3 3.8 %shard_map.117 = (f32[20,32,128]{2,1,0:T(8,128)}, f32[20,16,128]{2,1,0:T(8,128)S(1)}, f32[16,128]{1,0:T(8,128)S(1)}) custom-call(f32[52,8,128]{2,1,0:T(8,128)S(1)} %get-tuple-element.13.coef, f32[20,32,128]{2,1,0:T(8,128)S(1)} %bitcast.17, f32[20,32,128]{2,1,0:T(8,128)S(1)} %bitcast.22, f32[32,128]{1,0:T(8,128)S(1)} %copy-done.2, ...), custom_call_target="tpu_custom_call" | custom-call | flops 1000 | bytes 1000 | tf_op jit(solution)/shard_map/pallas_call | solution.py:434
  26.1 12.2 %all_to_all.22 = f32[16,1,128]{2,1,0:T(1,128)S(1)} all-to-all(f32[16,1,128]{2,1,0:T(1,128)S(1)} %bitcast.26), channel_id=1, replica_groups=mesh['x'=4,'yl'=4,'z'=8,'yh'=2,'core'=2] {'yl','yh','core'}, dimensions={0} | all-to-all | bytes 16384 | tf_op jit(solution)/shard_map/all_to_all | solution.py:441
  38.2 0.1 shard_map.118
  38.4 22.9 %all_to_all.23 = f32[32,1,128]{2,1,0:T(1,128)S(1)} all-to-all(f32[32,1,128]{2,1,0:T(1,128)S(1)} %bitcast.24), channel_id=1, replica_groups=mesh['x'=4,'yl'=4,'z'=8,'yh'=2,'core'=2] {'x','z'}, dimensions={0} | all-to-all | bytes 32768 | tf_op jit(solution)/shard_map/all_to_all | solution.py:443
  61.3 1.3 %shard_map.119 = (f32[1,2,2,72]{3,2,1,0:T(2,128)}, f32[20,32,128]{2,1,0:T(8,128)}) custom-call(f32[32,128]{1,0:T(8,128)S(1)} %bitcast.23, f32[48,128]{1,0:T(8,128)S(1)} %get-tuple-element.15.table_ref, f32[20,16,128]{2,1,0:T(8,128)S(1)} %get-tuple-element.20.half_ref, f32[20,32,128]{2,1,0:T(8,128)} %get-tuple-element.21._), custom_call_target="tpu_custom_call", output_to_operand_aliasing={{1}: (3, {})} | custom-call | flops 1000 | bytes 1000 | tf_op jit(solution)/shard_map/pallas_call | solution.py:444
Async XLA Ops:
  0.6 10.6 %copy-start = (f32[1,2,2,5,32,128]{5,4,3,2,1,0:T(8,128)S(1)}, f32[1,2,2,5,32,128]{5,4,3,2,1,0:T(8,128)}, u32[]{:S(2)}) copy-start(f32[1,2,2,5,32,128]{5,4,3,2,1,0:T(8,128)} %param.10) | copy-start | bytes 983044
  0.6 10.6 %copy-start.1 = (f32[2,2,5,32,128]{4,3,2,1,0:T(8,128)S(1)}, f32[2,2,5,32,128]{4,3,2,1,0:T(8,128)}, u32[]{:S(2)}) copy-start(f32[2,2,5,32,128]{4,3,2,1,0:T(8,128)} %param.11) | copy-start | bytes 983044
  0.6 10.6 %copy-start.2 = (f32[32,128]{1,0:T(8,128)S(1)}, f32[32,128]{1,0:T(8,128)}, u32[]{:S(2)}) copy-start(f32[32,128]{1,0:T(8,128)} %t_ref.9) | copy-start | bytes 49156
  1.8 20.5 %collective-permute-start = (f32[480,128]{1,0:T(8,128)S(1)}, f32[480,128]{1,0:T(8,128)S(1)}, u32[]{:S(2)}, u32[]{:S(2)}) collective-permute-start(f32[480,128]{1,0:T(8,128)S(1)} %shard_map.113._), channel_id=1, source_target_pairs={{1,2},{2,1},{3,4},{4,3},{5,6},{6,5},{7,8},{8,7},{9,10},{10,9},{11,... | collective-permute-start | bytes 737288 | tf_op jit(solution)/shard_map/ppermute | solution.py:422
  12.8 5.9 %collective-permute-start.1 = (f32[472,128]{1,0:T(8,128)S(1)}, f32[472,128]{1,0:T(8,128)S(1)}, u32[]{:S(2)}, u32[]{:S(2)}) collective-permute-start(f32[472,128]{1,0:T(8,128)S(1)} %get-tuple-element.18), channel_id=1, source_target_pairs={{0,1},{1,0},{2,3},{3,2},{4,5},{5,4},{6,7},{7,6},{8,9},{9,8},{10,11... | collective-permute-start | bytes 725000 | tf_op jit(solution)/shard_map/ppermute | solution.py:423

commit v7 on v6

--- a/solution.py
+++ b/solution.py
@@ -25,7 +25,7 @@
 FAR_MSG = MSG + 8
 LEVELS = HALO
 OWN = 8
-PART = 32
+RIM = 48
 TILE = 8
 
 
@@ -66,11 +66,12 @@
     core = lax.axis_index("core")
     wide = q_buf.shape[1]
     rows = pl.ds(pl.multiple_of(core * (ROWS - wide), TILE), wide)
-    copies = [
-        pltpu.make_async_copy(q_ref.at[:, rows, :], q_buf, sems.at[0]),
-        pltpu.make_async_copy(s_ref.at[:, rows, :], s_buf, sems.at[1]),
-        pltpu.make_async_copy(t_ref.at[rows, :], t_buf, sems.at[2]),
-    ]
+    piece = PLANES // 4
+    copies = [pltpu.make_async_copy(t_ref.at[rows, :], t_buf, sems.at[8])]
+    for i in range(4):
+        some = slice(i * piece, (i + 1) * piece)
+        copies.append(pltpu.make_async_copy(q_ref.at[some, rows, :], q_buf.at[some], sems.at[i]))
+        copies.append(pltpu.make_async_copy(s_ref.at[some, rows, :], s_buf.at[some], sems.at[4 + i]))
     for copy in copies:
         copy.start()
     for copy in copies:
@@ -100,40 +101,64 @@
     return is_first, is_last, turn_c, turn_s
 
 
+def block_update(load, store, freq, dt, coef, phase):
+    is_first, is_last, turn_c, turn_s = phase
+    center = [load("cur", p, 0) for p in range(10)]
+    axial, circ, total = [], [], []
+    for p in range(10):
+        up, down = load("cur", p, 1), load("cur", p, -1)
+        mid, other = center[p], center[(p + 5) % 10]
+        turned = turn_c * mid + turn_s * other if p < 5 else turn_c * mid - turn_s * other
+        right = pltpu.roll(jnp.where(is_first, turned, mid), LANES - 1, 1)
+        left = pltpu.roll(jnp.where(is_last, turned, mid), 1, 1)
+        axial.append(up - down)
+        circ.append(right - left)
+        total.append((up + down) + (right + left))
+    for p in range(10):
+        c, u = divmod(p, 5)
+        acc = total[p] + load("forced", p, 0) - 4.0 * center[p]
+        spin = freq * center[(p + 5) % 10]
+        acc = acc + spin if c == 0 else acc - spin
+        conv = None
+        for v in range(5):
+            a = coef[u * 5 + v] * axial[c * 5 + v]
+            b = coef[25 + u * 5 + v] * circ[c * 5 + v]
+            conv = a + b if conv is None else conv + (a + b)
+        store(p, load("base", p, 0) + dt * (acc - conv))
+
+
 def tile_update(cur, base, new, forced, step, coef, phase, alpha, row):
-    is_first, is_last, turn_c, turn_s = phase
+    refs = dict(cur=cur, base=base, forced=forced)
     here = pl.ds(row, TILE)
     dt = step[here, :] * (alpha * 0.2)
     for e in range(2):
-        center, axial, circ, total = [], [], [], []
-        for c in range(2):
-            for v in range(5):
-                center.append(cur[e * 10 + c * 5 + v, here, :])
-        for c in range(2):
-            for v in range(5):
-                i = e * 10 + c * 5 + v
-                up = cur[i, pl.ds(row + 1, TILE), :]
-                down = cur[i, pl.ds(row - 1, TILE), :]
-                mid, other = center[c * 5 + v], center[(1 - c) * 5 + v]
-                turned = turn_c * mid + turn_s * other if c == 0 else turn_c * mid - turn_s * other
-                right = pltpu.roll(jnp.where(is_first, turned, mid), LANES - 1, 1)
-                left = pltpu.roll(jnp.where(is_last, turned, mid), 1, 1)
-                axial.append(up - down)
-                circ.append(right - left)
-                total.append((up + down) + (right + left))
-        freq = coef[50 + e]
-        for c in range(2):
-            for u in range(5):
-                i = e * 10 + c * 5 + u
-                acc = total[c * 5 + u] + forced[i, here, :] - 4.0 * center[c * 5 + u]
-                spin = freq * center[(1 - c) * 5 + u]
-                acc = acc + spin if c == 0 else acc - spin
-                conv = None
-                for v in range(5):
-                    a = coef[u * 5 + v] * axial[c * 5 + v]
-                    b = coef[25 + u * 5 + v] * circ[c * 5 + v]
-                    conv = a + b if conv is None else conv + (a + b)
-                new[i, here, :] = base[i, here, :] + dt * (acc - conv)
+
+        def load(kind, p, shift, e=e):
+            return refs[kind][e * 10 + p, pl.ds(row + shift, TILE), :]
+
+        def store(p, value, e=e):
+            new[e * 10 + p, here, :] = value
+
+        block_update(load, store, coef[50 + e], dt, coef, phase)
+
+
+def mixed_update(cur, base, new, forced, step, coef, phase, alpha, row):
+    refs = dict(cur=cur, base=base, forced=forced)
+    upper = lax.broadcasted_iota(jnp.int32, (TILE, LANES), 0) < 4
+    places = (pl.ds(row, TILE), pl.ds(row - 4, TILE))
+
+    def load(kind, p, shift):
+        ref = refs[kind]
+        first = ref[p, pl.ds(row + shift, TILE), :]
+        second = ref[10 + p, pl.ds(row - 4 + shift, TILE), :]
+        return jnp.where(upper, first, second)
+
+    def store(p, value):
+        new[p, places[0], :] = value
+        new[10 + p, places[1], :] = value
+
+    dt = jnp.where(upper, step[places[0], :], step[places[1], :]) * (alpha * 0.2)
+    block_update(load, store, jnp.where(upper, coef[50], coef[51]), dt, coef, phase)
 
 
 def make_moments(cell_ref, weight_ref, count_ref, moments_ref):
@@ -225,11 +250,12 @@
 def rim_sections(last_end, halo_ref, q_ref, s_ref, t_ref, rim_ref, table_ref, coef, scratch):
     base, other, first, second, forced, step = scratch
     phase = phases(table_ref)
-    half = PART // 2
+    half = ROWS // 2
+    low, mid = TILE, TILE + half
     taken = pl.ds(pl.multiple_of(last_end * half, half), half)
-    own = pl.ds(pl.multiple_of((1 - last_end) * half, half), half)
-    halo = pl.ds(jnp.where(last_end == 1, half, half - HALO), HALO)
-    fewer = pl.ds(jnp.where(last_end == 1, half, half - HALO + 1), HALO - 1)
+    own = pl.ds(pl.multiple_of(jnp.where(last_end == 1, low, mid), TILE), half)
+    halo = pl.ds(jnp.where(last_end == 1, mid, mid - HALO), HALO)
+    fewer = pl.ds(jnp.where(last_end == 1, mid, mid - HALO + 1), HALO - 1)
     for i in range(PLANES):
         base[i, own, :] = q_ref[i, taken, :]
         base[i, halo, :] = halo_ref[i * HALO : (i + 1) * HALO, :]
@@ -245,15 +271,16 @@
         for k in range(SECTIONS):
             t = it * SECTIONS + k + 1
             cur, new = bufs[k], bufs[k + 1]
-            row = jnp.where(last_end == 1, half - t, half - HALO + t)
-            for shift in (0, HALO - TILE):
-                tile_update(cur, start, new, forced, step, coef, phase, ALPHAS[k], row + shift)
+            shared = jnp.where(last_end == 1, mid - t, mid - 4 + t)
+            alone = jnp.where(last_end == 1, mid - t + 4, mid - HALO + t)
+            mixed_update(cur, start, new, forced, step, coef, phase, ALPHAS[k], shared)
+            tile_update(cur, start, new, forced, step, coef, phase, ALPHAS[k], alone)
             if t < LEVELS:
                 kept = pl.ds(last_end * 4, 4)
-                place = pl.ds(jnp.where(last_end == 1, half - 4 - t, half + t), 4)
+                place = pl.ds(jnp.where(last_end == 1, mid - 4 - t, mid + t), 4)
                 for i in range(PLANES):
                     new[i, place, :] = rim_ref[t - 1, i, kept, :]
-    return end, jnp.where(last_end == 1, half - HALO, half)
+    return end, jnp.where(last_end == 1, mid - HALO, mid)
 
 
 def reduce_to_lanes(items):
@@ -340,9 +367,14 @@
     out_ref[...] = jnp.broadcast_to(total, out_ref.shape)
 
 
-def final_kernel(in_ref, table_ref, half_ref, _, out_ref, result_ref, sem):
-    copy = pltpu.make_async_copy(half_ref, half_of(result_ref, lax.axis_index("core")), sem)
-    copy.start()
+def final_kernel(in_ref, table_ref, half_ref, _, out_ref, result_ref, out, sems):
+    place = half_of(result_ref, lax.axis_index("core"))
+    piece = PLANES // 4
+    copies = []
+    for i in range(4):
+        some = slice(i * piece, (i + 1) * piece)
+        copies.append(pltpu.make_async_copy(half_ref.at[some], place.at[some], sems.at[i]))
+        copies[i].start()
     mine = lax.axis_index("x")
     depth = SIZES[2]
     parts = [
@@ -363,9 +395,12 @@
             real = r if real is None else real + r
             imag = i if imag is None else imag + i
         scale = 1.0 / BLADES
-        out_ref[0, 0, e : e + 1, :] = (jnp.sum(real, axis=0, keepdims=True) * scale)[:, :BLADES]
-        out_ref[0, 1, e : e + 1, :] = (jnp.sum(imag, axis=0, keepdims=True) * scale)[:, :BLADES]
-    copy.wait()
+        out[0, 0, e : e + 1, :] = (jnp.sum(real, axis=0, keepdims=True) * scale)[:, :BLADES]
+        out[0, 1, e : e + 1, :] = (jnp.sum(imag, axis=0, keepdims=True) * scale)[:, :BLADES]
+    copies.append(pltpu.make_async_copy(out, out_ref, sems.at[4]))
+    copies[4].start()
+    for copy in copies:
+        copy.wait()
 
 
 def shape(*dims):
@@ -404,7 +439,7 @@
         far_kernel,
         shape(FAR_MSG, LANES),
         [ANY] * 3,
-        [edge, edge, pltpu.VMEM((16, LANES), jnp.float32), pltpu.SemaphoreType.DMA((3,))],
+        [edge, edge, pltpu.VMEM((16, LANES), jnp.float32), pltpu.SemaphoreType.DMA((9,))],
     )(*map(in_hbm, (q, src, time_step)))
     big = pltpu.VMEM((PLANES, ROWS + 16, LANES), jnp.float32)
     faces = surf_cell.shape[0]
@@ -427,8 +462,8 @@
         [VMEM] * 5,
         [big, big, big, big, pltpu.VMEM((ROWS + 16, LANES), jnp.float32)],
     )(coef, q, src, time_step, table)
-    big = pltpu.VMEM((PLANES, PART, LANES), jnp.float32)
-    scratch = [big] * 5 + [pltpu.VMEM((PART, LANES), jnp.float32)]
+    big = pltpu.VMEM((PLANES, RIM, LANES), jnp.float32)
+    scratch = [big] * 5 + [pltpu.VMEM((RIM, LANES), jnp.float32)]
     half = shape(PLANES, ROWS // 2, LANES)
     near_half = call(near_rim_kernel, half, [VMEM] * 8, scratch)(coef, q, src, time_step, near, table, rim, core)
     result, far_half, force = call(
@@ -445,8 +480,8 @@
         final_kernel,
         (shape(1, 2, 2, BLADES), shape(PLANES, ROWS, LANES)),
         [VMEM] * 3 + [ANY],
-        [pltpu.SemaphoreType.DMA],
-        out_specs=(VMEM, ANY),
+        [pltpu.VMEM((1, 2, 2, BLADES), jnp.float32), pltpu.SemaphoreType.DMA((5,))],
+        out_specs=(ANY, ANY),
         aliases={3: 1},
     )(got, table, far_half, result)
     return result.reshape(perturbation.shape), influence

time: 62.9 us -> 62.2 us (0.989)
  Pallas kernels: 15.3 us -> 14 us
where the time goes in v7:
time: 62.2 us; the launch traced here: 61.9 us
  blocking collectives  35.7 us (57%)
  Pallas kernels  14 us (23%)
  starting transfers between devices  10.8 us (17%)
  between operations  1.39 us (2%)
    all_to_all x1, blocking collectives, per_device(): got = lax.all_to_all(middle, ('x', 'z'), 0, 0, tiled=True)  22.9 us
    all_to_all x1, blocking collectives, per_device(): got = lax.all_to_all(force, ('yl', 'yh', 'core'), 0, 0, tiled=True)  12.7 us
    ppermute x1, starting transfers between devices, per_device(): far = lax.ppermute(far, AXES, swap_pairs(False))  8.83 us
    pallas_call x1, Pallas kernels, per_device(): call(inner_kernel, (shape(LEVELS - 1, PLANES, TILE, LANES), shape(PLANES,...  4 us
    pallas_call x1, Pallas kernels, per_device(): call(far_rim_kernel, (shape(PLANES, ROWS, LANES), half, shape(16, LANES))...  3.54 us
    pallas_call x1, Pallas kernels, per_device(): call(near_rim_kernel, half, [VMEM] * 8, scratch)  2.94 us
    ppermute x1, starting transfers between devices, per_device(): near = lax.ppermute(near, AXES, swap_pairs(True))  1.92 us
    pallas_call x1, Pallas kernels, per_device(): call(prep_kernel, (shape(MSG, LANES), shape(16 * ROWS, LANES), shape(48,...  1.5 us
  transfers between devices with their start and end apart: 2, of which 0 were waited for; matrix products, arithmetic and copies ran while one was open for 0% of the time, Pallas kernels for 14%

profile of v7, /device:TPU:1, one launch (start us, length us, event | category | flops | bytes accessed | tf_op | source)
XLA Modules:
  0.0 61.9 jit_solution(4801506319868272215)
XLA Ops:
  0.6 0.0 copy-start
  0.6 0.0 copy-start.1
  0.6 0.0 copy-start.2
  0.7 1.1 %shard_map.113._ = f32[480,128]{1,0:T(8,128)S(1)} custom-call(f32[20,32,128]{2,1,0:T(8,128)} %bitcast.13, f32[20,32,128]{2,1,0:T(8,128)} %bitcast.18, f32[32,128]{1,0:T(8,128)} %t_ref.9), custom_call_target="tpu_custom_call" | custom-call | flops 1000 | bytes 1000 | tf_op jit(solution)/shard_map/pallas_call | solution.py:438
  1.8 8.8 %collective-permute-start = (f32[480,128]{1,0:T(8,128)S(1)}, f32[480,128]{1,0:T(8,128)S(1)}, u32[]{:S(2)}, u32[]{:S(2)}) collective-permute-start(f32[480,128]{1,0:T(8,128)S(1)} %shard_map.113._), channel_id=1, source_target_pairs={{1,2},{2,1},{3,4},{4,3},{5,6},{6,5},{7,8},{8,7},{9,10},{10,9},{11,... | collective-permute-start | bytes 737288 | tf_op jit(solution)/shard_map/ppermute | solution.py:457
  11.3 0.0 copy-done
  11.3 0.0 copy-done.1
  11.3 0.0 copy-done.2
  11.3 1.5 %shard_map.114 = (f32[472,128]{1,0:T(8,128)S(1)}, f32[512,128]{1,0:T(8,128)S(1)}, f32[48,128]{1,0:T(8,128)S(1)}, f32[52,8,128]{2,1,0:T(8,128)S(1)}) custom-call(s32[1,512]{1,0:T(1,128)} %bitcast.28, f32[16,512]{1,0:T(8,128)} %weight_ref.1, s32[16]{0:T(128)} %ids_ref.1, f32[5,5]{1,0:T(8,128)} %ja_ref.1, f32[5,5]{1,0:T(8,128)} %jc_ref.1, f32[1,2]{1,0:T(1,128)} %bitcast.29, ...), custom_call_target="tpu_custom_call" | custom-call | flops 1000 | bytes 1000 | tf_op jit(solution)/shard_map/pallas_call | solution.py:446
  12.8 1.9 %collective-permute-start.1 = (f32[472,128]{1,0:T(8,128)S(1)}, f32[472,128]{1,0:T(8,128)S(1)}, u32[]{:S(2)}, u32[]{:S(2)}) collective-permute-start(f32[472,128]{1,0:T(8,128)S(1)} %get-tuple-element.18), channel_id=1, source_target_pairs={{0,1},{1,0},{2,3},{3,2},{4,5},{5,4},{6,7},{7,6},{8,9},{9,8},{10,11... | collective-permute-start | bytes 725000 | tf_op jit(solution)/shard_map/ppermute | solution.py:458
  14.7 4.0 %shard_map.115 = (f32[11,20,8,128]{3,2,1,0:T(8,128)S(1)}, f32[20,8,128]{2,1,0:T(8,128)S(1)}) custom-call(f32[52,8,128]{2,1,0:T(8,128)S(1)} %get-tuple-element.13.coef, f32[20,32,128]{2,1,0:T(8,128)S(1)} %bitcast.15, f32[20,32,128]{2,1,0:T(8,128)S(1)} %bitcast.20, f32[32,128]{1,0:T(8,128)S(1)} %copy-done.2, f32[48,128]{1,0:T(8,128)S(1)} %get-tuple-element.15.table_ref), custom_call_target="tpu_custom_call" | custom-call | flops 1000 | bytes 1000 | tf_op jit(solution)/shard_map/pallas_call | solution.py:459
  18.7 0.0 collective-permute-done.1.halo_ref
  18.7 2.9 %shard_map.116.near_ref = f32[20,16,128]{2,1,0:T(8,128)S(1)} custom-call(f32[52,8,128]{2,1,0:T(8,128)S(1)} %get-tuple-element.13.coef, f32[20,32,128]{2,1,0:T(8,128)S(1)} %bitcast.16, f32[20,32,128]{2,1,0:T(8,128)S(1)} %bitcast.21, f32[32,128]{1,0:T(8,128)S(1)} %copy-done.2, f32[472,128]{1,0:T(8,128)S(1)} %collective-permute-done.1.halo_ref, ...), custom_call_target="tpu_custom_call" | custom-call | flops 1000 | bytes 1000 | tf_op jit(solution)/shard_map/pallas_call | solution.py:468
  21.7 0.0 collective-permute-done.halo_ref
  21.7 3.5 %shard_map.117 = (f32[20,32,128]{2,1,0:T(8,128)}, f32[20,16,128]{2,1,0:T(8,128)S(1)}, f32[16,128]{1,0:T(8,128)S(1)}) custom-call(f32[52,8,128]{2,1,0:T(8,128)S(1)} %get-tuple-element.13.coef, f32[20,32,128]{2,1,0:T(8,128)S(1)} %bitcast.17, f32[20,32,128]{2,1,0:T(8,128)S(1)} %bitcast.22, f32[32,128]{1,0:T(8,128)S(1)} %copy-done.2, ...), custom_call_target="tpu_custom_call" | custom-call | flops 1000 | bytes 1000 | tf_op jit(solution)/shard_map/pallas_call | solution.py:469
  25.3 12.7 %all_to_all.22 = f32[16,1,128]{2,1,0:T(1,128)S(1)} all-to-all(f32[16,1,128]{2,1,0:T(1,128)S(1)} %bitcast.26), channel_id=1, replica_groups=mesh['x'=4,'yl'=4,'z'=8,'yh'=2,'core'=2] {'yl','yh','core'}, dimensions={0} | all-to-all | bytes 16384 | tf_op jit(solution)/shard_map/all_to_all | solution.py:476
  38.0 0.1 shard_map.118
  38.1 22.9 %all_to_all.23 = f32[32,1,128]{2,1,0:T(1,128)S(1)} all-to-all(f32[32,1,128]{2,1,0:T(1,128)S(1)} %bitcast.24), channel_id=1, replica_groups=mesh['x'=4,'yl'=4,'z'=8,'yh'=2,'core'=2] {'x','z'}, dimensions={0} | all-to-all | bytes 32768 | tf_op jit(solution)/shard_map/all_to_all | solution.py:478
  61.1 0.8 %shard_map.119 = (f32[1,2,2,72]{3,2,1,0:T(2,128)}, f32[20,32,128]{2,1,0:T(8,128)}) custom-call(f32[32,128]{1,0:T(8,128)S(1)} %bitcast.23, f32[48,128]{1,0:T(8,128)S(1)} %get-tuple-element.15.table_ref, f32[20,16,128]{2,1,0:T(8,128)S(1)} %get-tuple-element.20.half_ref, f32[20,32,128]{2,1,0:T(8,128)} %get-tuple-element.21._), custom_call_target="tpu_custom_call", output_to_operand_aliasing={{1}: (3, {})} | custom-call | flops 1000 | bytes 1000 | tf_op jit(solution)/shard_map/pallas_call | solution.py:479
Async XLA Ops:
  0.6 10.6 %copy-start = (f32[1,2,2,5,32,128]{5,4,3,2,1,0:T(8,128)S(1)}, f32[1,2,2,5,32,128]{5,4,3,2,1,0:T(8,128)}, u32[]{:S(2)}) copy-start(f32[1,2,2,5,32,128]{5,4,3,2,1,0:T(8,128)} %param.10) | copy-start | bytes 983044
  0.6 10.6 %copy-start.1 = (f32[2,2,5,32,128]{4,3,2,1,0:T(8,128)S(1)}, f32[2,2,5,32,128]{4,3,2,1,0:T(8,128)}, u32[]{:S(2)}) copy-start(f32[2,2,5,32,128]{4,3,2,1,0:T(8,128)} %param.11) | copy-start | bytes 983044
  0.6 10.6 %copy-start.2 = (f32[32,128]{1,0:T(8,128)S(1)}, f32[32,128]{1,0:T(8,128)}, u32[]{:S(2)}) copy-start(f32[32,128]{1,0:T(8,128)} %t_ref.9) | copy-start | bytes 49156
  1.8 19.9 %collective-permute-start = (f32[480,128]{1,0:T(8,128)S(1)}, f32[480,128]{1,0:T(8,128)S(1)}, u32[]{:S(2)}, u32[]{:S(2)}) collective-permute-start(f32[480,128]{1,0:T(8,128)S(1)} %shard_map.113._), channel_id=1, source_target_pairs={{1,2},{2,1},{3,4},{4,3},{5,6},{6,5},{7,8},{8,7},{9,10},{10,9},{11,... | collective-permute-start | bytes 737288 | tf_op jit(solution)/shard_map/ppermute | solution.py:457
  12.8 5.9 %collective-permute-start.1 = (f32[472,128]{1,0:T(8,128)S(1)}, f32[472,128]{1,0:T(8,128)S(1)}, u32[]{:S(2)}, u32[]{:S(2)}) collective-permute-start(f32[472,128]{1,0:T(8,128)S(1)} %get-tuple-element.18), channel_id=1, source_target_pairs={{0,1},{1,0},{2,3},{3,2},{4,5},{5,4},{6,7},{7,6},{8,9},{9,8},{10,11... | collective-permute-start | bytes 725000 | tf_op jit(solution)/shard_map/ppermute | solution.py:458

commit v8 on v7

--- a/solution.py
+++ b/solution.py
@@ -187,8 +187,8 @@
 def make_tables(ids_ref, table_ref):
     blade = lax.broadcasted_iota(jnp.int32, (1, LANES), 1)
     rows = []
-    for yl, x in itertools.product(range(SIZES[1]), range(SIZES[0])):
-        rows.append(blade * ids_ref[x * SIZES[1] + yl])
+    for slot in range(SIZES[0] * SIZES[1]):
+        rows.append(blade * ids_ref[slot])
     product = jnp.concatenate(rows, axis=0)
     turns = ((product.astype(jnp.float32) + 0.5) * (1.0 / BLADES)).astype(jnp.int32)
     angle = 2.0 * jnp.pi * (product - turns * BLADES).astype(jnp.float32) / BLADES
@@ -351,20 +351,17 @@
 
 
 def middle_kernel(in_ref, out_ref):
-    got = in_ref[...]
-    mine = lax.axis_index("yl")
-    lane = lax.broadcasted_iota(jnp.int32, (1, LANES), 1)
-    keep = lane % 32 < 4
-    at = mine // 2 * 16 + mine % 2 * 4
-    total = None
-    for yl in range(SIZES[1]):
-        part = jnp.sum(got[yl * 4 : yl * 4 + 4, :], axis=0, keepdims=True)
-        part = pltpu.roll(part, (LANES - at) % LANES, 1)
-        part = jnp.where(keep, part, 0.0)
-        if yl:
-            part = pltpu.roll(part, 4 * yl, 1)
-        total = part if total is None else total + part
-    out_ref[...] = jnp.broadcast_to(total, out_ref.shape)
+    x, yl = lax.axis_index("x"), lax.axis_index("yl")
+    slots = SIZES[0] * SIZES[1]
+    rows = [in_ref[2 * n : 2 * n + 1, :] + in_ref[2 * n + 1 : 2 * n + 2, :] for n in range(slots)]
+    got = jnp.concatenate(rows, axis=0)
+    got = pltpu.roll(got, (LANES - (x * 32 + yl // 2 * 16 + yl % 2 * 4)) % LANES, 1)
+    lane = lax.broadcasted_iota(jnp.int32, got.shape, 1)
+    got = jnp.where(lane < 4, got, 0.0)
+    for shift in (4, 8, 16, 32):
+        got = got + pltpu.roll(got, shift, 1)
+    kept = jnp.where(lane // 4 == lax.broadcasted_iota(jnp.int32, got.shape, 0), got, 0.0)
+    out_ref[...] = jnp.broadcast_to(jnp.sum(kept, axis=0, keepdims=True), out_ref.shape)
 
 
 def final_kernel(in_ref, table_ref, half_ref, _, out_ref, result_ref, out, sems):
@@ -375,25 +372,15 @@
         some = slice(i * piece, (i + 1) * piece)
         copies.append(pltpu.make_async_copy(half_ref.at[some], place.at[some], sems.at[i]))
         copies[i].start()
-    mine = lax.axis_index("x")
-    depth = SIZES[2]
-    parts = [
-        jnp.sum(in_ref[x * depth : (x + 1) * depth, :], axis=0, keepdims=True) for x in range(SIZES[0])
-    ]
-    force = pltpu.roll(jnp.concatenate(parts, axis=0), (LANES - 32 * mine) % LANES, 1)
     n = SIZES[0] * SIZES[1]
+    total = jnp.broadcast_to(jnp.sum(in_ref[...], axis=0, keepdims=True), (n, LANES))
+    place = lax.broadcasted_iota(jnp.int32, (n, LANES), 1) - 4 * lax.broadcasted_iota(jnp.int32, (n, LANES), 0)
+    cosine, sine = table_ref[0:n, :], table_ref[n : 2 * n, :]
     for e in range(2):
-        real, imag = None, None
-        for yl in range(SIZES[1]):
-            at = yl * 4 + e * 2
-            f_r = force[:, at : at + 1]
-            f_i = force[:, at + 1 : at + 2]
-            cosine = table_ref[yl * 4 : yl * 4 + 4, :]
-            sine = table_ref[n + yl * 4 : n + yl * 4 + 4, :]
-            r = f_r * cosine - f_i * sine
-            i = f_r * sine + f_i * cosine
-            real = r if real is None else real + r
-            imag = i if imag is None else imag + i
+        f_r = jnp.sum(jnp.where(place == 2 * e, total, 0.0), axis=1, keepdims=True)
+        f_i = jnp.sum(jnp.where(place == 2 * e + 1, total, 0.0), axis=1, keepdims=True)
+        real = f_r * cosine - f_i * sine
+        imag = f_r * sine + f_i * cosine
         scale = 1.0 / BLADES
         out[0, 0, e : e + 1, :] = (jnp.sum(real, axis=0, keepdims=True) * scale)[:, :BLADES]
         out[0, 1, e : e + 1, :] = (jnp.sum(imag, axis=0, keepdims=True) * scale)[:, :BLADES]
@@ -468,14 +455,14 @@
     near_half = call(near_rim_kernel, half, [VMEM] * 8, scratch)(coef, q, src, time_step, near, table, rim, core)
     result, far_half, force = call(
         far_rim_kernel,
-        (shape(PLANES, ROWS, LANES), half, shape(16, LANES)),
+        (shape(PLANES, ROWS, LANES), half, shape(32, LANES)),
         [VMEM] * 10,
         [pltpu.SemaphoreType.DMA] + scratch,
         out_specs=(ANY, VMEM, VMEM),
     )(coef, q, src, time_step, far, moments, table, rim, core, near_half)
-    got = lax.all_to_all(force, ("yl", "yh", "core"), 0, 0, tiled=True)
-    middle = call(middle_kernel, shape(32, LANES), [VMEM])(got)
-    got = lax.all_to_all(middle, ("x", "z"), 0, 0, tiled=True)
+    got = lax.all_to_all(force, ("x", "yl", "yh"), 0, 0, tiled=True)
+    middle = call(middle_kernel, shape(16, LANES), [VMEM])(got)
+    got = lax.all_to_all(middle, ("z", "core"), 0, 0, tiled=True)
     influence, result = call(
         final_kernel,
         (shape(1, 2, 2, BLADES), shape(PLANES, ROWS, LANES)),

time: 62.2 us -> 63.4 us (1.019)
  blocking collectives: 35.7 us -> 36.7 us
    all_to_all x2, blocking collectives: 35.7 us -> 36.7 us  [the longest x1 19.9 us: per_device(): got = lax.all_to_all(middle, ('z', 'core'), 0, 0, tiled=True)]
  transfers between devices with their start and end apart: 2 -> 2, of which waited for: 0 -> 0; matrix products, arithmetic and copies ran while one was open for 0% -> 0% of each run, Pallas kernels for 14% -> 13%
where the time goes in v8:
time: 63.4 us; the launch traced here: 63.1 us
  blocking collectives  36.7 us (58%)
  Pallas kernels  14.2 us (22%)
  starting transfers between devices  10.8 us (17%)
  between operations  1.39 us (2%)
    all_to_all x1, blocking collectives, per_device(): got = lax.all_to_all(middle, ('z', 'core'), 0, 0, tiled=True)  19.9 us
    all_to_all x1, blocking collectives, per_device(): got = lax.all_to_all(force, ('x', 'yl', 'yh'), 0, 0, tiled=True)  16.8 us
    ppermute x1, starting transfers between devices, per_device(): far = lax.ppermute(far, AXES, swap_pairs(False))  8.83 us
    pallas_call x1, Pallas kernels, per_device(): call(inner_kernel, (shape(LEVELS - 1, PLANES, TILE, LANES), shape(PLANES,...  4.01 us
    pallas_call x1, Pallas kernels, per_device(): call(far_rim_kernel, (shape(PLANES, ROWS, LANES), half, shape(32, LANES))...  3.55 us
    pallas_call x1, Pallas kernels, per_device(): call(near_rim_kernel, half, [VMEM] * 8, scratch)  2.97 us
    ppermute x1, starting transfers between devices, per_device(): near = lax.ppermute(near, AXES, swap_pairs(True))  1.92 us
    pallas_call x1, Pallas kernels, per_device(): call(prep_kernel, (shape(MSG, LANES), shape(16 * ROWS, LANES), shape(48,...  1.5 us
  transfers between devices with their start and end apart: 2, of which 0 were waited for; matrix products, arithmetic and copies ran while one was open for 0% of the time, Pallas kernels for 13%

profile of v8, /device:TPU:1, one launch (start us, length us, event | category | flops | bytes accessed | tf_op | source)
XLA Modules:
  0.0 63.1 jit_solution(55153696474219759)
XLA Ops:
  0.6 0.0 copy-start
  0.6 0.0 copy-start.1
  0.6 0.0 copy-start.2
  0.7 1.1 %shard_map.113._ = f32[480,128]{1,0:T(8,128)S(1)} custom-call(f32[20,32,128]{2,1,0:T(8,128)} %bitcast.13, f32[20,32,128]{2,1,0:T(8,128)} %bitcast.18, f32[32,128]{1,0:T(8,128)} %t_ref.9), custom_call_target="tpu_custom_call" | custom-call | flops 1000 | bytes 1000 | tf_op jit(solution)/shard_map/pallas_call | solution.py:425
  1.8 8.8 %collective-permute-start = (f32[480,128]{1,0:T(8,128)S(1)}, f32[480,128]{1,0:T(8,128)S(1)}, u32[]{:S(2)}, u32[]{:S(2)}) collective-permute-start(f32[480,128]{1,0:T(8,128)S(1)} %shard_map.113._), channel_id=1, source_target_pairs={{1,2},{2,1},{3,4},{4,3},{5,6},{6,5},{7,8},{8,7},{9,10},{10,9},{11,... | collective-permute-start | bytes 737288 | tf_op jit(solution)/shard_map/ppermute | solution.py:444
  11.3 0.0 copy-done
  11.3 0.0 copy-done.1
  11.3 0.0 copy-done.2
  11.3 1.5 %shard_map.114 = (f32[472,128]{1,0:T(8,128)S(1)}, f32[512,128]{1,0:T(8,128)S(1)}, f32[48,128]{1,0:T(8,128)S(1)}, f32[52,8,128]{2,1,0:T(8,128)S(1)}) custom-call(s32[1,512]{1,0:T(1,128)} %bitcast.28, f32[16,512]{1,0:T(8,128)} %weight_ref.1, s32[16]{0:T(128)} %ids_ref.1, f32[5,5]{1,0:T(8,128)} %ja_ref.1, f32[5,5]{1,0:T(8,128)} %jc_ref.1, f32[1,2]{1,0:T(1,128)} %bitcast.29, ...), custom_call_target="tpu_custom_call" | custom-call | flops 1000 | bytes 1000 | tf_op jit(solution)/shard_map/pallas_call | solution.py:433
  12.8 1.9 %collective-permute-start.1 = (f32[472,128]{1,0:T(8,128)S(1)}, f32[472,128]{1,0:T(8,128)S(1)}, u32[]{:S(2)}, u32[]{:S(2)}) collective-permute-start(f32[472,128]{1,0:T(8,128)S(1)} %get-tuple-element.18), channel_id=1, source_target_pairs={{0,1},{1,0},{2,3},{3,2},{4,5},{5,4},{6,7},{7,6},{8,9},{9,8},{10,11... | collective-permute-start | bytes 725000 | tf_op jit(solution)/shard_map/ppermute | solution.py:445
  14.7 4.0 %shard_map.115 = (f32[11,20,8,128]{3,2,1,0:T(8,128)S(1)}, f32[20,8,128]{2,1,0:T(8,128)S(1)}) custom-call(f32[52,8,128]{2,1,0:T(8,128)S(1)} %get-tuple-element.13.coef, f32[20,32,128]{2,1,0:T(8,128)S(1)} %bitcast.15, f32[20,32,128]{2,1,0:T(8,128)S(1)} %bitcast.20, f32[32,128]{1,0:T(8,128)S(1)} %copy-done.2, f32[48,128]{1,0:T(8,128)S(1)} %get-tuple-element.15.table_ref), custom_call_target="tpu_custom_call" | custom-call | flops 1000 | bytes 1000 | tf_op jit(solution)/shard_map/pallas_call | solution.py:446
  18.8 0.0 collective-permute-done.1.halo_ref
  18.8 3.0 %shard_map.116.near_ref = f32[20,16,128]{2,1,0:T(8,128)S(1)} custom-call(f32[52,8,128]{2,1,0:T(8,128)S(1)} %get-tuple-element.13.coef, f32[20,32,128]{2,1,0:T(8,128)S(1)} %bitcast.16, f32[20,32,128]{2,1,0:T(8,128)S(1)} %bitcast.21, f32[32,128]{1,0:T(8,128)S(1)} %copy-done.2, f32[472,128]{1,0:T(8,128)S(1)} %collective-permute-done.1.halo_ref, ...), custom_call_target="tpu_custom_call" | custom-call | flops 1000 | bytes 1000 | tf_op jit(solution)/shard_map/pallas_call | solution.py:455
  21.7 0.0 collective-permute-done.halo_ref
  21.7 3.6 %shard_map.117 = (f32[20,32,128]{2,1,0:T(8,128)}, f32[20,16,128]{2,1,0:T(8,128)S(1)}, f32[32,128]{1,0:T(8,128)S(1)}) custom-call(f32[52,8,128]{2,1,0:T(8,128)S(1)} %get-tuple-element.13.coef, f32[20,32,128]{2,1,0:T(8,128)S(1)} %bitcast.17, f32[20,32,128]{2,1,0:T(8,128)S(1)} %bitcast.22, f32[32,128]{1,0:T(8,128)S(1)} %copy-done.2, ...), custom_call_target="tpu_custom_call" | custom-call | flops 1000 | bytes 1000 | tf_op jit(solution)/shard_map/pallas_call | solution.py:456
  25.3 16.8 %all_to_all.22 = f32[32,1,128]{2,1,0:T(1,128)S(1)} all-to-all(f32[32,1,128]{2,1,0:T(1,128)S(1)} %bitcast.26), channel_id=1, replica_groups=mesh['x'=4,'yl'=4,'z'=8,'yh'=2,'core'=2] {'x','yl','yh'}, dimensions={0} | all-to-all | bytes 32768 | tf_op jit(solution)/shard_map/all_to_all | solution.py:463
  42.1 0.4 shard_map.118
  42.4 19.9 %all_to_all.23 = f32[16,1,128]{2,1,0:T(1,128)S(1)} all-to-all(f32[16,1,128]{2,1,0:T(1,128)S(1)} %bitcast.25), channel_id=1, replica_groups=mesh['x'=4,'yl'=4,'z'=8,'yh'=2,'core'=2] {'z','core'}, dimensions={0} | all-to-all | bytes 16384 | tf_op jit(solution)/shard_map/all_to_all | solution.py:465
  62.4 0.7 %shard_map.119 = (f32[1,2,2,72]{3,2,1,0:T(2,128)}, f32[20,32,128]{2,1,0:T(8,128)}) custom-call(f32[16,128]{1,0:T(8,128)S(1)} %bitcast.24, f32[48,128]{1,0:T(8,128)S(1)} %get-tuple-element.15.table_ref, f32[20,16,128]{2,1,0:T(8,128)S(1)} %get-tuple-element.20.half_ref, f32[20,32,128]{2,1,0:T(8,128)} %get-tuple-element.21._), custom_call_target="tpu_custom_call", output_to_operand_aliasing={{1}: (3, {})} | custom-call | flops 1000 | bytes 1000 | tf_op jit(solution)/shard_map/pallas_call | solution.py:466
Async XLA Ops:
  0.6 10.6 %copy-start = (f32[1,2,2,5,32,128]{5,4,3,2,1,0:T(8,128)S(1)}, f32[1,2,2,5,32,128]{5,4,3,2,1,0:T(8,128)}, u32[]{:S(2)}) copy-start(f32[1,2,2,5,32,128]{5,4,3,2,1,0:T(8,128)} %param.10) | copy-start | bytes 983044
  0.6 10.6 %copy-start.1 = (f32[2,2,5,32,128]{4,3,2,1,0:T(8,128)S(1)}, f32[2,2,5,32,128]{4,3,2,1,0:T(8,128)}, u32[]{:S(2)}) copy-start(f32[2,2,5,32,128]{4,3,2,1,0:T(8,128)} %param.11) | copy-start | bytes 983044
  0.6 10.6 %copy-start.2 = (f32[32,128]{1,0:T(8,128)S(1)}, f32[32,128]{1,0:T(8,128)}, u32[]{:S(2)}) copy-start(f32[32,128]{1,0:T(8,128)} %t_ref.9) | copy-start | bytes 49156
  1.8 20.0 %collective-permute-start = (f32[480,128]{1,0:T(8,128)S(1)}, f32[480,128]{1,0:T(8,128)S(1)}, u32[]{:S(2)}, u32[]{:S(2)}) collective-permute-start(f32[480,128]{1,0:T(8,128)S(1)} %shard_map.113._), channel_id=1, source_target_pairs={{1,2},{2,1},{3,4},{4,3},{5,6},{6,5},{7,8},{8,7},{9,10},{10,9},{11,... | collective-permute-start | bytes 737288 | tf_op jit(solution)/shard_map/ppermute | solution.py:444
  12.8 6.0 %collective-permute-start.1 = (f32[472,128]{1,0:T(8,128)S(1)}, f32[472,128]{1,0:T(8,128)S(1)}, u32[]{:S(2)}, u32[]{:S(2)}) collective-permute-start(f32[472,128]{1,0:T(8,128)S(1)} %get-tuple-element.18), channel_id=1, source_target_pairs={{0,1},{1,0},{2,3},{3,2},{4,5},{5,4},{6,7},{7,6},{8,9},{9,8},{10,11... | collective-permute-start | bytes 725000 | tf_op jit(solution)/shard_map/ppermute | solution.py:445

commit v9 on v7

--- a/solution.py
+++ b/solution.py
@@ -203,20 +203,23 @@
 
 
 def prep_kernel(
-    cell_ref, weight_ref, ids_ref, ja_ref, jc_ref, omega_ref, _, count_ref, q_ref, s_ref, t_ref, near_ref,
-    moments_ref, table_ref, coef_ref, cell, weight, ids, ja, jc, omega, sems,
+    cell_ref, weight_ref, ids_ref, ja_ref, jc_ref, omega_ref, q_hbm, s_hbm, t_hbm, _, count_ref, near_ref,
+    moments_ref, table_ref, coef_ref, q_ref, s_ref, t_ref, cell, weight, ids, ja, jc, omega, sems,
 ):
     pairs = ((cell_ref, cell), (weight_ref, weight), (ids_ref, ids), (ja_ref, ja), (jc_ref, jc), (omega_ref, omega))
+    pairs += ((q_hbm, q_ref), (s_hbm, s_ref), (t_hbm, t_ref))
     copies = [pltpu.make_async_copy(a, b, sems.at[i]) for i, (a, b) in enumerate(pairs)]
     for copy in copies:
         copy.start()
     last_end = 1 - lax.axis_index("core")
-    fill_message(near_ref, last_end * (ROWS - HALO), last_end, q_ref, s_ref, t_ref)
-    for copy in copies:
+    for copy in copies[:6]:
         copy.wait()
     make_coefficients(ja, jc, omega, coef_ref)
     make_tables(ids, table_ref)
     make_moments(cell, weight, count_ref, moments_ref)
+    for copy in copies[6:]:
+        copy.wait()
+    fill_message(near_ref, last_end * (ROWS - HALO), last_end, q_ref, s_ref, t_ref)
 
 
 def inner_kernel(
@@ -443,16 +446,20 @@
     )(*map(in_hbm, (q, src, time_step)))
     big = pltpu.VMEM((PLANES, ROWS + 16, LANES), jnp.float32)
     faces = surf_cell.shape[0]
-    near, moments, table, coef = call(
+    held = tuple(map(in_hbm, (q, src, time_step)))
+    near, moments, table, coef, q, src, time_step = call(
         prep_kernel,
-        (shape(MSG, LANES), shape(16 * ROWS, LANES), shape(48, LANES), shape(52, TILE, LANES)),
-        [ANY] * 7 + [SMEM] + [VMEM] * 3,
+        (
+            shape(MSG, LANES), shape(16 * ROWS, LANES), shape(48, LANES), shape(52, TILE, LANES),
+            shape(*q.shape), shape(*q.shape), shape(ROWS, LANES),
+        ),
+        [ANY] * 10 + [SMEM],
         [pltpu.VMEM((1, faces), jnp.int32), pltpu.VMEM((16, faces), jnp.float32)]
         + [pltpu.SMEM(diam_ids.shape, jnp.int32), pltpu.VMEM((5, 5), jnp.float32), pltpu.VMEM((5, 5), jnp.float32)]
-        + [pltpu.VMEM((1, 2), jnp.float32), pltpu.SemaphoreType.DMA((6,))],
+        + [pltpu.VMEM((1, 2), jnp.float32), pltpu.SemaphoreType.DMA((9,))],
     )(
         *map(in_hbm, (surf_cell.reshape(1, -1), surf_weight, diam_ids, jac_axial, jac_circ, omega.reshape(1, 2))),
-        far, face_count, q, src, time_step,
+        *held, far, face_count,
     )
     far = lax.ppermute(far, AXES, swap_pairs(False))
     near = lax.ppermute(near, AXES, swap_pairs(True))

time: 62.2 us -> 62.1 us (level)
  no operation moved by 1% of the time
where the time goes in v9:
time: 62.1 us; the launch traced here: 61.8 us
  blocking collectives  35.5 us (57%)
  Pallas kernels  14.2 us (23%)
  starting transfers between devices  10.8 us (17%)
  between operations  1.34 us (2%)
    all_to_all x1, blocking collectives, per_device(): got = lax.all_to_all(middle, ('x', 'z'), 0, 0, tiled=True)  22.9 us
    all_to_all x1, blocking collectives, per_device(): got = lax.all_to_all(force, ('yl', 'yh', 'core'), 0, 0, tiled=True)  12.6 us
    ppermute x1, starting transfers between devices, per_device(): far = lax.ppermute(far, AXES, swap_pairs(False))  8.83 us
    pallas_call x1, Pallas kernels, per_device(): call(inner_kernel, (shape(LEVELS - 1, PLANES, TILE, LANES), shape(PLANES,...  4.15 us
    pallas_call x1, Pallas kernels, per_device(): call(far_rim_kernel, (shape(PLANES, ROWS, LANES), half, shape(16, LANES))...  3.51 us
    pallas_call x1, Pallas kernels, per_device(): call(near_rim_kernel, half, [VMEM] * 8, scratch)  2.92 us
    ppermute x1, starting transfers between devices, per_device(): near = lax.ppermute(near, AXES, swap_pairs(True))  1.92 us
    pallas_call x1, Pallas kernels, per_device(): call(prep_kernel, (shape(MSG, LANES), shape(16 * ROWS, LANES), shape(48,...  1.56 us
  transfers between devices with their start and end apart: 2, of which 0 were waited for; matrix products, arithmetic and copies ran while one was open for 0% of the time, Pallas kernels for 14%

profile of v9, /device:TPU:1, one launch (start us, length us, event | category | flops | bytes accessed | tf_op | source)
XLA Modules:
  0.0 61.8 jit_solution(14227163564413425986)
XLA Ops:
  0.6 1.1 %shard_map.113._ = f32[480,128]{1,0:T(8,128)S(1)} custom-call(f32[20,32,128]{2,1,0:T(8,128)} %bitcast.17, f32[20,32,128]{2,1,0:T(8,128)} %bitcast.19, f32[32,128]{1,0:T(8,128)} %t_hbm.1), custom_call_target="tpu_custom_call" | custom-call | flops 1000 | bytes 1000 | tf_op jit(solution)/shard_map/pallas_call | solution.py:441
  1.7 8.8 %collective-permute-start = (f32[480,128]{1,0:T(8,128)S(1)}, f32[480,128]{1,0:T(8,128)S(1)}, u32[]{:S(2)}, u32[]{:S(2)}) collective-permute-start(f32[480,128]{1,0:T(8,128)S(1)} %shard_map.113._), channel_id=1, source_target_pairs={{1,2},{2,1},{3,4},{4,3},{5,6},{6,5},{7,8},{8,7},{9,10},{10,9},{11,... | collective-permute-start | bytes 737288 | tf_op jit(solution)/shard_map/ppermute | solution.py:464
  11.2 1.6 %shard_map.114 = (f32[472,128]{1,0:T(8,128)S(1)}, f32[512,128]{1,0:T(8,128)S(1)}, f32[48,128]{1,0:T(8,128)S(1)}, f32[52,8,128]{2,1,0:T(8,128)S(1)}, f32[20,32,12...) custom-call(s32[1,512]{1,0:T(1,128)} %bitcast.22, f32[16,512]{1,0:T(8,128)} %weight_ref.1, ...), custom_call_target="tpu_custom_call" | custom-call | flops 1000 | bytes 1000 | tf_op jit(solution)/shard_map/pallas_call | solution.py:450
  12.7 1.9 %collective-permute-start.1 = (f32[472,128]{1,0:T(8,128)S(1)}, f32[472,128]{1,0:T(8,128)S(1)}, u32[]{:S(2)}, u32[]{:S(2)}) collective-permute-start(f32[472,128]{1,0:T(8,128)S(1)} %get-tuple-element.24), channel_id=1, source_target_pairs={{0,1},{1,0},{2,3},{3,2},{4,5},{5,4},{6,7},{7,6},{8,9},{9,8},{10,11... | collective-permute-start | bytes 725000 | tf_op jit(solution)/shard_map/ppermute | solution.py:465
  14.7 4.2 %shard_map.115 = (f32[11,20,8,128]{3,2,1,0:T(8,128)S(1)}, f32[20,8,128]{2,1,0:T(8,128)S(1)}) custom-call(f32[52,8,128]{2,1,0:T(8,128)S(1)} %get-tuple-element.16.coef, f32[20,32,128]{2,1,0:T(8,128)S(1)} %get-tuple-element.17.q_ref, f32[20,32,128]{2,1,0:T(8,128)S(1)} %get-tuple-element.18.s_ref, f32[32,128]{1,0:T(8,128)S(1)} %get-tuple-element.19.t_ref, ...), custom_call_target="tpu_custom_call" | custom-call | flops 1000 | bytes 1000 | tf_op jit(solution)/shard_map/pallas_call | solution.py:466
  18.8 0.0 collective-permute-done.1.halo_ref
  18.8 2.9 %shard_map.116.near_ref = f32[20,16,128]{2,1,0:T(8,128)S(1)} custom-call(f32[52,8,128]{2,1,0:T(8,128)S(1)} %get-tuple-element.16.coef, f32[20,32,128]{2,1,0:T(8,128)S(1)} %get-tuple-element.17.q_ref, f32[20,32,128]{2,1,0:T(8,128)S(1)} %get-tuple-element.18.s_ref, f32[32,128]{1,0:T(8,128)S(1)} %get-tuple-element.19.t_ref, ...), custom_call_target="tpu_custom_call" | custom-call | flops 1000 | bytes 1000 | tf_op jit(solution)/shard_map/pallas_call | solution.py:475
  21.8 0.0 collective-permute-done.halo_ref
  21.8 3.5 %shard_map.117 = (f32[20,32,128]{2,1,0:T(8,128)}, f32[20,16,128]{2,1,0:T(8,128)S(1)}, f32[16,128]{1,0:T(8,128)S(1)}) custom-call(f32[52,8,128]{2,1,0:T(8,128)S(1)} %get-tuple-element.16.coef, f32[20,32,128]{2,1,0:T(8,128)S(1)} %get-tuple-element.17.q_ref, f32[20,32,128]{2,1,0:T(8,128)S(1)} %get-tuple-element.18.s_ref, ...), custom_call_target="tpu_custom_call" | custom-call | flops 1000 | bytes 1000 | tf_op jit(solution)/shard_map/pallas_call | solution.py:476
  25.3 12.6 %all_to_all.22 = f32[16,1,128]{2,1,0:T(1,128)S(1)} all-to-all(f32[16,1,128]{2,1,0:T(1,128)S(1)} %bitcast.16), channel_id=1, replica_groups=mesh['x'=4,'yl'=4,'z'=8,'yh'=2,'core'=2] {'yl','yh','core'}, dimensions={0} | all-to-all | bytes 16384 | tf_op jit(solution)/shard_map/all_to_all | solution.py:483
  37.9 0.1 shard_map.118
  38.0 22.9 %all_to_all.23 = f32[32,1,128]{2,1,0:T(1,128)S(1)} all-to-all(f32[32,1,128]{2,1,0:T(1,128)S(1)} %bitcast.14), channel_id=1, replica_groups=mesh['x'=4,'yl'=4,'z'=8,'yh'=2,'core'=2] {'x','z'}, dimensions={0} | all-to-all | bytes 32768 | tf_op jit(solution)/shard_map/all_to_all | solution.py:485
  61.0 0.8 %shard_map.119 = (f32[1,2,2,72]{3,2,1,0:T(2,128)}, f32[20,32,128]{2,1,0:T(8,128)}) custom-call(f32[32,128]{1,0:T(8,128)S(1)} %bitcast.13, f32[48,128]{1,0:T(8,128)S(1)} %get-tuple-element.21.table_ref, f32[20,16,128]{2,1,0:T(8,128)S(1)} %get-tuple-element.26.half_ref, f32[20,32,128]{2,1,0:T(8,128)} %get-tuple-element.27._), custom_call_target="tpu_custom_call", output_to_operand_aliasing={{1}: (3, {})} | custom-call | flops 1000 | bytes 1000 | tf_op jit(solution)/shard_map/pallas_call | solution.py:486
Async XLA Ops:
  1.7 20.1 %collective-permute-start = (f32[480,128]{1,0:T(8,128)S(1)}, f32[480,128]{1,0:T(8,128)S(1)}, u32[]{:S(2)}, u32[]{:S(2)}) collective-permute-start(f32[480,128]{1,0:T(8,128)S(1)} %shard_map.113._), channel_id=1, source_target_pairs={{1,2},{2,1},{3,4},{4,3},{5,6},{6,5},{7,8},{8,7},{9,10},{10,9},{11,... | collective-permute-start | bytes 737288 | tf_op jit(solution)/shard_map/ppermute | solution.py:464
  12.7 6.1 %collective-permute-start.1 = (f32[472,128]{1,0:T(8,128)S(1)}, f32[472,128]{1,0:T(8,128)S(1)}, u32[]{:S(2)}, u32[]{:S(2)}) collective-permute-start(f32[472,128]{1,0:T(8,128)S(1)} %get-tuple-element.24), channel_id=1, source_target_pairs={{0,1},{1,0},{2,3},{3,2},{4,5},{5,4},{6,7},{7,6},{8,9},{9,8},{10,11... | collective-permute-start | bytes 725000 | tf_op jit(solution)/shard_map/ppermute | solution.py:465
